TPU v7x, 32 devices: a whole 2x2x4 slice. The times are simulated.
32 devices in a mesh: row: 16 (over z, y, core), col: 2 (over x).
Axes of the slice: x: 2, y: 2, z: 4, core: 2. Of those that a mesh axis runs over, the one named last changes fastest.
Arguments:
- obs_summaries: bfloat16 [8192, 256], P(('row', 'col')), may hold values from -6 to 6
- sim_summaries: bfloat16 [4096, 256], P('row'), may hold values from -6 to 6
- neighbours: int32 [8192, 16], P(('row', 'col')), may hold values from 0 to 4095
- field: bfloat16 [4096, 2048], P('row', 'col'), may hold values from -6 to 6
Outputs:
- posterior: bfloat16 [8192, 2048], P('row', 'col')
Inputs may be any that keep to these rules, and one draw needn't show every extreme that they name: `neighbours`: each entry names a row of sim_summaries.
All inputs are finite; a program needn't handle non-finite values.
Results may differ from a plain program's by a relative error of at most 0.005.
Values may be sent and summed in bfloat16 or wider, within the bound.
No kernel may reach another device: no remote copies, remote signals or barrier semaphores. Data moves between devices by JAX's collectives and lax.ppermute only.
A program may use at most 128 MiB of HBM per device.

v0:
```python
import jax
import jax.numpy as jnp
from jax import lax
from jax.sharding import PartitionSpec as P

SHARPNESS = 32.0
EPSILON = 1e-06


def neighbour_widths(obs_rows, index_rows, sims_full, sim_square):
    obs_float = obs_rows.astype(jnp.float32)
    near_rows = jnp.take(sims_full, index_rows, axis=0).astype(jnp.float32)
    inner_prod = jnp.einsum("rd,rkd->rk", obs_float, near_rows)
    obs_square = jnp.sum(obs_float * obs_float, axis=1)
    near_square = jnp.take(sim_square, index_rows, axis=0)
    distance = obs_square[:, None] + near_square - 2.0 * inner_prod
    return jnp.mean(distance, axis=1) + EPSILON


def per_device(obs_summaries, sim_summaries, neighbours, field):
    sims_full = lax.all_gather(sim_summaries, "row", axis=0, tiled=True)
    sim_float = sims_full.astype(jnp.float32)
    sim_square = jnp.sum(sim_float * sim_float, axis=1)
    obs_block = lax.all_gather(obs_summaries, "col", axis=0, tiled=True)
    index_block = lax.all_gather(neighbours, "col", axis=0, tiled=True)
    width = neighbour_widths(obs_block, index_block, sims_full, sim_square)
    obs_float = obs_block.astype(jnp.float32)
    obs_square = jnp.sum(obs_float * obs_float, axis=1)
    cross = lax.dot_general(
        obs_block, sims_full, (((1,), (1,)), ((), ())), preferred_element_type=jnp.float32
    )
    distance = obs_square[:, None] + sim_square[None, :] - 2.0 * cross
    weight = jnp.exp(-SHARPNESS * distance / width[:, None])
    numer = jnp.dot(
        weight.astype(jnp.bfloat16),
        lax.all_gather(field, "row", axis=0, tiled=True),
        preferred_element_type=jnp.float32,
    )
    total = jnp.sum(weight, axis=1)
    numer, total = (numer, total)
    return (numer / total[:, None]).astype(jnp.bfloat16)


def solution(mesh):
    return jax.shard_map(
        per_device,
        mesh=mesh,
        in_specs=(
            P(("row", "col"), None),
            P("row", None),
            P(("row", "col"), None),
            P("row", "col"),
        ),
        out_specs=P("row", "col"),
        check_vma=False,
    )
```

profile of v0, /device:TPU:0, one launch (start us, length us, event | category | flops | bytes accessed | tf_op | source)
XLA Modules:
  0.0 161.7 jit_solution(11917042524184065091)
XLA Ops:
  6.5 0.0 all-gather.3.cloned.1.call-start
  6.5 0.7 all-gather.3.cloned.1.call-update
  7.3 0.0 all-gather.5.cloned.1.call-start
  7.3 0.7 all-gather.5.cloned.1.call-update
  8.0 0.8 copy.6
  8.8 7.1 %all_gather.14 = s32[512,16]{1,0:T(8,128)S(1)} all-gather(s32[256,16]{1,0:T(8,128)S(1)} %copy.6), channel_id=1, replica_groups=mesh['row'=16,'col'=2] {'col'}, dimensions={0}, use_global_device_ids=true | all-gather | bytes 49152 | tf_op jit(solution)/shard_map/all_gather | solution.py:25
  15.9 0.1 reshape.14
  16.1 5.9 %all_gather.12 = bf16[512,256]{1,0:T(8,128)(2,1)S(1)} all-gather(bf16[256,256]{1,0:T(8,128)(2,1)} %param.4), channel_id=1, replica_groups=mesh['row'=16,'col'=2] {'col'}, dimensions={0}, use_global_device_ids=true | all-gather | bytes 393216 | tf_op jit(solution)/shard_map/all_gather | solution.py:24
  21.9 0.1 multiply_reduce_fusion.1
  22.1 0.1 compare_and_fusion
  22.2 31.5 %all-gather.3.cloned.1.call-done = bf16[4096,256]{1,0:T(8,128)(2,1)} async-done(((bf16[256,256]{1,0:T(8,128)(2,1)}), bf16[4096,256]{1,0:T(8,128)(2,1)}) %all-gather.3.cloned.1.call-update) | async-done | bytes 2097168 | tf_op jit(solution)/shard_map/all_gather | solution.py:21
  53.7 2.2 %multiply_reduce_fusion = f32[4096]{0:T(1024)S(1)} fusion(bf16[4096,256]{1,0:T(8,128)(2,1)} %all-gather.3.cloned.1.call-done), kind=kLoop, calls=%fused_computation.7 | loop fusion | flops 3141632 | bytes 2113536 | tf_op jit(solution)/shard_map/reduce_sum | solution.py:23
  55.9 0.0 copy-start
  55.9 45.5 %gather_fusion = f32[8192]{0:T(1024)S(1)} fusion(f32[4096]{0:T(1024)S(1)} %multiply_reduce_fusion, s32[8192]{0:T(1024)S(1)} %broadcast_clamp_fusion), kind=kCustom, calls=%fused_computation | custom fusion | bytes 98304 | tf_op jit(solution)/shard_map/jit(_take)/gather | solution.py:15
  101.4 0.1 reshape.13
  101.5 0.0 copy-done
  101.6 32.9 %gather_fusion.1 = bf16[8192,256]{1,0:T(8,128)(2,1)} fusion(bf16[4096,256]{1,0:T(8,128)(2,1)S(1)} %copy-done, s32[8192]{0:T(1024)S(1)} %broadcast_clamp_fusion), kind=kCustom, calls=%fused_computation.1 | custom fusion | bytes 8421376 | tf_op jit(solution)/shard_map/jit(_take)/gather | solution.py:12
  134.5 5.6 %fusion.2 = f32[512,1,16]{2,1,0:T(1,128)S(1)} fusion(bf16[512,16,256]{2,1,0:T(8,128)(2,1)} %bitcast.8, pred[512,16]{1,0:T(8,128)(4,1)S(1)} %compare_and_fusion, bf16[512,256,1]{1,0,2:T(8,128)(2,1)S(1)} %bitcast.9), kind=kOutput, calls=%fused_computation.5 | convolution fusion | flops 6291456 | bytes 4497408 | tf_op jit(solution)/shard_map/rd,rkd->rk/dot_general | solution.py:13
  140.1 0.2 subtract_reduce_fusion
  140.4 4.4 %fusion.10 = (f32[512]{0:T(512)S(1)}, bf16[512,4096]{1,0:T(8,128)(2,1)}) fusion(f32[512]{0:T(512)S(1)} %multiply_add_fusion, bf16[512,256]{1,0:T(8,128)(2,1)S(1)} %all_gather.12, bf16[4096,256]{1,0:T(8,128)(2,1)S(1)} %copy-done, f32[4096]{0:T(1024)S(1)} %multiply_reduce_fusion, f32[512]{0:T(512)S(1)} %multiply_reduce_fusion.1), kind=kOutput, calls=%fused_computation.19 | convolution fusion | flops 1088421376 | bytes 6576128 | tf_op jit(solution)/shard_map/dot_general | solution.py:29
  144.8 0.0 all-gather.5.cloned.1.call-done
  144.8 10.1 %divide_convert_fusion = bf16[512,1024]{1,0:T(8,128)(2,1)} fusion(bf16[4096,1024]{1,0:T(8,128)(2,1)} %all-gather.5.cloned.1.call-done, bf16[512,4096]{1,0:T(8,128)(2,1)} %get-tuple-element.6, f32[512]{0:T(512)S(1)} %get-tuple-element.5), kind=kOutput, calls=%fused_computation.9 | convolution fusion | flops 4296015872 | bytes 13633536 | tf_op jit(solution)/shard_map/dot_general | solution.py:34
  (3 shorter events, 0.0 us)
Async XLA Ops:
  6.5 47.1 %all-gather.3.cloned.1.call-start = ((), (), s32[]{:S(2)}) async-start(), calls=%async_computation | async-start | bytes 2228224 | tf_op jit(solution)/shard_map/all_gather | solution.py:21
  7.3 137.5 %all-gather.5.cloned.1.call-start = ((), (), s32[]{:S(2)}) async-start(), calls=%async_computation.1 | async-start | bytes 8912896 | tf_op jit(solution)/shard_map/all_gather | solution.py:36
  55.9 45.7 %copy-start = (bf16[4096,256]{1,0:T(8,128)(2,1)S(1)}, bf16[4096,256]{1,0:T(8,128)(2,1)}, u32[]{:S(2)}) copy-start(bf16[4096,256]{1,0:T(8,128)(2,1)} %all-gather.3.cloned.1.call-done) | copy-start | bytes 6291460
Sparse Core Ops, SparseCore 0:
  9.5 44.0 all-gather.2
  55.8 73.6 all-gather.4
where the time goes:
time: 162 us
  local copies, waits for them, and re-layouts  79.5 us (49%)
  waiting for transfers between devices  32.9 us (20%)
  matrix products  20.2 us (12%)
  between operations  13.5 us (8%)
  blocking collectives  12.9 us (8%)
  other arithmetic  2.71 us (2%)
    gather x2, local copies, waits for them, and re-layouts, neighbour_widths(): near_square = jnp.take(sim_square, index_rows, axis=0)  45.7 us
    gather x1, local copies, waits for them, and re-layouts, neighbour_widths(): near_rows = jnp.take(sims_full, index_rows, axis=0).astype(jnp.float32)  32.9 us
    all_gather x1, waiting for transfers between devices, per_device(): sims_full = lax.all_gather(sim_summaries, 'row', axis=0, tiled=True)  31.5 us
    dot_general x1, matrix products, per_device(): jnp.dot(weight.astype(jnp.bfloat16), lax.all_gather(field, 'row', axis=0,...  10.1 us
    all_gather x1, blocking collectives, per_device(): index_block = lax.all_gather(neighbours, 'col', axis=0, tiled=True)  7.09 us
    all_gather x1, blocking collectives, per_device(): obs_block = lax.all_gather(obs_summaries, 'col', axis=0, tiled=True)  5.86 us
    dot_general x1, matrix products, neighbour_widths(): inner_prod = jnp.einsum('rd,rkd->rk', obs_float, near_rows)  5.62 us
    dot_general x1, matrix products, per_device(): lax.dot_general(obs_block, sims_full, (((1,), (1,)), ((), ())), preferred...  4.43 us
  transfers between devices with their start and end apart: 2, of which 1 were waited for; matrix products, arithmetic and copies ran while one was open for 57% of the time, Pallas kernels for 0%

commit v1 on v0

v1 whole, which is shorter than its diff:
```python
import functools
import math

import jax
import jax.numpy as jnp
from jax import lax
from jax.experimental import pallas as pl
from jax.experimental.pallas import tpu as pltpu
from jax.sharding import PartitionSpec as P

SHARPNESS = 32.0
EPSILON = 1e-06
LANES = 128
CORE_BIT = 1
Y_BIT = 2
VMEM = pl.BlockSpec(memory_space=pltpu.VMEM)
SMEM = pl.BlockSpec(memory_space=pltpu.SMEM)


def swap(value, axis, size, bit):
    return lax.ppermute(value, axis, [(i, i ^ bit) for i in range(size)])


def gather_steps(size):
    n_z = size // 4
    steps = []
    if n_z == 4:
        across = [(i ^ 12) if (i >> 2) in (1, 2) else (i ^ Y_BIT) for i in range(size)]
        inside = [i ^ 4 for i in range(size)]
        for sent, first in ((0, inside), (0, across), (1, across), (2, inside), (3, inside), (4, across), (5, across)):
            second = across if first is inside else inside
            steps.append((sent, [(i, second[i] if i & CORE_BIT else first[i]) for i in range(size)]))
        return steps
    held = 1
    for bit in [Y_BIT << k for k in range(n_z.bit_length())]:
        steps += [(sent, [(i, i ^ bit) for i in range(size)]) for sent in range(held)]
        held *= 2
    return steps


def owners(size):
    held = [[i] for i in range(size)]
    for sent, pairs in gather_steps(size):
        source = {target: i for i, target in pairs}
        moved = [held[source[i]][sent] for i in range(size)]
        for i in range(size):
            held[i].append(moved[i])
    held = [held[i] + held[i ^ CORE_BIT] for i in range(size)]
    assert all(sorted(row) == list(range(size)) for row in held)
    return held


def gather_rows(value, size, after=None):
    blocks = [value]
    for k, (sent, pairs) in enumerate(gather_steps(size)):
        block = blocks[sent]
        if after and k in after:
            block = lax.optimization_barrier((block, after[k]))[0]
        blocks.append(lax.ppermute(block, "row", pairs))
    return blocks, [swap(block, "row", size, CORE_BIT) for block in blocks]


def weight_kernel(n_sim, n_piece, owner_ref, *refs):
    obs_in, near_in = refs[:n_piece], refs[n_piece : 2 * n_piece]
    sims = refs[2 * n_piece : 2 * n_piece + n_sim]
    weight_out, total_out, obs_scr, low_scr, high_scr, value_scr = refs[2 * n_piece + n_sim :]
    my_row, my_col = lax.axis_index("row"), lax.axis_index("col")
    rows = obs_in[0].shape[0]
    near = near_in[0].shape[0]
    depth = sims[0].shape[0]
    n_obs = n_piece * rows
    for i in range(n_piece):
        slot = lax.bitwise_xor(my_col, i)
        at = pl.ds(pl.multiple_of(slot * rows, rows), rows)
        obs_scr[at, :] = obs_in[i][...]
        index = near_in[i][...].astype(jnp.float32).T.astype(jnp.int32)
        pad = jnp.zeros((rows, LANES - near), jnp.int32)
        high_scr[at, :] = jnp.concatenate([index // LANES, pad - 1], axis=1)
        low_scr[at, :] = jnp.concatenate([index % LANES, pad], axis=1)
    obs = obs_scr[...]
    obs_float = obs.astype(jnp.float32)
    obs_square = jnp.sum(obs_float * obs_float, axis=1, keepdims=True)
    low, high = low_scr[...], high_scr[...]
    near_sum = jnp.zeros((n_obs, LANES), jnp.float32)
    for b in range(n_sim):
        block = sims[b][...]
        squares = block.astype(jnp.float32)
        squares = squares * squares
        folded = squares[:, :LANES]
        for g in range(1, block.shape[1] // LANES):
            folded += squares[:, g * LANES : (g + 1) * LANES]
        sim_square = jnp.sum(folded.T, axis=0, keepdims=True)
        cross = lax.dot_general(obs, block, (((1,), (1,)), ((), ())), preferred_element_type=jnp.float32)
        values = sim_square - 2.0 * cross
        value_scr[:, b * depth : (b + 1) * depth] = values
        owner = owner_ref[my_row * n_sim + b] * (depth // LANES)
        for g in range(depth // LANES):
            found = jnp.take_along_axis(values[:, g * LANES : (g + 1) * LANES], low, axis=1)
            near_sum += jnp.where(high == owner + g, found, 0.0)
    width = obs_square + jnp.sum(near_sum, axis=1, keepdims=True) / near + EPSILON
    factor = (-SHARPNESS * math.log2(math.e)) / width
    total = jnp.zeros((n_obs, LANES), jnp.float32)
    for b in range(n_sim):
        at = slice(b * depth, (b + 1) * depth)
        weight = jnp.exp2(factor * (obs_square + value_scr[:, at]))
        weight_out[:, at] = weight.astype(jnp.bfloat16)
        for g in range(depth // LANES):
            total += weight[:, g * LANES : (g + 1) * LANES]
    total_out[...] = jnp.broadcast_to(jnp.sum(total, axis=1, keepdims=True), total.shape)


def product_kernel(columns, depth, first, last, weight, *refs):
    blocks, rest, out = refs[: len(columns)], refs[len(columns) : -1], refs[-1]
    so_far = None if first else rest[-1]
    total_ref = rest[0] if last else None
    cells = out.shape[1]
    step = min(cells, 256)
    for j in range(cells // step):
        at = slice(j * step, (j + 1) * step)
        total = None if so_far is None else so_far[:, at]
        for column, block in zip(columns, blocks):
            term = jnp.dot(
                weight[:, column * depth : (column + 1) * depth], block[:, at], preferred_element_type=jnp.float32
            )
            total = term if total is None else total + term
        if total_ref is not None:
            total = total / total_ref[:, :1]
        out[:, at] = total.astype(out.dtype)


def call(kernel, vmem, **kw):
    return pl.pallas_call(kernel, compiler_params=pltpu.CompilerParams(vmem_limit_bytes=vmem << 20), **kw)


def per_device(n_row, n_col, obs_summaries, sim_summaries, neighbours, field):
    f32, bf16 = jnp.float32, jnp.bfloat16
    rows, dims = obs_summaries.shape
    depth, cells = field.shape

    obs, near = [obs_summaries], [neighbours.T]
    for k in range(n_col.bit_length() - 1):
        obs = obs + [swap(p, "col", n_col, 1 << k) for p in obs]
        near = near + [swap(p, "col", n_col, 1 << k) for p in near]

    own_sims, other_sims = gather_rows(sim_summaries, n_row)
    sims = own_sims + other_sims
    n_sim, n_piece = len(sims), len(obs)
    owner_table = jnp.array(owners(n_row), jnp.int32).reshape(-1)
    n_obs = n_piece * rows
    weight, total = call(
        functools.partial(weight_kernel, n_sim, n_piece),
        40,
        in_specs=[SMEM] + [VMEM] * (2 * n_piece + n_sim),
        out_specs=[VMEM] * 2,
        out_shape=[
            jax.ShapeDtypeStruct((n_obs, n_sim * depth), bf16),
            jax.ShapeDtypeStruct((n_obs, LANES), f32),
        ],
        scratch_shapes=[
            pltpu.VMEM((n_obs, dims), bf16),
            pltpu.VMEM((n_obs, LANES), jnp.int32),
            pltpu.VMEM((n_obs, LANES), jnp.int32),
            pltpu.VMEM((n_obs, n_sim * depth), f32),
        ],
        cost_estimate=pl.CostEstimate(
            flops=4 * n_obs * n_sim * depth * dims,
            bytes_accessed=8 << 20,
            transcendentals=n_obs * n_sim * depth,
        ),
        name="weights",
    )(owner_table, *obs, *near, *sims)

    after = {k: own_sims[2 * k + 1] for k in range(len(own_sims) // 2)}
    own_blocks, other_blocks = gather_rows(field, n_row, after)
    n_half = n_sim // 2
    cuts = (0, n_half // 2, n_half - 1, n_half)
    groups = [tuple(range(a, b)) for a, b in zip(cuts[:-1], cuts[1:])]
    result = None
    for g, group in enumerate(groups):
        columns = group + tuple(k + n_half for k in group)
        blocks = [own_blocks[k] for k in group] + [other_blocks[k] for k in group]
        last = g == len(groups) - 1
        extra = ([total] if last else []) + ([] if result is None else [result])
        result = call(
            functools.partial(product_kernel, columns, depth, g == 0, last),
            28,
            in_specs=[VMEM] * (1 + len(columns) + len(extra)),
            out_specs=VMEM,
            out_shape=jax.ShapeDtypeStruct((n_obs, cells), bf16 if last else f32),
            cost_estimate=pl.CostEstimate(
                flops=2 * n_obs * len(columns) * depth * cells,
                bytes_accessed=len(columns) * depth * (n_obs + cells) * 2,
                transcendentals=0,
            ),
            name="product",
        )(weight, *blocks, *extra)
    return result


def solution(mesh):
    return jax.shard_map(
        functools.partial(per_device, mesh.shape["row"], mesh.shape["col"]),
        mesh=mesh,
        in_specs=(
            P(("row", "col"), None),
            P("row", None),
            P(("row", "col"), None),
            P("row", "col"),
        ),
        out_specs=P("row", "col"),
        check_vma=False,
    )
```

time: 162 us -> 82.9 us (0.51)
  local copies, waits for them, and re-layouts: 79.5 us -> 3.21 us
  starting transfers between devices: 0.04 us -> 27.1 us
  matrix products: 20.2 us -> 0 us
  Pallas kernels: 0 us -> 15.9 us
  between operations: 13.5 us -> 0.1 us
  blocking collectives: 12.9 us -> 0 us
  waiting for transfers between devices: 32.9 us -> 36.4 us
  other arithmetic: 2.71 us -> 0 us
    gather x3 -> x0, local copies, waits for them, and re-layouts: 78.6 us -> none  [the longest x2 45.7 us: neighbour_widths(): near_square = jnp.take(sim_square, index_rows, axis=0)]
    ppermute x0 -> x32, waiting for transfers between devices: none -> 36.4 us  [the longest x14 32.2 us: gather_rows(): blocks.append(lax.ppermute(block, 'row', pairs))]
    all_gather x2 -> x0, waiting for transfers between devices: 31.5 us -> none  [the longest x1 31.5 us: per_device(): sims_full = lax.all_gather(sim_summaries, 'row', axis=0, tiled=True)]
    ppermute x0 -> x32, starting transfers between devices: none -> 27.1 us  [the longest x14 19.6 us: gather_rows(): blocks.append(lax.ppermute(block, 'row', pairs))]
    dot_general x3 -> x0, matrix products: 20.2 us -> none  [the longest x1 10.1 us: per_device(): jnp.dot(weight.astype(jnp.bfloat16), lax.all_gather(field, 'row', axis=0,...]
    pallas_call x0 -> x4, Pallas kernels: none -> 15.9 us  [the longest x1 10 us: per_device(): call(functools.partial(weight_kernel, n_sim, n_piece), 40, in_specs=[SMEM...]
    all_gather x2 -> x0, blocking collectives: 12.9 us -> none  [the longest x1 7.09 us: per_device(): index_block = lax.all_gather(neighbours, 'col', axis=0, tiled=True)]
    reduce_sum x3 -> x0, other arithmetic: 2.59 us -> none  [the longest x1 2.21 us: per_device(): sim_square = jnp.sum(sim_float * sim_float, axis=1)]
  transfers between devices with their start and end apart: 2 -> 32, of which waited for: 1 -> 12; matrix products, arithmetic and copies ran while one was open for 57% -> 0% of each run, Pallas kernels for 0% -> 17%
where the time goes in v1:
time: 82.9 us; the launch traced here: 82.7 us
  waiting for transfers between devices  36.4 us (44%)
  starting transfers between devices  27.1 us (33%)
  Pallas kernels  15.9 us (19%)
  local copies, waits for them, and re-layouts  3.21 us (4%)
    ppermute x14, waiting for transfers between devices, gather_rows(): blocks.append(lax.ppermute(block, 'row', pairs))  32.2 us
    ppermute x14, starting transfers between devices, gather_rows(): blocks.append(lax.ppermute(block, 'row', pairs))  19.6 us
    pallas_call x1, Pallas kernels, per_device(): call(functools.partial(weight_kernel, n_sim, n_piece), 40, in_specs=[SMEM...  10 us
    ppermute x18, starting transfers between devices, swap(): return lax.ppermute(value, axis, [(i, i ^ bit) for i in range(size)])  7.54 us
    pallas_call x3, Pallas kernels, per_device(): call(functools.partial(product_kernel, columns, depth, g == 0, last), 28,...  5.85 us
    ppermute x18, waiting for transfers between devices, swap(): return lax.ppermute(value, axis, [(i, i ^ bit) for i in range(size)])  4.21 us
    unnamed x10, local copies, waits for them, and re-layouts  3.21 us
  transfers between devices with their start and end apart: 32, of which 12 were waited for; matrix products, arithmetic and copies ran while one was open for 0% of the time, Pallas kernels for 17%

profile of v1, /device:TPU:0, one launch (start us, length us, event | category | flops | bytes accessed | tf_op | source)
XLA Modules:
  0.0 82.7 jit_solution(14735228428978747023)
XLA Ops:
  0.0 3.0 %collective-permute-start.2 = (bf16[256,256]{1,0:T(8,128)(2,1)}, bf16[256,256]{1,0:T(8,128)(2,1)S(1)}, u32[]{:S(2)}, u32[]{:S(2)}) collective-permute-start(bf16[256,256]{1,0:T(8,128)(2,1)} %refs_4_.1), channel_id=1, source_target_pairs={{0,8},{2,6},{4,12},{6,2},{8,0},{10,18},{12,4},{14,22},{16,24},{18,... | collective-permute-start | bytes 393224 | tf_op jit(solution)/shard_map/ppermute | solution.py:59
  3.0 3.2 %collective-permute-done.2.refs_5_ = bf16[256,256]{1,0:T(8,128)(2,1)S(1)} collective-permute-done((bf16[256,256]{1,0:T(8,128)(2,1)}, bf16[256,256]{1,0:T(8,128)(2,1)S(1)}, u32[]{:S(2)}, u32[]{:S(2)}) %collective-permute-start.2) | collective-permute-done | bytes 131104 | tf_op jit(solution)/shard_map/ppermute | solution.py:59
  6.2 2.0 %collective-permute-start.17 = (bf16[256,1024]{1,0:T(8,128)(2,1)}, bf16[256,1024]{1,0:T(8,128)(2,1)S(1)}, u32[]{:S(2)}, u32[]{:S(2)}) collective-permute-start(bf16[256,1024]{1,0:T(8,128)(2,1)} %refs_0_.3), channel_id=1, source_target_pairs={{0,8},{2,6},{4,12},{6,2},{8,0},{10,18},{12,4},{14,22},{16,24},{18,... | collective-permute-start | bytes 1572872 | tf_op jit(solution)/shard_map/ppermute | solution.py:59
  8.2 1.5 %collective-permute-start.4 = (bf16[256,256]{1,0:T(8,128)(2,1)S(1)}, bf16[256,256]{1,0:T(8,128)(2,1)S(1)}, u32[]{:S(2)}, u32[]{:S(2)}) collective-permute-start(bf16[256,256]{1,0:T(8,128)(2,1)S(1)} %collective-permute-done.2.refs_5_), channel_id=1, source_target_pairs={{0,4},{2,10},{4,0},{6,14},{8,16},{10,2},{12,20},{14,6},{16,8},{18,... | collective-permute-start | bytes 393224 | tf_op jit(solution)/shard_map/ppermute | solution.py:59
  9.7 4.9 %collective-permute-done.4.refs_7_ = bf16[256,256]{1,0:T(8,128)(2,1)S(1)} collective-permute-done((bf16[256,256]{1,0:T(8,128)(2,1)S(1)}, bf16[256,256]{1,0:T(8,128)(2,1)S(1)}, u32[]{:S(2)}, u32[]{:S(2)}) %collective-permute-start.4) | collective-permute-done | bytes 131104 | tf_op jit(solution)/shard_map/ppermute | solution.py:59
  14.6 1.1 %collective-permute-start.6 = (bf16[256,256]{1,0:T(8,128)(2,1)S(1)}, bf16[256,256]{1,0:T(8,128)(2,1)S(1)}, u32[]{:S(2)}, u32[]{:S(2)}) collective-permute-start(bf16[256,256]{1,0:T(8,128)(2,1)S(1)} %collective-permute-done.4.refs_7_), channel_id=1, source_target_pairs={{0,8},{2,6},{4,12},{6,2},{8,0},{10,18},{12,4},{14,22},{16,24},{18,... | collective-permute-start | bytes 393224 | tf_op jit(solution)/shard_map/ppermute | solution.py:59
  15.8 1.5 %collective-permute-start.22 = (bf16[256,1024]{1,0:T(8,128)(2,1)}, bf16[256,1024]{1,0:T(8,128)(2,1)S(1)}, u32[]{:S(2)}, u32[]{:S(2)}) collective-permute-start(bf16[256,1024]{1,0:T(8,128)(2,1)} %refs_0_.3), channel_id=1, source_target_pairs={{0,4},{2,10},{4,0},{6,14},{8,16},{10,2},{12,20},{14,6},{16,8},{18,... | collective-permute-start | bytes 1572872 | tf_op jit(solution)/shard_map/ppermute | solution.py:59
  17.3 3.8 %collective-permute-done.6.refs_9_ = bf16[256,256]{1,0:T(8,128)(2,1)S(1)} collective-permute-done((bf16[256,256]{1,0:T(8,128)(2,1)S(1)}, bf16[256,256]{1,0:T(8,128)(2,1)S(1)}, u32[]{:S(2)}, u32[]{:S(2)}) %collective-permute-start.6) | collective-permute-done | bytes 131104 | tf_op jit(solution)/shard_map/ppermute | solution.py:59
  21.1 0.0 collective-permute-done.17.refs_1_
  21.1 1.5 %collective-permute-start.18 = (bf16[256,1024]{1,0:T(8,128)(2,1)S(1)}, bf16[256,1024]{1,0:T(8,128)(2,1)S(1)}, u32[]{:S(2)}, u32[]{:S(2)}) collective-permute-start(bf16[256,1024]{1,0:T(8,128)(2,1)S(1)} %collective-permute-done.17.refs_1_), channel_id=1, source_target_pairs={{0,4},{2,10},{4,0},{6,14},{8,16},{10,2},{12,20},{14,6},{16,8},{18,... | collective-permute-start | bytes 1572872 | tf_op jit(solution)/shard_map/ppermute | solution.py:59
  22.6 0.5 collective-permute-start.3
  23.1 1.5 %collective-permute-start.8 = (bf16[256,256]{1,0:T(8,128)(2,1)S(1)}, bf16[256,256]{1,0:T(8,128)(2,1)S(1)}, u32[]{:S(2)}, u32[]{:S(2)}) collective-permute-start(bf16[256,256]{1,0:T(8,128)(2,1)S(1)} %collective-permute-done.6.refs_9_), channel_id=1, source_target_pairs={{0,4},{2,10},{4,0},{6,14},{8,16},{10,2},{12,20},{14,6},{16,8},{18,... | collective-permute-start | bytes 393224 | tf_op jit(solution)/shard_map/ppermute | solution.py:59
  24.6 1.5 %collective-permute-start = (bf16[256,256]{1,0:T(8,128)(2,1)}, bf16[256,256]{1,0:T(8,128)(2,1)S(1)}, u32[]{:S(2)}, u32[]{:S(2)}) collective-permute-start(bf16[256,256]{1,0:T(8,128)(2,1)} %refs_0_.2), channel_id=1, source_target_pairs={{0,1},{1,0},{2,3},{3,2},{4,5},{5,4},{6,7},{7,6},{8,9},{9,8},{10,11... | collective-permute-start | bytes 393224 | tf_op jit(solution)/shard_map/ppermute | solution.py:21
  26.1 6.1 %collective-permute-done.3.refs_6_ = bf16[256,256]{1,0:T(8,128)(2,1)S(1)} collective-permute-done((bf16[256,256]{1,0:T(8,128)(2,1)}, bf16[256,256]{1,0:T(8,128)(2,1)S(1)}, u32[]{:S(2)}, u32[]{:S(2)}) %collective-permute-start.3) | collective-permute-done | bytes 131104 | tf_op jit(solution)/shard_map/ppermute | solution.py:59
  32.2 1.5 %collective-permute-start.1 = (s32[16,256]{1,0:T(8,128)}, s32[16,256]{1,0:T(8,128)S(1)}, u32[]{:S(2)}, u32[]{:S(2)}) collective-permute-start(s32[16,256]{1,0:T(8,128)} %bitcast.1), channel_id=1, source_target_pairs={{0,1},{1,0},{2,3},{3,2},{4,5},{5,4},{6,7},{7,6},{8,9},{9,8},{10,11... | collective-permute-start | bytes 49160 | tf_op jit(solution)/shard_map/ppermute | solution.py:21
  33.7 0.0 collective-permute-done.8.refs_11_
  33.7 1.0 %collective-permute-start.5 = (bf16[256,256]{1,0:T(8,128)(2,1)S(1)}, bf16[256,256]{1,0:T(8,128)(2,1)S(1)}, u32[]{:S(2)}, u32[]{:S(2)}) collective-permute-start(bf16[256,256]{1,0:T(8,128)(2,1)S(1)} %collective-permute-done.3.refs_6_), channel_id=1, source_target_pairs={{0,8},{2,6},{4,12},{6,2},{8,0},{10,18},{12,4},{14,22},{16,24},{18,... | collective-permute-start | bytes 393224 | tf_op jit(solution)/shard_map/ppermute | solution.py:59
  34.6 1.5 %collective-permute-done.1.refs_3_ = s32[16,256]{1,0:T(8,128)S(1)} collective-permute-done((s32[16,256]{1,0:T(8,128)}, s32[16,256]{1,0:T(8,128)S(1)}, u32[]{:S(2)}, u32[]{:S(2)}) %collective-permute-start.1) | collective-permute-done | bytes 16416 | tf_op jit(solution)/shard_map/ppermute | solution.py:21
  36.1 0.9 %collective-permute-start.23 = (bf16[256,1024]{1,0:T(8,128)(2,1)S(1)}, bf16[256,1024]{1,0:T(8,128)(2,1)S(1)}, u32[]{:S(2)}, u32[]{:S(2)}) collective-permute-start(bf16[256,1024]{1,0:T(8,128)(2,1)S(1)} %collective-permute-done.22.refs_2_), channel_id=1, source_target_pairs={{0,8},{2,6},{4,12},{6,2},{8,0},{10,18},{12,4},{14,22},{16,24},{18,... | collective-permute-start | bytes 1572872 | tf_op jit(solution)/shard_map/ppermute | solution.py:59
  37.0 0.0 collective-permute-done.refs_1_
  37.0 0.0 collective-permute-start.10
  37.0 0.0 collective-permute-done.18.refs_3_
  37.0 1.2 %collective-permute-start.19 = (bf16[256,1024]{1,0:T(8,128)(2,1)S(1)}, bf16[256,1024]{1,0:T(8,128)(2,1)S(1)}, u32[]{:S(2)}, u32[]{:S(2)}) collective-permute-start(bf16[256,1024]{1,0:T(8,128)(2,1)S(1)} %collective-permute-done.18.refs_3_), channel_id=1, source_target_pairs={{0,8},{2,6},{4,12},{6,2},{8,0},{10,18},{12,4},{14,22},{16,24},{18,... | collective-permute-start | bytes 1572872 | tf_op jit(solution)/shard_map/ppermute | solution.py:59
  38.2 1.1 %collective-permute-start.11 = (bf16[256,256]{1,0:T(8,128)(2,1)S(1)}, bf16[256,256]{1,0:T(8,128)(2,1)S(1)}, u32[]{:S(2)}, u32[]{:S(2)}) collective-permute-start(bf16[256,256]{1,0:T(8,128)(2,1)S(1)} %collective-permute-done.3.refs_6_), channel_id=1, source_target_pairs={{0,2},{2,0},{4,6},{6,4},{8,10},{10,8},{12,14},{14,12},{16,18},{18,... | collective-permute-start | bytes 393224 | tf_op jit(solution)/shard_map/ppermute | solution.py:21
  39.3 0.0 collective-permute-done.5.refs_8_
  39.3 0.1 collective-permute-start.12
  39.4 0.0 collective-permute-done.10.refs_13_
  39.4 0.4 collective-permute-start.28
  39.8 0.5 collective-permute-done.11.refs_14_
  40.3 0.8 collective-permute-start.7
  41.1 0.0 collective-permute-done.12.refs_15_
  41.1 0.9 %collective-permute-start.13 = (bf16[256,256]{1,0:T(8,128)(2,1)S(1)}, bf16[256,256]{1,0:T(8,128)(2,1)S(1)}, u32[]{:S(2)}, u32[]{:S(2)}) collective-permute-start(bf16[256,256]{1,0:T(8,128)(2,1)S(1)} %collective-permute-done.5.refs_8_), channel_id=1, source_target_pairs={{0,2},{2,0},{4,6},{6,4},{8,10},{10,8},{12,14},{14,12},{16,18},{18,... | collective-permute-start | bytes 393224 | tf_op jit(solution)/shard_map/ppermute | solution.py:21
  42.0 4.7 %collective-permute-done.7.refs_10_ = bf16[256,256]{1,0:T(8,128)(2,1)S(1)} collective-permute-done((bf16[256,256]{1,0:T(8,128)(2,1)S(1)}, bf16[256,256]{1,0:T(8,128)(2,1)S(1)}, u32[]{:S(2)}, u32[]{:S(2)}) %collective-permute-start.7) | collective-permute-done | bytes 131104 | tf_op jit(solution)/shard_map/ppermute | solution.py:59
  46.7 0.0 collective-permute-start.14
  46.8 0.0 collective-permute-done.13.refs_16_
  46.8 0.5 collective-permute-start.15
  47.3 0.8 %collective-permute-done.14.refs_17_ = bf16[256,256]{1,0:T(8,128)(2,1)S(1)} collective-permute-done((bf16[256,256]{1,0:T(8,128)(2,1)S(1)}, bf16[256,256]{1,0:T(8,128)(2,1)S(1)}, u32[]{:S(2)}, u32[]{:S(2)}) %collective-permute-start.14) | collective-permute-done | bytes 131104 | tf_op jit(solution)/shard_map/ppermute | solution.py:21
  48.1 0.1 collective-permute-start.29
  48.2 0.0 collective-permute-done.15.refs_18_
  48.3 0.3 collective-permute-start.30
  48.6 0.8 collective-permute-start.24
  49.4 3.8 %collective-permute-done.19.refs_1_ = bf16[256,1024]{1,0:T(8,128)(2,1)S(1)} collective-permute-done((bf16[256,1024]{1,0:T(8,128)(2,1)S(1)}, bf16[256,1024]{1,0:T(8,128)(2,1)S(1)}, u32[]{:S(2)}, u32[]{:S(2)}) %collective-permute-start.19) | collective-permute-done | bytes 524320 | tf_op jit(solution)/shard_map/ppermute | solution.py:59
  53.2 2.2 %collective-permute-start.20 = (bf16[256,1024]{1,0:T(8,128)(2,1)S(1)}, bf16[256,1024]{1,0:T(8,128)(2,1)S(1)}, u32[]{:S(2)}, u32[]{:S(2)}) collective-permute-start(bf16[256,1024]{1,0:T(8,128)(2,1)S(1)} %collective-permute-done.19.refs_1_), channel_id=1, source_target_pairs={{0,4},{2,10},{4,0},{6,14},{8,16},{10,2},{12,20},{14,6},{16,8},{18,... | collective-permute-start | bytes 1572872 | tf_op jit(solution)/shard_map/ppermute | solution.py:59
  55.4 0.0 collective-permute-done.28.refs_4_
  55.4 0.0 collective-permute-start.16
  55.4 1.3 %collective-permute-done.16.refs_19_ = bf16[256,256]{1,0:T(8,128)(2,1)S(1)} collective-permute-done((bf16[256,256]{1,0:T(8,128)(2,1)S(1)}, bf16[256,256]{1,0:T(8,128)(2,1)S(1)}, u32[]{:S(2)}, u32[]{:S(2)}) %collective-permute-start.16) | collective-permute-done | bytes 131104 | tf_op jit(solution)/shard_map/ppermute | solution.py:21
  56.7 0.1 collective-permute-start.31
  56.9 0.0 collective-permute-done.29.refs_5_
  56.9 0.4 collective-permute-start.25
  57.3 0.1 collective-permute-start.26
  57.4 0.4 collective-permute-done.24.refs_2_
  57.8 0.3 collective-permute-start.27
  58.1 5.3 %collective-permute-done.20.refs_0_ = bf16[256,1024]{1,0:T(8,128)(2,1)S(1)} collective-permute-done((bf16[256,1024]{1,0:T(8,128)(2,1)S(1)}, bf16[256,1024]{1,0:T(8,128)(2,1)S(1)}, u32[]{:S(2)}, u32[]{:S(2)}) %collective-permute-start.20) | collective-permute-done | bytes 524320 | tf_op jit(solution)/shard_map/ppermute | solution.py:59
  63.4 0.1 collective-permute-start.21
  63.5 0.9 %copy-done.1 = bf16[256,256]{1,0:T(8,128)(2,1)S(1)} copy-done((bf16[256,256]{1,0:T(8,128)(2,1)S(1)}, bf16[256,256]{1,0:T(8,128)(2,1)}, u32[]{:S(2)}) %copy-start.1) | copy-done | bytes 131096
  64.4 0.9 %copy-done.2 = bf16[256,256]{1,0:T(8,128)(2,1)S(1)} copy-done((bf16[256,256]{1,0:T(8,128)(2,1)S(1)}, bf16[256,256]{1,0:T(8,128)(2,1)}, u32[]{:S(2)}) %copy-start.2) | copy-done | bytes 131096
  65.3 0.7 copy-done.3
  66.1 0.7 copy-done.4
  66.7 10.0 %weights.1 = (bf16[512,4096]{1,0:T(8,128)(2,1)S(1)}, f32[512,128]{1,0:T(8,128)S(1)}) custom-call(s32[256]{0:T(256)S(1)} %copy-done.4, bf16[256,256]{1,0:T(8,128)(2,1)S(1)} %copy-done.1, bf16[256,256]{1,0:T(8,128)(2,1)S(1)} %collective-permute-done.refs_1_, s32[16,256]{1,0:T(8,128)S(1)} %bitcast.2, s32[16,256]{1,0:T(8,128)S(1)} %collective-permute-done.1.refs_3_, ...), custom_call_target="tpu_custom_call" | custom-call | flops 2147483648 | bytes 8388608 | tf_op jit(solution)/shard_map/weights/pallas_call | solution.py:150
  76.8 2.3 %product.3.refs_6_ = f32[512,1024]{1,0:T(8,128)S(1)} custom-call(bf16[512,4096]{1,0:T(8,128)(2,1)S(1)} %get-tuple-element.11.weight, bf16[256,1024]{1,0:T(8,128)(2,1)S(1)} %copy-done, bf16[256,1024]{1,0:T(8,128)(2,1)S(1)} %collective-permute-done.17.refs_1_, bf16[256,1024]{1,0:T(8,128)(2,1)S(1)} %collective-permute-done.22.refs_2_, ...), custom_call_target="tpu_custom_call" | custom-call | flops 2147483648 | bytes 6291456 | tf_op jit(solution)/shard_map/product/pallas_call | solution.py:184
  79.1 0.0 collective-permute-done.25.refs_3_
  79.1 0.0 collective-permute-done.26.refs_4_
  79.2 1.8 %product.4.refs_3_ = f32[512,1024]{1,0:T(8,128)S(1)} custom-call(bf16[512,4096]{1,0:T(8,128)(2,1)S(1)} %get-tuple-element.11.weight, bf16[256,1024]{1,0:T(8,128)(2,1)S(1)} %collective-permute-done.23.refs_0_, bf16[256,1024]{1,0:T(8,128)(2,1)S(1)} %collective-permute-done.19.refs_1_, bf16[256,1024]{1,0:T(8,128)(2,1)S(1)} %collective-permute-done.24.refs_2_, ...), custom_call_target="tpu_custom_call" | custom-call | flops 1610612736 | bytes 4718592 | tf_op jit(solution)/shard_map/product/pallas_call | solution.py:184
  81.0 1.7 %product.5 = bf16[512,1024]{1,0:T(8,128)(2,1)} custom-call(bf16[512,4096]{1,0:T(8,128)(2,1)S(1)} %get-tuple-element.11.weight, bf16[256,1024]{1,0:T(8,128)(2,1)S(1)} %collective-permute-done.20.refs_0_, bf16[256,1024]{1,0:T(8,128)(2,1)S(1)} %collective-permute-done.21.refs_1_, f32[512,128]{1,0:T(8,128)S(1)} %get-tuple-element.14.refs_2_, ...), custom_call_target="tpu_custom_call" | custom-call | flops 536870912 | bytes 1572864 | tf_op jit(solution)/shard_map/product/pallas_call | solution.py:184
  (14 shorter events, 0.0 us)
Async XLA Ops:
  0.0 6.2 %collective-permute-start.2 = (bf16[256,256]{1,0:T(8,128)(2,1)}, bf16[256,256]{1,0:T(8,128)(2,1)S(1)}, u32[]{:S(2)}, u32[]{:S(2)}) collective-permute-start(bf16[256,256]{1,0:T(8,128)(2,1)} %refs_4_.1), channel_id=1, source_target_pairs={{0,8},{2,6},{4,12},{6,2},{8,0},{10,18},{12,4},{14,22},{16,24},{18,... | collective-permute-start | bytes 393224 | tf_op jit(solution)/shard_map/ppermute | solution.py:59
  6.2 14.9 %collective-permute-start.17 = (bf16[256,1024]{1,0:T(8,128)(2,1)}, bf16[256,1024]{1,0:T(8,128)(2,1)S(1)}, u32[]{:S(2)}, u32[]{:S(2)}) collective-permute-start(bf16[256,1024]{1,0:T(8,128)(2,1)} %refs_0_.3), channel_id=1, source_target_pairs={{0,8},{2,6},{4,12},{6,2},{8,0},{10,18},{12,4},{14,22},{16,24},{18,... | collective-permute-start | bytes 1572872 | tf_op jit(solution)/shard_map/ppermute | solution.py:59
  8.2 6.4 %collective-permute-start.4 = (bf16[256,256]{1,0:T(8,128)(2,1)S(1)}, bf16[256,256]{1,0:T(8,128)(2,1)S(1)}, u32[]{:S(2)}, u32[]{:S(2)}) collective-permute-start(bf16[256,256]{1,0:T(8,128)(2,1)S(1)} %collective-permute-done.2.refs_5_), channel_id=1, source_target_pairs={{0,4},{2,10},{4,0},{6,14},{8,16},{10,2},{12,20},{14,6},{16,8},{18,... | collective-permute-start | bytes 393224 | tf_op jit(solution)/shard_map/ppermute | solution.py:59
  14.6 6.4 %collective-permute-start.6 = (bf16[256,256]{1,0:T(8,128)(2,1)S(1)}, bf16[256,256]{1,0:T(8,128)(2,1)S(1)}, u32[]{:S(2)}, u32[]{:S(2)}) collective-permute-start(bf16[256,256]{1,0:T(8,128)(2,1)S(1)} %collective-permute-done.4.refs_7_), channel_id=1, source_target_pairs={{0,8},{2,6},{4,12},{6,2},{8,0},{10,18},{12,4},{14,22},{16,24},{18,... | collective-permute-start | bytes 393224 | tf_op jit(solution)/shard_map/ppermute | solution.py:59
  15.8 17.9 %collective-permute-start.22 = (bf16[256,1024]{1,0:T(8,128)(2,1)}, bf16[256,1024]{1,0:T(8,128)(2,1)S(1)}, u32[]{:S(2)}, u32[]{:S(2)}) collective-permute-start(bf16[256,1024]{1,0:T(8,128)(2,1)} %refs_0_.3), channel_id=1, source_target_pairs={{0,4},{2,10},{4,0},{6,14},{8,16},{10,2},{12,20},{14,6},{16,8},{18,... | collective-permute-start | bytes 1572872 | tf_op jit(solution)/shard_map/ppermute | solution.py:59
  21.1 16.0 %collective-permute-start.18 = (bf16[256,1024]{1,0:T(8,128)(2,1)S(1)}, bf16[256,1024]{1,0:T(8,128)(2,1)S(1)}, u32[]{:S(2)}, u32[]{:S(2)}) collective-permute-start(bf16[256,1024]{1,0:T(8,128)(2,1)S(1)} %collective-permute-done.17.refs_1_), channel_id=1, source_target_pairs={{0,4},{2,10},{4,0},{6,14},{8,16},{10,2},{12,20},{14,6},{16,8},{18,... | collective-permute-start | bytes 1572872 | tf_op jit(solution)/shard_map/ppermute | solution.py:59
  22.6 9.6 %collective-permute-start.3 = (bf16[256,256]{1,0:T(8,128)(2,1)}, bf16[256,256]{1,0:T(8,128)(2,1)S(1)}, u32[]{:S(2)}, u32[]{:S(2)}) collective-permute-start(bf16[256,256]{1,0:T(8,128)(2,1)} %refs_4_.1), channel_id=1, source_target_pairs={{0,4},{2,10},{4,0},{6,14},{8,16},{10,2},{12,20},{14,6},{16,8},{18,... | collective-permute-start | bytes 393224 | tf_op jit(solution)/shard_map/ppermute | solution.py:59
  23.1 10.6 %collective-permute-start.8 = (bf16[256,256]{1,0:T(8,128)(2,1)S(1)}, bf16[256,256]{1,0:T(8,128)(2,1)S(1)}, u32[]{:S(2)}, u32[]{:S(2)}) collective-permute-start(bf16[256,256]{1,0:T(8,128)(2,1)S(1)} %collective-permute-done.6.refs_9_), channel_id=1, source_target_pairs={{0,4},{2,10},{4,0},{6,14},{8,16},{10,2},{12,20},{14,6},{16,8},{18,... | collective-permute-start | bytes 393224 | tf_op jit(solution)/shard_map/ppermute | solution.py:59
  24.6 12.4 %collective-permute-start = (bf16[256,256]{1,0:T(8,128)(2,1)}, bf16[256,256]{1,0:T(8,128)(2,1)S(1)}, u32[]{:S(2)}, u32[]{:S(2)}) collective-permute-start(bf16[256,256]{1,0:T(8,128)(2,1)} %refs_0_.2), channel_id=1, source_target_pairs={{0,1},{1,0},{2,3},{3,2},{4,5},{5,4},{6,7},{7,6},{8,9},{9,8},{10,11... | collective-permute-start | bytes 393224 | tf_op jit(solution)/shard_map/ppermute | solution.py:21
  32.2 44.6 %copy-start = (bf16[256,1024]{1,0:T(8,128)(2,1)S(1)}, bf16[256,1024]{1,0:T(8,128)(2,1)}, u32[]{:S(2)}) copy-start(bf16[256,1024]{1,0:T(8,128)(2,1)} %refs_0_.3) | copy-start | bytes 1572868
  32.2 3.9 %collective-permute-start.1 = (s32[16,256]{1,0:T(8,128)}, s32[16,256]{1,0:T(8,128)S(1)}, u32[]{:S(2)}, u32[]{:S(2)}) collective-permute-start(s32[16,256]{1,0:T(8,128)} %bitcast.1), channel_id=1, source_target_pairs={{0,1},{1,0},{2,3},{3,2},{4,5},{5,4},{6,7},{7,6},{8,9},{9,8},{10,11... | collective-permute-start | bytes 49160 | tf_op jit(solution)/shard_map/ppermute | solution.py:21
  33.7 4.6 %collective-permute-start.9 = (bf16[256,256]{1,0:T(8,128)(2,1)}, bf16[256,256]{1,0:T(8,128)(2,1)S(1)}, u32[]{:S(2)}, u32[]{:S(2)}) collective-permute-start(bf16[256,256]{1,0:T(8,128)(2,1)} %refs_4_.1), channel_id=1, source_target_pairs={{0,2},{2,0},{4,6},{6,4},{8,10},{10,8},{12,14},{14,12},{16,18},{18,... | collective-permute-start | bytes 393224 | tf_op jit(solution)/shard_map/ppermute | solution.py:21
  33.7 5.6 %collective-permute-start.5 = (bf16[256,256]{1,0:T(8,128)(2,1)S(1)}, bf16[256,256]{1,0:T(8,128)(2,1)S(1)}, u32[]{:S(2)}, u32[]{:S(2)}) collective-permute-start(bf16[256,256]{1,0:T(8,128)(2,1)S(1)} %collective-permute-done.3.refs_6_), channel_id=1, source_target_pairs={{0,8},{2,6},{4,12},{6,2},{8,0},{10,18},{12,4},{14,22},{16,24},{18,... | collective-permute-start | bytes 393224 | tf_op jit(solution)/shard_map/ppermute | solution.py:59
  36.1 12.5 %collective-permute-start.23 = (bf16[256,1024]{1,0:T(8,128)(2,1)S(1)}, bf16[256,1024]{1,0:T(8,128)(2,1)S(1)}, u32[]{:S(2)}, u32[]{:S(2)}) collective-permute-start(bf16[256,1024]{1,0:T(8,128)(2,1)S(1)} %collective-permute-done.22.refs_2_), channel_id=1, source_target_pairs={{0,8},{2,6},{4,12},{6,2},{8,0},{10,18},{12,4},{14,22},{16,24},{18,... | collective-permute-start | bytes 1572872 | tf_op jit(solution)/shard_map/ppermute | solution.py:59
  37.0 2.4 %collective-permute-start.10 = (bf16[256,256]{1,0:T(8,128)(2,1)S(1)}, bf16[256,256]{1,0:T(8,128)(2,1)S(1)}, u32[]{:S(2)}, u32[]{:S(2)}) collective-permute-start(bf16[256,256]{1,0:T(8,128)(2,1)S(1)} %collective-permute-done.2.refs_5_), channel_id=1, source_target_pairs={{0,2},{2,0},{4,6},{6,4},{8,10},{10,8},{12,14},{14,12},{16,18},{18,... | collective-permute-start | bytes 393224 | tf_op jit(solution)/shard_map/ppermute | solution.py:21
  37.0 16.2 %collective-permute-start.19 = (bf16[256,1024]{1,0:T(8,128)(2,1)S(1)}, bf16[256,1024]{1,0:T(8,128)(2,1)S(1)}, u32[]{:S(2)}, u32[]{:S(2)}) collective-permute-start(bf16[256,1024]{1,0:T(8,128)(2,1)S(1)} %collective-permute-done.18.refs_3_), channel_id=1, source_target_pairs={{0,8},{2,6},{4,12},{6,2},{8,0},{10,18},{12,4},{14,22},{16,24},{18,... | collective-permute-start | bytes 1572872 | tf_op jit(solution)/shard_map/ppermute | solution.py:59
  38.2 2.1 %collective-permute-start.11 = (bf16[256,256]{1,0:T(8,128)(2,1)S(1)}, bf16[256,256]{1,0:T(8,128)(2,1)S(1)}, u32[]{:S(2)}, u32[]{:S(2)}) collective-permute-start(bf16[256,256]{1,0:T(8,128)(2,1)S(1)} %collective-permute-done.3.refs_6_), channel_id=1, source_target_pairs={{0,2},{2,0},{4,6},{6,4},{8,10},{10,8},{12,14},{14,12},{16,18},{18,... | collective-permute-start | bytes 393224 | tf_op jit(solution)/shard_map/ppermute | solution.py:21
  39.3 1.8 %collective-permute-start.12 = (bf16[256,256]{1,0:T(8,128)(2,1)S(1)}, bf16[256,256]{1,0:T(8,128)(2,1)S(1)}, u32[]{:S(2)}, u32[]{:S(2)}) collective-permute-start(bf16[256,256]{1,0:T(8,128)(2,1)S(1)} %collective-permute-done.4.refs_7_), channel_id=1, source_target_pairs={{0,2},{2,0},{4,6},{6,4},{8,10},{10,8},{12,14},{14,12},{16,18},{18,... | collective-permute-start | bytes 393224 | tf_op jit(solution)/shard_map/ppermute | solution.py:21
  39.4 16.0 %collective-permute-start.28 = (bf16[256,1024]{1,0:T(8,128)(2,1)}, bf16[256,1024]{1,0:T(8,128)(2,1)S(1)}, u32[]{:S(2)}, u32[]{:S(2)}) collective-permute-start(bf16[256,1024]{1,0:T(8,128)(2,1)} %refs_0_.3), channel_id=1, source_target_pairs={{0,2},{2,0},{4,6},{6,4},{8,10},{10,8},{12,14},{14,12},{16,18},{18,... | collective-permute-start | bytes 1572872 | tf_op jit(solution)/shard_map/ppermute | solution.py:21
  40.3 6.4 %collective-permute-start.7 = (bf16[256,256]{1,0:T(8,128)(2,1)S(1)}, bf16[256,256]{1,0:T(8,128)(2,1)S(1)}, u32[]{:S(2)}, u32[]{:S(2)}) collective-permute-start(bf16[256,256]{1,0:T(8,128)(2,1)S(1)} %collective-permute-done.5.refs_8_), channel_id=1, source_target_pairs={{0,4},{2,10},{4,0},{6,14},{8,16},{10,2},{12,20},{14,6},{16,8},{18,... | collective-permute-start | bytes 393224 | tf_op jit(solution)/shard_map/ppermute | solution.py:59
  41.1 5.6 %collective-permute-start.13 = (bf16[256,256]{1,0:T(8,128)(2,1)S(1)}, bf16[256,256]{1,0:T(8,128)(2,1)S(1)}, u32[]{:S(2)}, u32[]{:S(2)}) collective-permute-start(bf16[256,256]{1,0:T(8,128)(2,1)S(1)} %collective-permute-done.5.refs_8_), channel_id=1, source_target_pairs={{0,2},{2,0},{4,6},{6,4},{8,10},{10,8},{12,14},{14,12},{16,18},{18,... | collective-permute-start | bytes 393224 | tf_op jit(solution)/shard_map/ppermute | solution.py:21
  46.7 1.3 %collective-permute-start.14 = (bf16[256,256]{1,0:T(8,128)(2,1)S(1)}, bf16[256,256]{1,0:T(8,128)(2,1)S(1)}, u32[]{:S(2)}, u32[]{:S(2)}) collective-permute-start(bf16[256,256]{1,0:T(8,128)(2,1)S(1)} %collective-permute-done.6.refs_9_), channel_id=1, source_target_pairs={{0,2},{2,0},{4,6},{6,4},{8,10},{10,8},{12,14},{14,12},{16,18},{18,... | collective-permute-start | bytes 393224 | tf_op jit(solution)/shard_map/ppermute | solution.py:21
  46.8 1.5 %collective-permute-start.15 = (bf16[256,256]{1,0:T(8,128)(2,1)S(1)}, bf16[256,256]{1,0:T(8,128)(2,1)S(1)}, u32[]{:S(2)}, u32[]{:S(2)}) collective-permute-start(bf16[256,256]{1,0:T(8,128)(2,1)S(1)} %collective-permute-done.7.refs_10_), channel_id=1, source_target_pairs={{0,2},{2,0},{4,6},{6,4},{8,10},{10,8},{12,14},{14,12},{16,18},{18,... | collective-permute-start | bytes 393224 | tf_op jit(solution)/shard_map/ppermute | solution.py:21
  48.1 8.8 %collective-permute-start.29 = (bf16[256,1024]{1,0:T(8,128)(2,1)S(1)}, bf16[256,1024]{1,0:T(8,128)(2,1)S(1)}, u32[]{:S(2)}, u32[]{:S(2)}) collective-permute-start(bf16[256,1024]{1,0:T(8,128)(2,1)S(1)} %collective-permute-done.17.refs_1_), channel_id=1, source_target_pairs={{0,2},{2,0},{4,6},{6,4},{8,10},{10,8},{12,14},{14,12},{16,18},{18,... | collective-permute-start | bytes 1572872 | tf_op jit(solution)/shard_map/ppermute | solution.py:21
  48.3 9.0 %collective-permute-start.30 = (bf16[256,1024]{1,0:T(8,128)(2,1)S(1)}, bf16[256,1024]{1,0:T(8,128)(2,1)S(1)}, u32[]{:S(2)}, u32[]{:S(2)}) collective-permute-start(bf16[256,1024]{1,0:T(8,128)(2,1)S(1)} %collective-permute-done.22.refs_2_), channel_id=1, source_target_pairs={{0,2},{2,0},{4,6},{6,4},{8,10},{10,8},{12,14},{14,12},{16,18},{18,... | collective-permute-start | bytes 1572872 | tf_op jit(solution)/shard_map/ppermute | solution.py:21
  48.6 9.2 %collective-permute-start.24 = (bf16[256,1024]{1,0:T(8,128)(2,1)S(1)}, bf16[256,1024]{1,0:T(8,128)(2,1)S(1)}, u32[]{:S(2)}, u32[]{:S(2)}) collective-permute-start(bf16[256,1024]{1,0:T(8,128)(2,1)S(1)} %collective-permute-done.23.refs_0_), channel_id=1, source_target_pairs={{0,4},{2,10},{4,0},{6,14},{8,16},{10,2},{12,20},{14,6},{16,8},{18,... | collective-permute-start | bytes 1572872 | tf_op jit(solution)/shard_map/ppermute | solution.py:59
  53.2 10.2 %collective-permute-start.20 = (bf16[256,1024]{1,0:T(8,128)(2,1)S(1)}, bf16[256,1024]{1,0:T(8,128)(2,1)S(1)}, u32[]{:S(2)}, u32[]{:S(2)}) collective-permute-start(bf16[256,1024]{1,0:T(8,128)(2,1)S(1)} %collective-permute-done.19.refs_1_), channel_id=1, source_target_pairs={{0,4},{2,10},{4,0},{6,14},{8,16},{10,2},{12,20},{14,6},{16,8},{18,... | collective-permute-start | bytes 1572872 | tf_op jit(solution)/shard_map/ppermute | solution.py:59
  55.4 1.3 %collective-permute-start.16 = (bf16[256,256]{1,0:T(8,128)(2,1)S(1)}, bf16[256,256]{1,0:T(8,128)(2,1)S(1)}, u32[]{:S(2)}, u32[]{:S(2)}) collective-permute-start(bf16[256,256]{1,0:T(8,128)(2,1)S(1)} %collective-permute-done.8.refs_11_), channel_id=1, source_target_pairs={{0,2},{2,0},{4,6},{6,4},{8,10},{10,8},{12,14},{14,12},{16,18},{18,... | collective-permute-start | bytes 393224 | tf_op jit(solution)/shard_map/ppermute | solution.py:21
  56.7 20.0 %collective-permute-start.31 = (bf16[256,1024]{1,0:T(8,128)(2,1)S(1)}, bf16[256,1024]{1,0:T(8,128)(2,1)S(1)}, u32[]{:S(2)}, u32[]{:S(2)}) collective-permute-start(bf16[256,1024]{1,0:T(8,128)(2,1)S(1)} %collective-permute-done.18.refs_3_), channel_id=1, source_target_pairs={{0,2},{2,0},{4,6},{6,4},{8,10},{10,8},{12,14},{14,12},{16,18},{18,... | collective-permute-start | bytes 1572872 | tf_op jit(solution)/shard_map/ppermute | solution.py:21
  56.9 22.2 %collective-permute-start.25 = (bf16[256,1024]{1,0:T(8,128)(2,1)S(1)}, bf16[256,1024]{1,0:T(8,128)(2,1)S(1)}, u32[]{:S(2)}, u32[]{:S(2)}) collective-permute-start(bf16[256,1024]{1,0:T(8,128)(2,1)S(1)} %collective-permute-done.23.refs_0_), channel_id=1, source_target_pairs={{0,2},{2,0},{4,6},{6,4},{8,10},{10,8},{12,14},{14,12},{16,18},{18,... | collective-permute-start | bytes 1572872 | tf_op jit(solution)/shard_map/ppermute | solution.py:21
  57.3 21.9 %collective-permute-start.26 = (bf16[256,1024]{1,0:T(8,128)(2,1)S(1)}, bf16[256,1024]{1,0:T(8,128)(2,1)S(1)}, u32[]{:S(2)}, u32[]{:S(2)}) collective-permute-start(bf16[256,1024]{1,0:T(8,128)(2,1)S(1)} %collective-permute-done.19.refs_1_), channel_id=1, source_target_pairs={{0,2},{2,0},{4,6},{6,4},{8,10},{10,8},{12,14},{14,12},{16,18},{18,... | collective-permute-start | bytes 1572872 | tf_op jit(solution)/shard_map/ppermute | solution.py:21
  57.8 21.3 %collective-permute-start.27 = (bf16[256,1024]{1,0:T(8,128)(2,1)S(1)}, bf16[256,1024]{1,0:T(8,128)(2,1)S(1)}, u32[]{:S(2)}, u32[]{:S(2)}) collective-permute-start(bf16[256,1024]{1,0:T(8,128)(2,1)S(1)} %collective-permute-done.24.refs_2_), channel_id=1, source_target_pairs={{0,2},{2,0},{4,6},{6,4},{8,10},{10,8},{12,14},{14,12},{16,18},{18,... | collective-permute-start | bytes 1572872 | tf_op jit(solution)/shard_map/ppermute | solution.py:21
  63.4 17.5 %collective-permute-start.21 = (bf16[256,1024]{1,0:T(8,128)(2,1)S(1)}, bf16[256,1024]{1,0:T(8,128)(2,1)S(1)}, u32[]{:S(2)}, u32[]{:S(2)}) collective-permute-start(bf16[256,1024]{1,0:T(8,128)(2,1)S(1)} %collective-permute-done.20.refs_0_), channel_id=1, source_target_pairs={{0,2},{2,0},{4,6},{6,4},{8,10},{10,8},{12,14},{14,12},{16,18},{18,... | collective-permute-start | bytes 1572872 | tf_op jit(solution)/shard_map/ppermute | solution.py:21
  63.5 0.9 %copy-start.1 = (bf16[256,256]{1,0:T(8,128)(2,1)S(1)}, bf16[256,256]{1,0:T(8,128)(2,1)}, u32[]{:S(2)}) copy-start(bf16[256,256]{1,0:T(8,128)(2,1)} %refs_0_.2) | copy-start | bytes 393220
  64.4 0.9 %copy-start.2 = (bf16[256,256]{1,0:T(8,128)(2,1)S(1)}, bf16[256,256]{1,0:T(8,128)(2,1)}, u32[]{:S(2)}) copy-start(bf16[256,256]{1,0:T(8,128)(2,1)} %refs_4_.1) | copy-start | bytes 393220
  65.3 0.7 copy-start.3
  66.1 0.7 copy-start.4

commit v2 on v1

v2 whole, which is shorter than its diff:
```python
import functools
import math

import jax
import jax.numpy as jnp
from jax import lax
from jax.experimental import pallas as pl
from jax.experimental.pallas import tpu as pltpu
from jax.sharding import PartitionSpec as P

SHARPNESS = 32.0
EPSILON = 1e-06
LANES = 128
CORE_BIT = 1
Y_BIT = 2
VMEM = pl.BlockSpec(memory_space=pltpu.VMEM)
SMALL = pl.CostEstimate(flops=1024, bytes_accessed=1024, transcendentals=0)


def swap(value, axis, size, bit):
    return lax.ppermute(value, axis, [(i, i ^ bit) for i in range(size)])


def gather_steps(size):
    n_z = size // 4
    steps = []
    if n_z == 4:
        across = [(i ^ 12) if (i >> 2) in (1, 2) else (i ^ Y_BIT) for i in range(size)]
        inside = [i ^ 4 for i in range(size)]
        for sent, first in ((0, inside), (0, across), (1, across), (2, inside), (3, inside), (4, across), (5, across)):
            second = across if first is inside else inside
            steps.append((sent, [(i, second[i] if i & CORE_BIT else first[i]) for i in range(size)]))
        return steps
    held = 1
    for bit in [Y_BIT << k for k in range(n_z.bit_length())]:
        steps += [(sent, [(i, i ^ bit) for i in range(size)]) for sent in range(held)]
        held *= 2
    return steps


def owners(size):
    held = [[i] for i in range(size)]
    for sent, pairs in gather_steps(size):
        source = {target: i for i, target in pairs}
        moved = [held[source[i]][sent] for i in range(size)]
        for i in range(size):
            held[i].append(moved[i])
    held = [held[i] + held[i ^ CORE_BIT] for i in range(size)]
    assert all(sorted(row) == list(range(size)) for row in held)
    return held


PAIR_STEPS = ((False, 4, 8), (False, 14, 2), (True, 2, 4), (True, 2, 2))
PAIR_OFFSETS = ((4, 14, 6), (8, 2, 12, 10))

ORDER = {
    "F1": ("S1", "S2"),
    "F2": ("S1", "S2", "S3", "S4"),
    "F3": ("S3", "S4"),
    "F4": ("S3", "S4"),
    "F5": ("Sx",),
    "F7": ("K",),
    "D7": ("P2",),
    "Sx": ("Ox",),
    "ScSx": ("Sx",),
}
MERGED = False
GROUPS = (4, 3, 1)


class Work:
    def __init__(self, order):
        self.order, self.made, self.makers = order, {}, {}

    def add(self, name, operand, make):
        self.makers[name] = (operand, make)

    def get(self, name):
        if name not in self.made:
            operand, make = self.makers[name]
            value = operand()
            others = [self.get(other) for other in self.order.get(name, ())]
            if others:
                value = lax.optimization_barrier((value, others))[0]
            self.made[name] = make(value)
        return self.made[name]


def share_sims(work, sims, obs, codes, n_row, n_col):
    rows, depth = obs.shape[0], sims.shape[0]

    def add_swap(name, of, axis, size, bit):
        work.add(name, lambda: work.get(of), lambda value: swap(value, axis, size, bit))

    work.add("own", lambda: sims, lambda value: value)
    work.add("obs0", lambda: obs, lambda value: value)
    work.add("codes0", lambda: codes, lambda value: value)
    if (n_row, n_col) != (16, 2):
        names = ["own"]
        for k, (sent, pairs) in enumerate(gather_steps(n_row)):
            names.append(f"S{k + 1}")
            work.add(
                names[-1],
                lambda of=names[sent]: work.get(of),
                lambda value, pairs=pairs: lax.ppermute(value, "row", pairs),
            )
        names += [f"{name}c" for name in names]
        for name in names[n_row // 2 :]:
            add_swap(name, name[:-1], "row", n_row, CORE_BIT)
        for what in ("obs", "codes"):
            names.append(f"{what}0")
            for k in range(1, n_col):
                top = 1 << (k.bit_length() - 1)
                names.append(f"{what}{k}")
                add_swap(names[-1], f"{what}{k ^ top}", "col", n_col, top)
        at = [(k, 0) for k in range(len(names))]
        n = n_row + n_col
        table = [held for held in owners(n_row) for _ in range(n_col)]
        return names, [(a, a) for a in at[:n_row]], at[n_row:n], at[n:], table
    for k, (again, off_a, off_b) in enumerate(PAIR_STEPS):
        pairs = [(2 * r + c, 2 * (r ^ (off_b if c else off_a)) + c) for r in range(n_row) for c in range(2)]
        work.add(
            f"S{k + 1}",
            lambda of="S1" if again else "own": work.get(of),
            lambda value, pairs=pairs: lax.ppermute(value, ("row", "col"), pairs),
        )
    arrived = lambda: [work.get(f"S{k + 1}") for k in range(4)]
    if MERGED:
        work.add("mine", lambda: arrived() + [obs, codes], lambda parts: jnp.concatenate(parts, axis=0))
        obs_at = [(1, 4 * depth), (2, 4 * depth)]
        names = ["own", "mine", "Sx"]
    else:
        work.add("mine", arrived, lambda parts: jnp.concatenate(parts, axis=0))
        work.add("both", lambda: [obs, codes], lambda parts: jnp.concatenate(parts, axis=0))
        add_swap("Ox", "both", "col", n_col, 1)
        names = ["own", "mine", "Sx"]
        obs_at = [(6, 0), (7, 0)]
    add_swap("Sx", "mine", "col", n_col, 1)
    blocks = [((0, 0), (0, 0))]
    for k in range(3):
        blocks += [((1, k * depth),) * 2, ((2, k * depth),) * 2]
    blocks += [((2, 3 * depth), (1, 3 * depth))]
    blocks += [tuple((s + len(names), k) for s, k in block) for block in blocks]
    table = []
    for r in range(n_row):
        for c in range(2):
            here, there = PAIR_OFFSETS[c], PAIR_OFFSETS[1 - c]
            offs = [0] + [o for k in range(3) for o in (here[k], there[k])] + [PAIR_OFFSETS[1][3]]
            table.append([r ^ o for o in offs] + [r ^ CORE_BIT ^ o for o in offs])
            assert sorted(table[-1]) == list(range(n_row))
    for name in tuple(names):
        names.append(f"Sc{name}")
        add_swap(names[-1], name, "row", n_row, CORE_BIT)
    if not MERGED:
        names += ["both", "Ox"]
    return names, blocks, obs_at, [(s, k + rows) for s, k in obs_at], table


def kinds_of_place(n_row, n_col, table):
    held = owners(n_row)
    kind_of, seen = [], []
    for r in range(n_row):
        offsets = [r ^ owner for owner in held[r]]
        kind_of.append([])
        for c in range(n_col):
            what = (offsets, [held[r].index(owner) for owner in table[r * n_col + c]])
            if what not in seen:
                seen.append(what)
            kind_of[-1].append(seen.index(what))
    return kind_of, [w[0] for w in seen], [w[1] for w in seen]


def choose(index, options):
    if all(o == options[0] for o in options):
        return options[0]
    out = jnp.int32(options[0])
    for i, option in enumerate(options[1:], 1):
        out = jnp.where(index == i, option, out)
    return out


def weight_kernel(blocks, obs_at, codes_at, kinds, depth, rows, near, n_in, *refs):
    n_sim, n_piece = len(blocks), len(obs_at)
    arrays, (weight_out, total_out) = refs[:n_in], refs[n_in : n_in + 2]
    obs_scr, low_scr, high_scr, value_scr, square_scr, factor_scr, owner_scr = refs[n_in + 2 :]
    my_row, my_col = lax.axis_index("row"), lax.axis_index("col")
    n_obs = n_piece * rows
    groups = depth // LANES

    kind_of, offsets, places = kinds
    n_col = len(kind_of[0])
    kind = choose(my_row * n_col + my_col, [k for row in kind_of for k in row])
    for b in range(n_sim):
        owner_scr[b] = lax.bitwise_xor(my_row, choose(kind, [o[b] for o in offsets])) * groups

    for i in range(n_piece):
        at = pl.ds(pl.multiple_of(lax.bitwise_xor(my_col, i) * rows, rows), rows)
        (s, k), (t, m) = obs_at[i], codes_at[i]
        obs_scr[at, :] = arrays[s][k : k + rows, :]
        codes = arrays[t][m : m + 2 * near, :rows].astype(jnp.float32).T.astype(jnp.int32)
        pad = jnp.zeros((rows, LANES - near), jnp.int32)
        high_scr[at, :] = jnp.concatenate([codes[:, :near], pad - 1], axis=1)
        low_scr[at, :] = jnp.concatenate([codes[:, near:], pad], axis=1)
    obs = obs_scr[...]
    obs_float = obs.astype(jnp.float32)
    square_scr[...] = jnp.broadcast_to(jnp.sum(obs_float * obs_float, axis=1, keepdims=True), (n_obs, LANES))

    for b, at_cols in enumerate(blocks):
        block, at_one = [arrays[s][k : k + depth, :] for s, k in at_cols]
        if at_cols[0] != at_cols[1]:
            block = jnp.where(my_col == 0, block, at_one)
        squares = block.astype(jnp.float32)
        squares = squares * squares
        folded = squares[:, :LANES]
        for g in range(1, block.shape[1] // LANES):
            folded += squares[:, g * LANES : (g + 1) * LANES]
        sim_square = jnp.sum(folded.T, axis=0, keepdims=True)
        cross = lax.dot_general(obs, block, (((1,), (1,)), ((), ())), preferred_element_type=jnp.float32)
        place = choose(kind, [p[b] for p in places]) * groups
        for g in range(groups):
            at = slice(g * LANES, (g + 1) * LANES)
            value_scr[place + g] = sim_square[:, at] - 2.0 * cross[:, at]

    tile = 8
    some = min(n_obs, 64)

    def add_near(t, carry):
        for r in range(some // tile):
            at = pl.ds(pl.multiple_of(t * some + r * tile, tile), tile)
            low, high = low_scr[at, :], high_scr[at, :]
            total = jnp.zeros((tile, LANES), jnp.float32)
            for c in range(n_sim * groups):
                found = jnp.take_along_axis(value_scr[c, at, :], low, axis=1)
                total += jnp.where(high == owner_scr[c // groups] + c % groups, found, 0.0)
            factor_scr[at, :] = total
        return carry

    lax.fori_loop(0, n_obs // some, add_near, 0)
    width = square_scr[...] + jnp.sum(factor_scr[...], axis=1, keepdims=True) / near + EPSILON
    factor_scr[...] = (-SHARPNESS * math.log2(math.e)) / width
    part = min(n_obs, 32)

    def weigh(t, carry):
        at = pl.ds(pl.multiple_of(t * part, part), part)
        factor, square = factor_scr[at, :], square_scr[at, :]
        total = jnp.zeros((part, LANES), jnp.float32)
        for c in range(n_sim * groups):
            weight = jnp.exp2(factor * (square + value_scr[c, at, :]))
            weight_out[c // groups, at, c % groups * LANES : (c % groups + 1) * LANES] = weight.astype(jnp.bfloat16)
            total += weight
        total_out[at, :] = total
        return carry

    lax.fori_loop(0, n_obs // part, weigh, 0)
    total_out[...] = jnp.broadcast_to(jnp.sum(total_out[...], axis=1, keepdims=True), total_out.shape)


def product_kernel(columns, first, last, weight, *refs):
    blocks, rest, out = refs[: len(columns)], refs[len(columns) : -1], refs[-1]
    so_far = None if first else rest[-1]
    total_ref = rest[0] if last else None
    cells = out.shape[1]
    step = min(cells, 256)
    for j in range(cells // step):
        at = slice(j * step, (j + 1) * step)
        total = None if so_far is None else so_far[:, at]
        for column, block in zip(columns, blocks):
            term = jnp.dot(
                weight[column], block[:, at], preferred_element_type=jnp.float32
            )
            total = term if total is None else total + term
        if total_ref is not None:
            total = total / total_ref[:, :1]
        out[:, at] = total.astype(out.dtype)


def call(kernel, vmem, **kw):
    return pl.pallas_call(kernel, compiler_params=pltpu.CompilerParams(vmem_limit_bytes=vmem << 20), **kw)


def per_device(n_row, n_col, obs_summaries, sim_summaries, neighbours, field):
    f32, bf16 = jnp.float32, jnp.bfloat16
    rows, dims = obs_summaries.shape
    depth, cells = field.shape

    index = neighbours.T
    codes = jnp.concatenate([index // LANES, index % LANES], axis=0).astype(bf16)
    work = Work(ORDER if (n_row, n_col) == (16, 2) else {})
    names, at_blocks, at_obs, at_codes, table = share_sims(work, sim_summaries, obs_summaries, codes, n_row, n_col)
    n_sim, n_obs = n_row, n_col * rows
    kinds = kinds_of_place(n_row, n_col, table)
    weigh = call(
        functools.partial(
            weight_kernel, at_blocks, at_obs, at_codes, kinds, depth, rows, neighbours.shape[1], len(names)
        ),
        40,
        in_specs=[VMEM] * len(names),
        out_specs=[VMEM] * 2,
        out_shape=[
            jax.ShapeDtypeStruct((n_sim, n_obs, depth), bf16),
            jax.ShapeDtypeStruct((n_obs, LANES), f32),
        ],
        scratch_shapes=[
            pltpu.VMEM((n_obs, dims), bf16),
            pltpu.VMEM((n_obs, LANES), jnp.int32),
            pltpu.VMEM((n_obs, LANES), jnp.int32),
            pltpu.VMEM((n_sim * depth // LANES, n_obs, LANES), f32),
            pltpu.VMEM((n_obs, LANES), f32),
            pltpu.VMEM((n_obs, LANES), f32),
            pltpu.SMEM((n_sim,), jnp.int32),
        ],
        cost_estimate=SMALL,
        name="weights",
    )
    work.add("K", lambda: [work.get(name) for name in names], lambda arrays: weigh(*arrays))

    n_half = n_sim // 2
    work.add("F0", lambda: field, lambda value: value)
    for k, (sent, pairs) in enumerate(gather_steps(n_row)):
        work.add(
            f"F{k + 1}",
            lambda sent=sent: work.get(f"F{sent}"),
            lambda value, pairs=pairs: lax.ppermute(value, "row", pairs),
        )
    for k in range(n_half):
        work.add(f"D{k}", lambda k=k: work.get(f"F{k}"), lambda value: swap(value, "row", n_row, CORE_BIT))

    def product(first, last, parts):
        done, (weight, total), before, both = last == n_half, *parts
        columns = [*range(first, last), *range(n_half + first, n_half + last)]
        extra = ([total] if done else []) + ([] if before is None else [before])
        return call(
            functools.partial(product_kernel, columns, before is None, done),
            28,
            in_specs=[VMEM] * (1 + len(both) + len(extra)),
            out_specs=VMEM,
            out_shape=jax.ShapeDtypeStruct((n_obs, cells), bf16 if done else f32),
            cost_estimate=SMALL,
            name="product",
        )(weight, *both, *extra)

    groups = GROUPS if n_half == sum(GROUPS) else (n_half // 2, n_half - n_half // 2 - 1, 1)
    first = 0
    for g, count in enumerate(groups):
        at = range(first, first + count)
        work.add(
            f"P{g + 1}",
            lambda g=g, at=at: (
                work.get("K"),
                work.get(f"P{g}") if g else None,
                [work.get(f"F{k}") for k in at] + [work.get(f"D{k}") for k in at],
            ),
            lambda parts, at=at: product(at.start, at.stop, parts),
        )
        first += count
    return work.get(f"P{len(groups)}")


def solution(mesh):
    return jax.shard_map(
        functools.partial(per_device, mesh.shape["row"], mesh.shape["col"]),
        mesh=mesh,
        in_specs=(
            P(("row", "col"), None),
            P("row", None),
            P(("row", "col"), None),
            P("row", "col"),
        ),
        out_specs=P("row", "col"),
        check_vma=False,
    )
```

time: 82.9 us -> 70.1 us (0.85)
  waiting for transfers between devices: 36.4 us -> 30.9 us
  Pallas kernels: 15.9 us -> 12.2 us
  starting transfers between devices: 27.1 us -> 24.1 us
  local copies, waits for them, and re-layouts: 3.21 us -> 0.94 us
  other arithmetic: 0 us -> 1.65 us
    ppermute x14 -> x11, waiting for transfers between devices: 32.2 us -> 20.6 us  [the longest x4 11.1 us: share_sims(): lax.ppermute(value, ('row', 'col'), pairs)]
    ppermute x18 -> x13, waiting for transfers between devices: 4.21 us -> 10.4 us  [swap(): return lax.ppermute(value, axis, [(i, i ^ bit) for i in range(size)])]
    pallas_call x4, Pallas kernels: 15.9 us -> 12.2 us  [the longest x1 6.34 us: per_device(): weigh(*arrays)]
    unnamed x10 -> x7, local copies, waits for them, and re-layouts: 3.21 us -> 0.93 us
    ppermute x14 -> x11, starting transfers between devices: 19.6 us -> 17.6 us  [the longest x7 9.08 us: per_device(): lax.ppermute(value, 'row', pairs)]
    ppermute x18 -> x13, starting transfers between devices: 7.54 us -> 6.51 us  [swap(): return lax.ppermute(value, axis, [(i, i ^ bit) for i in range(size)])]
    concatenate x0 -> x1, other arithmetic: none -> 0.92 us  [share_sims(): jnp.concatenate(parts, axis=0)]
  transfers between devices with their start and end apart: 32 -> 24, of which waited for: 12 -> 10; matrix products, arithmetic and copies ran while one was open for 0% -> 2% of each run, Pallas kernels for 17% -> 15%
where the time goes in v2:
time: 70.1 us; the launch traced here: 69.9 us
  waiting for transfers between devices  30.9 us (44%)
  starting transfers between devices  24.1 us (34%)
  Pallas kernels  12.2 us (17%)
  other arithmetic  1.65 us (2%)
  local copies, waits for them, and re-layouts  0.94 us (1%)
    ppermute x4, waiting for transfers between devices, share_sims(): lax.ppermute(value, ('row', 'col'), pairs)  11.1 us
    ppermute x13, waiting for transfers between devices, swap(): return lax.ppermute(value, axis, [(i, i ^ bit) for i in range(size)])  10.4 us
    ppermute x7, waiting for transfers between devices, per_device(): lax.ppermute(value, 'row', pairs)  9.43 us
    ppermute x7, starting transfers between devices, per_device(): lax.ppermute(value, 'row', pairs)  9.08 us
    ppermute x4, starting transfers between devices, share_sims(): lax.ppermute(value, ('row', 'col'), pairs)  8.55 us
    ppermute x13, starting transfers between devices, swap(): return lax.ppermute(value, axis, [(i, i ^ bit) for i in range(size)])  6.51 us
    pallas_call x1, Pallas kernels, per_device(): weigh(*arrays)  6.34 us
    pallas_call x3, Pallas kernels, product(): call(functools.partial(product_kernel, columns, before is None, done), 28...  5.81 us
  transfers between devices with their start and end apart: 24, of which 10 were waited for; matrix products, arithmetic and copies ran while one was open for 2% of the time, Pallas kernels for 15%

profile of v2, /device:TPU:0, one launch (start us, length us, event | category | flops | bytes accessed | tf_op | source)
XLA Modules:
  0.0 69.9 jit_solution(10897543986707110047)
XLA Ops:
  0.0 0.0 copy-start
  0.0 3.0 %collective-permute-start = (bf16[256,256]{1,0:T(8,128)(2,1)}, bf16[256,256]{1,0:T(8,128)(2,1)S(1)}, u32[]{:S(2)}, u32[]{:S(2)}) collective-permute-start(bf16[256,256]{1,0:T(8,128)(2,1)} %refs_0_.2), channel_id=1, source_target_pairs={{0,8},{1,17},{2,10},{3,19},{4,12},{5,21},{6,14},{7,23},{8,0},{9,25... | collective-permute-start | bytes 393224 | tf_op jit(solution)/shard_map/ppermute | solution.py:125
  3.0 3.4 %collective-permute-start.1 = (bf16[256,256]{1,0:T(8,128)(2,1)}, bf16[256,256]{1,0:T(8,128)(2,1)S(1)}, u32[]{:S(2)}, u32[]{:S(2)}) collective-permute-start(bf16[256,256]{1,0:T(8,128)(2,1)} %refs_0_.2), channel_id=1, source_target_pairs={{0,28},{1,5},{2,30},{3,7},{4,24},{5,1},{6,26},{7,3},{8,20},{9,13},... | collective-permute-start | bytes 393224 | tf_op jit(solution)/shard_map/ppermute | solution.py:125
  6.5 0.7 %fusion = (bf16[16,256]{1,0:T(8,128)(2,1)S(1)}, bf16[16,256]{1,0:T(8,128)(2,1)S(1)}) fusion(s32[256,16]{0,1:T(8,128)} %param.6), kind=kLoop, calls=%fused_computation.6 | loop fusion | flops 86016 | bytes 32768 | tf_op jit(solution)/shard_map/convert
  7.2 0.9 %pad_maximum_fusion.refs_6_ = bf16[288,256]{1,0:T(8,128)(2,1)S(1)} fusion(bf16[16,256]{1,0:T(8,128)(2,1)S(1)} %get-tuple-element.28, bf16[16,256]{1,0:T(8,128)(2,1)S(1)} %get-tuple-element.27, bf16[256,256]{1,0:T(8,128)(2,1)} %param.4), kind=kLoop, calls=%fused_computation | loop fusion | flops 442368 | bytes 294912 | tf_op jit(solution)/shard_map/concatenate | solution.py:134
  8.1 0.7 collective-permute-start.4
  8.8 0.0 collective-permute-done
  8.8 4.0 %collective-permute-done.1 = bf16[256,256]{1,0:T(8,128)(2,1)S(1)} collective-permute-done((bf16[256,256]{1,0:T(8,128)(2,1)}, bf16[256,256]{1,0:T(8,128)(2,1)S(1)}, u32[]{:S(2)}, u32[]{:S(2)}) %collective-permute-start.1) | collective-permute-done | bytes 131104 | tf_op jit(solution)/shard_map/ppermute | solution.py:125
  12.8 0.6 collective-permute-start.9
  13.4 0.5 collective-permute-start.2
  13.9 1.6 %collective-permute-start.3 = (bf16[256,256]{1,0:T(8,128)(2,1)S(1)}, bf16[256,256]{1,0:T(8,128)(2,1)S(1)}, u32[]{:S(2)}, u32[]{:S(2)}) collective-permute-start(bf16[256,256]{1,0:T(8,128)(2,1)S(1)} %collective-permute-done), channel_id=1, source_target_pairs={{0,4},{1,5},{2,6},{3,7},{4,0},{5,1},{6,2},{7,3},{8,12},{9,13},{10,... | collective-permute-start | bytes 393224 | tf_op jit(solution)/shard_map/ppermute | solution.py:125
  15.5 4.3 %collective-permute-done.2 = bf16[256,256]{1,0:T(8,128)(2,1)S(1)} collective-permute-done((bf16[256,256]{1,0:T(8,128)(2,1)S(1)}, bf16[256,256]{1,0:T(8,128)(2,1)S(1)}, u32[]{:S(2)}, u32[]{:S(2)}) %collective-permute-start.2) | collective-permute-done | bytes 131104 | tf_op jit(solution)/shard_map/ppermute | solution.py:125
  19.9 2.8 %collective-permute-done.3 = bf16[256,256]{1,0:T(8,128)(2,1)S(1)} collective-permute-done((bf16[256,256]{1,0:T(8,128)(2,1)S(1)}, bf16[256,256]{1,0:T(8,128)(2,1)S(1)}, u32[]{:S(2)}, u32[]{:S(2)}) %collective-permute-start.3) | collective-permute-done | bytes 131104 | tf_op jit(solution)/shard_map/ppermute | solution.py:125
  22.7 0.0 collective-permute-done.4.refs_7_
  22.7 0.8 %collective-permute-start.5 = (bf16[1024,256]{1,0:T(8,128)(2,1)S(1)}, bf16[1024,256]{1,0:T(8,128)(2,1)S(1)}, u32[]{:S(2)}, u32[]{:S(2)}) collective-permute-start(bf16[1024,256]{1,0:T(8,128)(2,1)S(1)} %constant_dynamic-update-slice_fusion.refs_1_), channel_id=1, source_target_pairs={{0,1},{1,0},{2,3},{3,2},{4,5},{5,4},{6,7},{7,6},{8,9},{9,8},{10,11... | collective-permute-start | bytes 1572872 | tf_op jit(solution)/shard_map/ppermute | solution.py:21
  23.5 1.1 %collective-permute-start.13 = (bf16[256,1024]{1,0:T(8,128)(2,1)}, bf16[256,1024]{1,0:T(8,128)(2,1)S(1)}, u32[]{:S(2)}, u32[]{:S(2)}) collective-permute-start(bf16[256,1024]{1,0:T(8,128)(2,1)} %refs_0_.3), channel_id=1, source_target_pairs={{0,4},{2,10},{4,0},{6,14},{8,16},{10,2},{12,20},{14,6},{16,8},{18,... | collective-permute-start | bytes 1572872 | tf_op jit(solution)/shard_map/ppermute | solution.py:323
  24.5 0.0 collective-permute-done.9.refs_1_
  24.5 1.0 %collective-permute-start.10 = (bf16[256,1024]{1,0:T(8,128)(2,1)S(1)}, bf16[256,1024]{1,0:T(8,128)(2,1)S(1)}, u32[]{:S(2)}, u32[]{:S(2)}) collective-permute-start(bf16[256,1024]{1,0:T(8,128)(2,1)S(1)} %collective-permute-done.9.refs_1_), channel_id=1, source_target_pairs={{0,4},{2,10},{4,0},{6,14},{8,16},{10,2},{12,20},{14,6},{16,8},{18,... | collective-permute-start | bytes 1572872 | tf_op jit(solution)/shard_map/ppermute | solution.py:323
  25.5 1.7 %collective-permute-start.7 = (bf16[1024,256]{1,0:T(8,128)(2,1)S(1)}, bf16[1024,256]{1,0:T(8,128)(2,1)S(1)}, u32[]{:S(2)}, u32[]{:S(2)}) collective-permute-start(bf16[1024,256]{1,0:T(8,128)(2,1)S(1)} %constant_dynamic-update-slice_fusion.refs_1_), channel_id=1, source_target_pairs={{0,2},{2,0},{4,6},{6,4},{8,10},{10,8},{12,14},{14,12},{16,18},{18,... | collective-permute-start | bytes 1572872 | tf_op jit(solution)/shard_map/ppermute | solution.py:21
  27.2 8.4 %collective-permute-done.5.refs_2_ = bf16[1024,256]{1,0:T(8,128)(2,1)S(1)} collective-permute-done((bf16[1024,256]{1,0:T(8,128)(2,1)S(1)}, bf16[1024,256]{1,0:T(8,128)(2,1)S(1)}, u32[]{:S(2)}, u32[]{:S(2)}) %collective-permute-start.5) | collective-permute-done | bytes 524320 | tf_op jit(solution)/shard_map/ppermute | solution.py:21
  35.6 0.0 collective-permute-done.13.refs_2_
  35.6 0.0 collective-permute-start.14
  35.6 2.3 %collective-permute-start.8 = (bf16[1024,256]{1,0:T(8,128)(2,1)S(1)}, bf16[1024,256]{1,0:T(8,128)(2,1)S(1)}, u32[]{:S(2)}, u32[]{:S(2)}) collective-permute-start(bf16[1024,256]{1,0:T(8,128)(2,1)S(1)} %collective-permute-done.5.refs_2_), channel_id=1, source_target_pairs={{0,2},{2,0},{4,6},{6,4},{8,10},{10,8},{12,14},{14,12},{16,18},{18,... | collective-permute-start | bytes 1572872 | tf_op jit(solution)/shard_map/ppermute | solution.py:21
  37.9 0.0 collective-permute-start.6
  37.9 0.6 collective-permute-done.10.refs_3_
  38.5 5.1 %collective-permute-start.11 = (bf16[256,1024]{1,0:T(8,128)(2,1)S(1)}, bf16[256,1024]{1,0:T(8,128)(2,1)S(1)}, u32[]{:S(2)}, u32[]{:S(2)}) collective-permute-start(bf16[256,1024]{1,0:T(8,128)(2,1)S(1)} %collective-permute-done.10.refs_3_), channel_id=1, source_target_pairs={{0,8},{2,6},{4,12},{6,2},{8,0},{10,18},{12,4},{14,22},{16,24},{18,... | collective-permute-start | bytes 1572872 | tf_op jit(solution)/shard_map/ppermute | solution.py:323
  43.5 0.0 collective-permute-done.6.refs_3_
  43.6 0.0 collective-permute-start.19
  43.6 0.0 collective-permute-done.7.refs_4_
  43.6 0.5 collective-permute-start.20
  44.1 1.3 %collective-permute-done.14.refs_0_ = bf16[256,1024]{1,0:T(8,128)(2,1)S(1)} collective-permute-done((bf16[256,1024]{1,0:T(8,128)(2,1)S(1)}, bf16[256,1024]{1,0:T(8,128)(2,1)S(1)}, u32[]{:S(2)}, u32[]{:S(2)}) %collective-permute-start.14) | collective-permute-done | bytes 524320 | tf_op jit(solution)/shard_map/ppermute | solution.py:323
  45.3 0.9 %collective-permute-start.15 = (bf16[256,1024]{1,0:T(8,128)(2,1)S(1)}, bf16[256,1024]{1,0:T(8,128)(2,1)S(1)}, u32[]{:S(2)}, u32[]{:S(2)}) collective-permute-start(bf16[256,1024]{1,0:T(8,128)(2,1)S(1)} %collective-permute-done.14.refs_0_), channel_id=1, source_target_pairs={{0,4},{2,10},{4,0},{6,14},{8,16},{10,2},{12,20},{14,6},{16,8},{18,... | collective-permute-start | bytes 1572872 | tf_op jit(solution)/shard_map/ppermute | solution.py:323
  46.2 0.0 collective-permute-done.8.refs_5_
  46.2 0.0 collective-permute-start.21
  46.2 0.0 copy-start.1
  46.2 0.9 %copy-done.1 = bf16[256,256]{1,0:T(8,128)(2,1)S(1)} copy-done((bf16[256,256]{1,0:T(8,128)(2,1)S(1)}, bf16[256,256]{1,0:T(8,128)(2,1)}, u32[]{:S(2)}) %copy-start.1) | copy-done | bytes 131096
  47.1 6.3 %weights.1 = (bf16[16,512,256]{2,1,0:T(8,128)(2,1)S(1)}, f32[512,128]{1,0:T(8,128)S(1)}) custom-call(bf16[256,256]{1,0:T(8,128)(2,1)S(1)} %copy-done.1, bf16[1024,256]{1,0:T(8,128)(2,1)S(1)} %constant_dynamic-update-slice_fusion.refs_1_, bf16[1024,256]{1,0:T(8,128)(2,1)S(1)} %collective-permute-done.5.refs_2_, ...), custom_call_target="tpu_custom_call" | custom-call | flops 1024 | bytes 1024 | tf_op jit(solution)/shard_map/weights/pallas_call | solution.py:315
  53.5 0.6 collective-permute-done.11.refs_1_
  54.0 0.1 collective-permute-start.22
  54.1 0.0 collective-permute-done.19.refs_4_
  54.1 0.4 collective-permute-start.16
  54.6 0.0 collective-permute-done.20.refs_5_
  54.6 0.1 collective-permute-start.17
  54.6 2.5 %collective-permute-done.15.refs_2_ = bf16[256,1024]{1,0:T(8,128)(2,1)S(1)} collective-permute-done((bf16[256,1024]{1,0:T(8,128)(2,1)S(1)}, bf16[256,1024]{1,0:T(8,128)(2,1)S(1)}, u32[]{:S(2)}, u32[]{:S(2)}) %collective-permute-start.15) | collective-permute-done | bytes 524320 | tf_op jit(solution)/shard_map/ppermute | solution.py:323
  57.1 0.0 collective-permute-start.18
  57.1 0.0 collective-permute-done.21.refs_6_
  57.1 0.5 collective-permute-start.12
  57.6 0.0 collective-permute-done.22.refs_7_
  57.6 0.0 copy-done
  57.6 2.3 %product.3.refs_6_ = f32[512,1024]{1,0:T(8,128)S(1)} custom-call(bf16[16,512,256]{2,1,0:T(8,128)(2,1)S(1)} %get-tuple-element.18.weight, bf16[256,1024]{1,0:T(8,128)(2,1)S(1)} %copy-done, bf16[256,1024]{1,0:T(8,128)(2,1)S(1)} %collective-permute-done.9.refs_1_, bf16[256,1024]{1,0:T(8,128)(2,1)S(1)} %collective-permute-done.13.refs_2_, ...), custom_call_target="tpu_custom_call" | custom-call | flops 1024 | bytes 1024 | tf_op jit(solution)/shard_map/product/pallas_call | solution.py:332
  60.0 0.0 collective-permute-done.16.refs_3_
  60.0 0.0 collective-permute-done.17.refs_4_
  60.0 0.0 collective-permute-done.18.refs_5_
  60.0 1.8 %product.4.refs_3_ = f32[512,1024]{1,0:T(8,128)S(1)} custom-call(bf16[16,512,256]{2,1,0:T(8,128)(2,1)S(1)} %get-tuple-element.18.weight, bf16[256,1024]{1,0:T(8,128)(2,1)S(1)} %collective-permute-done.14.refs_0_, bf16[256,1024]{1,0:T(8,128)(2,1)S(1)} %collective-permute-done.11.refs_1_, bf16[256,1024]{1,0:T(8,128)(2,1)S(1)} %collective-permute-done.15.refs_2_, ...), custom_call_target="tpu_custom_call" | custom-call | flops 1024 | bytes 1024 | tf_op jit(solution)/shard_map/product/pallas_call | solution.py:332
  61.8 4.5 %collective-permute-done.12.refs_0_ = bf16[256,1024]{1,0:T(8,128)(2,1)S(1)} collective-permute-done((bf16[256,1024]{1,0:T(8,128)(2,1)S(1)}, bf16[256,1024]{1,0:T(8,128)(2,1)S(1)}, u32[]{:S(2)}, u32[]{:S(2)}) %collective-permute-start.12) | collective-permute-done | bytes 524320 | tf_op jit(solution)/shard_map/ppermute | solution.py:323
  66.3 0.0 collective-permute-start.23
  66.3 1.9 %collective-permute-done.23.refs_1_ = bf16[256,1024]{1,0:T(8,128)(2,1)S(1)} collective-permute-done((bf16[256,1024]{1,0:T(8,128)(2,1)S(1)}, bf16[256,1024]{1,0:T(8,128)(2,1)S(1)}, u32[]{:S(2)}, u32[]{:S(2)}) %collective-permute-start.23) | collective-permute-done | bytes 524320 | tf_op jit(solution)/shard_map/ppermute | solution.py:21
  68.2 1.7 %product.5 = bf16[512,1024]{1,0:T(8,128)(2,1)} custom-call(bf16[16,512,256]{2,1,0:T(8,128)(2,1)S(1)} %get-tuple-element.18.weight, bf16[256,1024]{1,0:T(8,128)(2,1)S(1)} %collective-permute-done.12.refs_0_, bf16[256,1024]{1,0:T(8,128)(2,1)S(1)} %collective-permute-done.23.refs_1_, f32[512,128]{1,0:T(8,128)S(1)} %get-tuple-element.22.refs_2_, ...), custom_call_target="tpu_custom_call" | custom-call | flops 1024 | bytes 1024 | tf_op jit(solution)/shard_map/product/pallas_call | solution.py:332
  (4 shorter events, 0.0 us)
Async XLA Ops:
  0.0 57.6 %copy-start = (bf16[256,1024]{1,0:T(8,128)(2,1)S(1)}, bf16[256,1024]{1,0:T(8,128)(2,1)}, u32[]{:S(2)}) copy-start(bf16[256,1024]{1,0:T(8,128)(2,1)} %refs_0_.3) | copy-start | bytes 1572868
  0.0 8.8 %collective-permute-start = (bf16[256,256]{1,0:T(8,128)(2,1)}, bf16[256,256]{1,0:T(8,128)(2,1)S(1)}, u32[]{:S(2)}, u32[]{:S(2)}) collective-permute-start(bf16[256,256]{1,0:T(8,128)(2,1)} %refs_0_.2), channel_id=1, source_target_pairs={{0,8},{1,17},{2,10},{3,19},{4,12},{5,21},{6,14},{7,23},{8,0},{9,25... | collective-permute-start | bytes 393224 | tf_op jit(solution)/shard_map/ppermute | solution.py:125
  3.0 9.8 %collective-permute-start.1 = (bf16[256,256]{1,0:T(8,128)(2,1)}, bf16[256,256]{1,0:T(8,128)(2,1)S(1)}, u32[]{:S(2)}, u32[]{:S(2)}) collective-permute-start(bf16[256,256]{1,0:T(8,128)(2,1)} %refs_0_.2), channel_id=1, source_target_pairs={{0,28},{1,5},{2,30},{3,7},{4,24},{5,1},{6,26},{7,3},{8,20},{9,13},... | collective-permute-start | bytes 393224 | tf_op jit(solution)/shard_map/ppermute | solution.py:125
  8.1 14.5 %collective-permute-start.4 = (bf16[288,256]{1,0:T(8,128)(2,1)S(1)}, bf16[288,256]{1,0:T(8,128)(2,1)S(1)}, u32[]{:S(2)}, u32[]{:S(2)}) collective-permute-start(bf16[288,256]{1,0:T(8,128)(2,1)S(1)} %pad_maximum_fusion.refs_6_), channel_id=1, source_target_pairs={{0,1},{1,0},{2,3},{3,2},{4,5},{5,4},{6,7},{7,6},{8,9},{9,8},{10,11... | collective-permute-start | bytes 442376 | tf_op jit(solution)/shard_map/ppermute | solution.py:21
  12.8 11.8 %collective-permute-start.9 = (bf16[256,1024]{1,0:T(8,128)(2,1)}, bf16[256,1024]{1,0:T(8,128)(2,1)S(1)}, u32[]{:S(2)}, u32[]{:S(2)}) collective-permute-start(bf16[256,1024]{1,0:T(8,128)(2,1)} %refs_0_.3), channel_id=1, source_target_pairs={{0,8},{2,6},{4,12},{6,2},{8,0},{10,18},{12,4},{14,22},{16,24},{18,... | collective-permute-start | bytes 1572872 | tf_op jit(solution)/shard_map/ppermute | solution.py:323
  13.4 6.4 %collective-permute-start.2 = (bf16[256,256]{1,0:T(8,128)(2,1)S(1)}, bf16[256,256]{1,0:T(8,128)(2,1)S(1)}, u32[]{:S(2)}, u32[]{:S(2)}) collective-permute-start(bf16[256,256]{1,0:T(8,128)(2,1)S(1)} %collective-permute-done), channel_id=1, source_target_pairs={{0,4},{1,9},{2,6},{3,11},{4,0},{5,13},{6,2},{7,15},{8,12},{9,1},{1... | collective-permute-start | bytes 393224 | tf_op jit(solution)/shard_map/ppermute | solution.py:125
  13.9 8.7 %collective-permute-start.3 = (bf16[256,256]{1,0:T(8,128)(2,1)S(1)}, bf16[256,256]{1,0:T(8,128)(2,1)S(1)}, u32[]{:S(2)}, u32[]{:S(2)}) collective-permute-start(bf16[256,256]{1,0:T(8,128)(2,1)S(1)} %collective-permute-done), channel_id=1, source_target_pairs={{0,4},{1,5},{2,6},{3,7},{4,0},{5,1},{6,2},{7,3},{8,12},{9,13},{10,... | collective-permute-start | bytes 393224 | tf_op jit(solution)/shard_map/ppermute | solution.py:125
  22.7 12.9 %collective-permute-start.5 = (bf16[1024,256]{1,0:T(8,128)(2,1)S(1)}, bf16[1024,256]{1,0:T(8,128)(2,1)S(1)}, u32[]{:S(2)}, u32[]{:S(2)}) collective-permute-start(bf16[1024,256]{1,0:T(8,128)(2,1)S(1)} %constant_dynamic-update-slice_fusion.refs_1_), channel_id=1, source_target_pairs={{0,1},{1,0},{2,3},{3,2},{4,5},{5,4},{6,7},{7,6},{8,9},{9,8},{10,11... | collective-permute-start | bytes 1572872 | tf_op jit(solution)/shard_map/ppermute | solution.py:21
  23.5 12.1 %collective-permute-start.13 = (bf16[256,1024]{1,0:T(8,128)(2,1)}, bf16[256,1024]{1,0:T(8,128)(2,1)S(1)}, u32[]{:S(2)}, u32[]{:S(2)}) collective-permute-start(bf16[256,1024]{1,0:T(8,128)(2,1)} %refs_0_.3), channel_id=1, source_target_pairs={{0,4},{2,10},{4,0},{6,14},{8,16},{10,2},{12,20},{14,6},{16,8},{18,... | collective-permute-start | bytes 1572872 | tf_op jit(solution)/shard_map/ppermute | solution.py:323
  24.5 13.9 %collective-permute-start.10 = (bf16[256,1024]{1,0:T(8,128)(2,1)S(1)}, bf16[256,1024]{1,0:T(8,128)(2,1)S(1)}, u32[]{:S(2)}, u32[]{:S(2)}) collective-permute-start(bf16[256,1024]{1,0:T(8,128)(2,1)S(1)} %collective-permute-done.9.refs_1_), channel_id=1, source_target_pairs={{0,4},{2,10},{4,0},{6,14},{8,16},{10,2},{12,20},{14,6},{16,8},{18,... | collective-permute-start | bytes 1572872 | tf_op jit(solution)/shard_map/ppermute | solution.py:323
  25.5 18.1 %collective-permute-start.7 = (bf16[1024,256]{1,0:T(8,128)(2,1)S(1)}, bf16[1024,256]{1,0:T(8,128)(2,1)S(1)}, u32[]{:S(2)}, u32[]{:S(2)}) collective-permute-start(bf16[1024,256]{1,0:T(8,128)(2,1)S(1)} %constant_dynamic-update-slice_fusion.refs_1_), channel_id=1, source_target_pairs={{0,2},{2,0},{4,6},{6,4},{8,10},{10,8},{12,14},{14,12},{16,18},{18,... | collective-permute-start | bytes 1572872 | tf_op jit(solution)/shard_map/ppermute | solution.py:21
  35.6 9.8 %collective-permute-start.14 = (bf16[256,1024]{1,0:T(8,128)(2,1)S(1)}, bf16[256,1024]{1,0:T(8,128)(2,1)S(1)}, u32[]{:S(2)}, u32[]{:S(2)}) collective-permute-start(bf16[256,1024]{1,0:T(8,128)(2,1)S(1)} %collective-permute-done.13.refs_2_), channel_id=1, source_target_pairs={{0,8},{2,6},{4,12},{6,2},{8,0},{10,18},{12,4},{14,22},{16,24},{18,... | collective-permute-start | bytes 1572872 | tf_op jit(solution)/shard_map/ppermute | solution.py:323
  35.6 10.6 %collective-permute-start.8 = (bf16[1024,256]{1,0:T(8,128)(2,1)S(1)}, bf16[1024,256]{1,0:T(8,128)(2,1)S(1)}, u32[]{:S(2)}, u32[]{:S(2)}) collective-permute-start(bf16[1024,256]{1,0:T(8,128)(2,1)S(1)} %collective-permute-done.5.refs_2_), channel_id=1, source_target_pairs={{0,2},{2,0},{4,6},{6,4},{8,10},{10,8},{12,14},{14,12},{16,18},{18,... | collective-permute-start | bytes 1572872 | tf_op jit(solution)/shard_map/ppermute | solution.py:21
  37.9 5.7 %collective-permute-start.6 = (bf16[256,256]{1,0:T(8,128)(2,1)}, bf16[256,256]{1,0:T(8,128)(2,1)S(1)}, u32[]{:S(2)}, u32[]{:S(2)}) collective-permute-start(bf16[256,256]{1,0:T(8,128)(2,1)} %refs_0_.2), channel_id=1, source_target_pairs={{0,2},{2,0},{4,6},{6,4},{8,10},{10,8},{12,14},{14,12},{16,18},{18,... | collective-permute-start | bytes 393224 | tf_op jit(solution)/shard_map/ppermute | solution.py:21
  38.5 15.6 %collective-permute-start.11 = (bf16[256,1024]{1,0:T(8,128)(2,1)S(1)}, bf16[256,1024]{1,0:T(8,128)(2,1)S(1)}, u32[]{:S(2)}, u32[]{:S(2)}) collective-permute-start(bf16[256,1024]{1,0:T(8,128)(2,1)S(1)} %collective-permute-done.10.refs_3_), channel_id=1, source_target_pairs={{0,8},{2,6},{4,12},{6,2},{8,0},{10,18},{12,4},{14,22},{16,24},{18,... | collective-permute-start | bytes 1572872 | tf_op jit(solution)/shard_map/ppermute | solution.py:323
  43.6 10.6 %collective-permute-start.19 = (bf16[256,1024]{1,0:T(8,128)(2,1)}, bf16[256,1024]{1,0:T(8,128)(2,1)S(1)}, u32[]{:S(2)}, u32[]{:S(2)}) collective-permute-start(bf16[256,1024]{1,0:T(8,128)(2,1)} %refs_0_.3), channel_id=1, source_target_pairs={{0,2},{2,0},{4,6},{6,4},{8,10},{10,8},{12,14},{14,12},{16,18},{18,... | collective-permute-start | bytes 1572872 | tf_op jit(solution)/shard_map/ppermute | solution.py:21
  43.6 11.0 %collective-permute-start.20 = (bf16[256,1024]{1,0:T(8,128)(2,1)S(1)}, bf16[256,1024]{1,0:T(8,128)(2,1)S(1)}, u32[]{:S(2)}, u32[]{:S(2)}) collective-permute-start(bf16[256,1024]{1,0:T(8,128)(2,1)S(1)} %collective-permute-done.9.refs_1_), channel_id=1, source_target_pairs={{0,2},{2,0},{4,6},{6,4},{8,10},{10,8},{12,14},{14,12},{16,18},{18,... | collective-permute-start | bytes 1572872 | tf_op jit(solution)/shard_map/ppermute | solution.py:21
  45.3 11.8 %collective-permute-start.15 = (bf16[256,1024]{1,0:T(8,128)(2,1)S(1)}, bf16[256,1024]{1,0:T(8,128)(2,1)S(1)}, u32[]{:S(2)}, u32[]{:S(2)}) collective-permute-start(bf16[256,1024]{1,0:T(8,128)(2,1)S(1)} %collective-permute-done.14.refs_0_), channel_id=1, source_target_pairs={{0,4},{2,10},{4,0},{6,14},{8,16},{10,2},{12,20},{14,6},{16,8},{18,... | collective-permute-start | bytes 1572872 | tf_op jit(solution)/shard_map/ppermute | solution.py:323
  46.2 10.9 %collective-permute-start.21 = (bf16[256,1024]{1,0:T(8,128)(2,1)S(1)}, bf16[256,1024]{1,0:T(8,128)(2,1)S(1)}, u32[]{:S(2)}, u32[]{:S(2)}) collective-permute-start(bf16[256,1024]{1,0:T(8,128)(2,1)S(1)} %collective-permute-done.13.refs_2_), channel_id=1, source_target_pairs={{0,2},{2,0},{4,6},{6,4},{8,10},{10,8},{12,14},{14,12},{16,18},{18,... | collective-permute-start | bytes 1572872 | tf_op jit(solution)/shard_map/ppermute | solution.py:21
  46.2 0.9 %copy-start.1 = (bf16[256,256]{1,0:T(8,128)(2,1)S(1)}, bf16[256,256]{1,0:T(8,128)(2,1)}, u32[]{:S(2)}) copy-start(bf16[256,256]{1,0:T(8,128)(2,1)} %refs_0_.2) | copy-start | bytes 393220
  54.0 3.6 %collective-permute-start.22 = (bf16[256,1024]{1,0:T(8,128)(2,1)S(1)}, bf16[256,1024]{1,0:T(8,128)(2,1)S(1)}, u32[]{:S(2)}, u32[]{:S(2)}) collective-permute-start(bf16[256,1024]{1,0:T(8,128)(2,1)S(1)} %collective-permute-done.10.refs_3_), channel_id=1, source_target_pairs={{0,2},{2,0},{4,6},{6,4},{8,10},{10,8},{12,14},{14,12},{16,18},{18,... | collective-permute-start | bytes 1572872 | tf_op jit(solution)/shard_map/ppermute | solution.py:21
  54.1 5.8 %collective-permute-start.16 = (bf16[256,1024]{1,0:T(8,128)(2,1)S(1)}, bf16[256,1024]{1,0:T(8,128)(2,1)S(1)}, u32[]{:S(2)}, u32[]{:S(2)}) collective-permute-start(bf16[256,1024]{1,0:T(8,128)(2,1)S(1)} %collective-permute-done.14.refs_0_), channel_id=1, source_target_pairs={{0,2},{2,0},{4,6},{6,4},{8,10},{10,8},{12,14},{14,12},{16,18},{18,... | collective-permute-start | bytes 1572872 | tf_op jit(solution)/shard_map/ppermute | solution.py:21
  54.6 5.4 %collective-permute-start.17 = (bf16[256,1024]{1,0:T(8,128)(2,1)S(1)}, bf16[256,1024]{1,0:T(8,128)(2,1)S(1)}, u32[]{:S(2)}, u32[]{:S(2)}) collective-permute-start(bf16[256,1024]{1,0:T(8,128)(2,1)S(1)} %collective-permute-done.11.refs_1_), channel_id=1, source_target_pairs={{0,2},{2,0},{4,6},{6,4},{8,10},{10,8},{12,14},{14,12},{16,18},{18,... | collective-permute-start | bytes 1572872 | tf_op jit(solution)/shard_map/ppermute | solution.py:21
  57.1 2.9 %collective-permute-start.18 = (bf16[256,1024]{1,0:T(8,128)(2,1)S(1)}, bf16[256,1024]{1,0:T(8,128)(2,1)S(1)}, u32[]{:S(2)}, u32[]{:S(2)}) collective-permute-start(bf16[256,1024]{1,0:T(8,128)(2,1)S(1)} %collective-permute-done.15.refs_2_), channel_id=1, source_target_pairs={{0,2},{2,0},{4,6},{6,4},{8,10},{10,8},{12,14},{14,12},{16,18},{18,... | collective-permute-start | bytes 1572872 | tf_op jit(solution)/shard_map/ppermute | solution.py:21
  57.1 9.2 %collective-permute-start.12 = (bf16[256,1024]{1,0:T(8,128)(2,1)S(1)}, bf16[256,1024]{1,0:T(8,128)(2,1)S(1)}, u32[]{:S(2)}, u32[]{:S(2)}) collective-permute-start(bf16[256,1024]{1,0:T(8,128)(2,1)S(1)} %collective-permute-done.11.refs_1_), channel_id=1, source_target_pairs={{0,4},{2,10},{4,0},{6,14},{8,16},{10,2},{12,20},{14,6},{16,8},{18,... | collective-permute-start | bytes 1572872 | tf_op jit(solution)/shard_map/ppermute | solution.py:323
  66.3 1.9 %collective-permute-start.23 = (bf16[256,1024]{1,0:T(8,128)(2,1)S(1)}, bf16[256,1024]{1,0:T(8,128)(2,1)S(1)}, u32[]{:S(2)}, u32[]{:S(2)}) collective-permute-start(bf16[256,1024]{1,0:T(8,128)(2,1)S(1)} %collective-permute-done.12.refs_0_), channel_id=1, source_target_pairs={{0,2},{2,0},{4,6},{6,4},{8,10},{10,8},{12,14},{14,12},{16,18},{18,... | collective-permute-start | bytes 1572872 | tf_op jit(solution)/shard_map/ppermute | solution.py:21

commit v3 on v2

--- a/solution.py
+++ b/solution.py
@@ -50,19 +50,14 @@
     return held
 
 
-PAIR_STEPS = ((False, 4, 8), (False, 14, 2), (True, 2, 4), (True, 2, 2))
-PAIR_OFFSETS = ((4, 14, 6), (8, 2, 12, 10))
+PAIR_STEPS = ((False, 4, 8), (False, 14, 2), (True, 2, 2), (True, 1, 4))
+PAIR_OFFSETS = ((4, 14, 6), (8, 2, 10, 12))
 
 ORDER = {
-    "F1": ("S1", "S2"),
-    "F2": ("S1", "S2", "S3", "S4"),
-    "F3": ("S3", "S4"),
-    "F4": ("S3", "S4"),
-    "F5": ("Sx",),
-    "F7": ("K",),
+    "F2": ("S3",),
+    "F7": ("K", "F6"),
     "D7": ("P2",),
-    "Sx": ("Ox",),
-    "ScSx": ("Sx",),
+    "Sx": ("Ox", "F1"),
 }
 MERGED = False
 GROUPS = (4, 3, 1)

time: 70.1 us -> 65 us (0.927)
  starting transfers between devices: 24.1 us -> 18.8 us
    ppermute x7, waiting for transfers between devices: 9.43 us -> 18.1 us  [per_device(): lax.ppermute(value, 'row', pairs)]
    ppermute x7, starting transfers between devices: 9.08 us -> 2.98 us  [per_device(): lax.ppermute(value, 'row', pairs)]
    ppermute x4, waiting for transfers between devices: 11.1 us -> 5.83 us  [share_sims(): lax.ppermute(value, ('row', 'col'), pairs)]
    ppermute x13, waiting for transfers between devices: 10.4 us -> 7.12 us  [swap(): return lax.ppermute(value, axis, [(i, i ^ bit) for i in range(size)])]
    ppermute x13, starting transfers between devices: 6.51 us -> 8.81 us  [swap(): return lax.ppermute(value, axis, [(i, i ^ bit) for i in range(size)])]
    ppermute x4, starting transfers between devices: 8.55 us -> 7.03 us  [share_sims(): lax.ppermute(value, ('row', 'col'), pairs)]
  transfers between devices with their start and end apart: 24 -> 24, of which waited for: 10 -> 9; matrix products, arithmetic and copies ran while one was open for 2% -> 3% of each run, Pallas kernels for 15% -> 16%
where the time goes in v3:
time: 65 us; the launch traced here: 64.8 us
  waiting for transfers between devices  31.1 us (48%)
  starting transfers between devices  18.8 us (29%)
  Pallas kernels  12.2 us (19%)
  other arithmetic  1.65 us (3%)
  local copies, waits for them, and re-layouts  0.95 us (1%)
    ppermute x7, waiting for transfers between devices, per_device(): lax.ppermute(value, 'row', pairs)  18.1 us
    ppermute x13, starting transfers between devices, swap(): return lax.ppermute(value, axis, [(i, i ^ bit) for i in range(size)])  8.81 us
    ppermute x13, waiting for transfers between devices, swap(): return lax.ppermute(value, axis, [(i, i ^ bit) for i in range(size)])  7.12 us
    ppermute x4, starting transfers between devices, share_sims(): lax.ppermute(value, ('row', 'col'), pairs)  7.03 us
    pallas_call x1, Pallas kernels, per_device(): weigh(*arrays)  6.34 us
    ppermute x4, waiting for transfers between devices, share_sims(): lax.ppermute(value, ('row', 'col'), pairs)  5.83 us
    pallas_call x3, Pallas kernels, product(): call(functools.partial(product_kernel, columns, before is None, done), 28...  5.82 us
    ppermute x7, starting transfers between devices, per_device(): lax.ppermute(value, 'row', pairs)  2.98 us
  transfers between devices with their start and end apart: 24, of which 9 were waited for; matrix products, arithmetic and copies ran while one was open for 3% of the time, Pallas kernels for 16%

profile of v3, /device:TPU:0, one launch (start us, length us, event | category | flops | bytes accessed | tf_op | source)
XLA Modules:
  0.0 64.8 jit_solution(15877350788657289377)
XLA Ops:
  0.0 0.0 copy-start
  0.0 3.0 %collective-permute-start = (bf16[256,256]{1,0:T(8,128)(2,1)}, bf16[256,256]{1,0:T(8,128)(2,1)S(1)}, u32[]{:S(2)}, u32[]{:S(2)}) collective-permute-start(bf16[256,256]{1,0:T(8,128)(2,1)} %refs_0_.2), channel_id=1, source_target_pairs={{0,8},{1,17},{2,10},{3,19},{4,12},{5,21},{6,14},{7,23},{8,0},{9,25... | collective-permute-start | bytes 393224 | tf_op jit(solution)/shard_map/ppermute | solution.py:120
  3.0 3.4 %collective-permute-start.1 = (bf16[256,256]{1,0:T(8,128)(2,1)}, bf16[256,256]{1,0:T(8,128)(2,1)S(1)}, u32[]{:S(2)}, u32[]{:S(2)}) collective-permute-start(bf16[256,256]{1,0:T(8,128)(2,1)} %refs_0_.2), channel_id=1, source_target_pairs={{0,28},{1,5},{2,30},{3,7},{4,24},{5,1},{6,26},{7,3},{8,20},{9,13},... | collective-permute-start | bytes 393224 | tf_op jit(solution)/shard_map/ppermute | solution.py:120
  6.5 0.7 %collective-permute-start.5 = (bf16[256,1024]{1,0:T(8,128)(2,1)}, bf16[256,1024]{1,0:T(8,128)(2,1)S(1)}, u32[]{:S(2)}, u32[]{:S(2)}) collective-permute-start(bf16[256,1024]{1,0:T(8,128)(2,1)} %refs_0_.3), channel_id=1, source_target_pairs={{0,8},{2,6},{4,12},{6,2},{8,0},{10,18},{12,4},{14,22},{16,24},{18,... | collective-permute-start | bytes 1572872 | tf_op jit(solution)/shard_map/ppermute | solution.py:318
  7.1 0.7 %fusion = (bf16[16,256]{1,0:T(8,128)(2,1)S(1)}, bf16[16,256]{1,0:T(8,128)(2,1)S(1)}) fusion(s32[256,16]{0,1:T(8,128)} %param.6), kind=kLoop, calls=%fused_computation.6 | loop fusion | flops 86016 | bytes 32768 | tf_op jit(solution)/shard_map/convert
  7.9 0.9 %pad_maximum_fusion.refs_6_ = bf16[288,256]{1,0:T(8,128)(2,1)S(1)} fusion(bf16[16,256]{1,0:T(8,128)(2,1)S(1)} %get-tuple-element.18, bf16[16,256]{1,0:T(8,128)(2,1)S(1)} %get-tuple-element.17, bf16[256,256]{1,0:T(8,128)(2,1)} %param.4), kind=kLoop, calls=%fused_computation | loop fusion | flops 442368 | bytes 294912 | tf_op jit(solution)/shard_map/concatenate | solution.py:129
  8.8 1.6 %collective-permute-start.4 = (bf16[288,256]{1,0:T(8,128)(2,1)S(1)}, bf16[288,256]{1,0:T(8,128)(2,1)S(1)}, u32[]{:S(2)}, u32[]{:S(2)}) collective-permute-start(bf16[288,256]{1,0:T(8,128)(2,1)S(1)} %pad_maximum_fusion.refs_6_), channel_id=1, source_target_pairs={{0,1},{1,0},{2,3},{3,2},{4,5},{5,4},{6,7},{7,6},{8,9},{9,8},{10,11... | collective-permute-start | bytes 442376 | tf_op jit(solution)/shard_map/ppermute | solution.py:21
  10.4 0.0 collective-permute-done
  10.4 0.5 collective-permute-start.2
  10.9 0.1 collective-permute-start.3
  11.0 1.9 %collective-permute-done.1 = bf16[256,256]{1,0:T(8,128)(2,1)S(1)} collective-permute-done((bf16[256,256]{1,0:T(8,128)(2,1)}, bf16[256,256]{1,0:T(8,128)(2,1)S(1)}, u32[]{:S(2)}, u32[]{:S(2)}) %collective-permute-start.1) | collective-permute-done | bytes 131104 | tf_op jit(solution)/shard_map/ppermute | solution.py:120
  12.9 3.9 %collective-permute-done.2 = bf16[256,256]{1,0:T(8,128)(2,1)S(1)} collective-permute-done((bf16[256,256]{1,0:T(8,128)(2,1)S(1)}, bf16[256,256]{1,0:T(8,128)(2,1)S(1)}, u32[]{:S(2)}, u32[]{:S(2)}) %collective-permute-start.2) | collective-permute-done | bytes 131104 | tf_op jit(solution)/shard_map/ppermute | solution.py:120
  16.8 0.5 collective-permute-start.12
  17.3 0.0 collective-permute-done.3
  17.3 0.0 collective-permute-done.4.refs_7_
  17.4 0.0 collective-permute-done.5.refs_1_
  17.4 3.4 %collective-permute-start.6 = (bf16[1024,256]{1,0:T(8,128)(2,1)S(1)}, bf16[1024,256]{1,0:T(8,128)(2,1)S(1)}, u32[]{:S(2)}, u32[]{:S(2)}) collective-permute-start(bf16[1024,256]{1,0:T(8,128)(2,1)S(1)} %constant_dynamic-update-slice_fusion.refs_1_), channel_id=1, source_target_pairs={{0,1},{1,0},{2,3},{3,2},{4,5},{5,4},{6,7},{7,6},{8,9},{9,8},{10,11... | collective-permute-start | bytes 1572872 | tf_op jit(solution)/shard_map/ppermute | solution.py:21
  20.8 0.8 %collective-permute-start.10 = (bf16[256,1024]{1,0:T(8,128)(2,1)S(1)}, bf16[256,1024]{1,0:T(8,128)(2,1)S(1)}, u32[]{:S(2)}, u32[]{:S(2)}) collective-permute-start(bf16[256,1024]{1,0:T(8,128)(2,1)S(1)} %collective-permute-done.5.refs_1_), channel_id=1, source_target_pairs={{0,4},{2,10},{4,0},{6,14},{8,16},{10,2},{12,20},{14,6},{16,8},{18,... | collective-permute-start | bytes 1572872 | tf_op jit(solution)/shard_map/ppermute | solution.py:318
  21.6 4.6 %collective-permute-done.12.refs_2_ = bf16[256,1024]{1,0:T(8,128)(2,1)S(1)} collective-permute-done((bf16[256,1024]{1,0:T(8,128)(2,1)}, bf16[256,1024]{1,0:T(8,128)(2,1)S(1)}, u32[]{:S(2)}, u32[]{:S(2)}) %collective-permute-start.12) | collective-permute-done | bytes 524320 | tf_op jit(solution)/shard_map/ppermute | solution.py:318
  26.2 0.0 collective-permute-start.13
  26.2 2.2 %collective-permute-start.8 = (bf16[1024,256]{1,0:T(8,128)(2,1)S(1)}, bf16[1024,256]{1,0:T(8,128)(2,1)S(1)}, u32[]{:S(2)}, u32[]{:S(2)}) collective-permute-start(bf16[1024,256]{1,0:T(8,128)(2,1)S(1)} %constant_dynamic-update-slice_fusion.refs_1_), channel_id=1, source_target_pairs={{0,2},{2,0},{4,6},{6,4},{8,10},{10,8},{12,14},{14,12},{16,18},{18,... | collective-permute-start | bytes 1572872 | tf_op jit(solution)/shard_map/ppermute | solution.py:21
  28.4 5.2 %collective-permute-done.6.refs_2_ = bf16[1024,256]{1,0:T(8,128)(2,1)S(1)} collective-permute-done((bf16[1024,256]{1,0:T(8,128)(2,1)S(1)}, bf16[1024,256]{1,0:T(8,128)(2,1)S(1)}, u32[]{:S(2)}, u32[]{:S(2)}) %collective-permute-start.6) | collective-permute-done | bytes 524320 | tf_op jit(solution)/shard_map/ppermute | solution.py:21
  33.5 0.1 collective-permute-start.9
  33.7 0.4 collective-permute-start.7
  34.1 0.0 collective-permute-done.10.refs_3_
  34.1 0.0 collective-permute-start.11
  34.1 5.2 %collective-permute-done.13.refs_0_ = bf16[256,1024]{1,0:T(8,128)(2,1)S(1)} collective-permute-done((bf16[256,1024]{1,0:T(8,128)(2,1)S(1)}, bf16[256,1024]{1,0:T(8,128)(2,1)S(1)}, u32[]{:S(2)}, u32[]{:S(2)}) %collective-permute-start.13) | collective-permute-done | bytes 524320 | tf_op jit(solution)/shard_map/ppermute | solution.py:318
  39.3 0.5 collective-permute-start.14
  39.8 0.0 collective-permute-done.7.refs_3_
  39.8 0.0 collective-permute-start.19
  39.8 0.0 collective-permute-done.8.refs_4_
  39.8 0.5 collective-permute-start.20
  40.3 0.0 collective-permute-done.9.refs_5_
  40.3 0.1 collective-permute-start.21
  40.4 0.0 copy-start.1
  40.4 0.9 %copy-done.1 = bf16[256,256]{1,0:T(8,128)(2,1)S(1)} copy-done((bf16[256,256]{1,0:T(8,128)(2,1)S(1)}, bf16[256,256]{1,0:T(8,128)(2,1)}, u32[]{:S(2)}) %copy-start.1) | copy-done | bytes 131096
  41.3 6.3 %weights.1 = (bf16[16,512,256]{2,1,0:T(8,128)(2,1)S(1)}, f32[512,128]{1,0:T(8,128)S(1)}) custom-call(bf16[256,256]{1,0:T(8,128)(2,1)S(1)} %copy-done.1, bf16[1024,256]{1,0:T(8,128)(2,1)S(1)} %constant_dynamic-update-slice_fusion.refs_1_, bf16[1024,256]{1,0:T(8,128)(2,1)S(1)} %collective-permute-done.6.refs_2_, ...), custom_call_target="tpu_custom_call" | custom-call | flops 1024 | bytes 1024 | tf_op jit(solution)/shard_map/weights/pallas_call | solution.py:310
  47.6 1.7 %collective-permute-done.11.refs_1_ = bf16[256,1024]{1,0:T(8,128)(2,1)S(1)} collective-permute-done((bf16[256,1024]{1,0:T(8,128)(2,1)S(1)}, bf16[256,1024]{1,0:T(8,128)(2,1)S(1)}, u32[]{:S(2)}, u32[]{:S(2)}) %collective-permute-start.11) | collective-permute-done | bytes 524320 | tf_op jit(solution)/shard_map/ppermute | solution.py:318
  49.3 0.0 collective-permute-start.22
  49.3 2.1 %collective-permute-done.14.refs_2_ = bf16[256,1024]{1,0:T(8,128)(2,1)S(1)} collective-permute-done((bf16[256,1024]{1,0:T(8,128)(2,1)S(1)}, bf16[256,1024]{1,0:T(8,128)(2,1)S(1)}, u32[]{:S(2)}, u32[]{:S(2)}) %collective-permute-start.14) | collective-permute-done | bytes 524320 | tf_op jit(solution)/shard_map/ppermute | solution.py:318
  51.4 0.0 collective-permute-start.16
  51.4 0.0 collective-permute-done.19.refs_4_
  51.4 0.5 collective-permute-start.17
  51.9 0.0 collective-permute-done.20.refs_5_
  51.9 0.1 collective-permute-start.18
  52.0 0.0 collective-permute-done.21.refs_6_
  52.0 0.5 collective-permute-start.15
  52.5 0.0 collective-permute-done.22.refs_7_
  52.5 0.0 copy-done
  52.5 2.3 %product.3.refs_6_ = f32[512,1024]{1,0:T(8,128)S(1)} custom-call(bf16[16,512,256]{2,1,0:T(8,128)(2,1)S(1)} %get-tuple-element.12.weight, bf16[256,1024]{1,0:T(8,128)(2,1)S(1)} %copy-done, bf16[256,1024]{1,0:T(8,128)(2,1)S(1)} %collective-permute-done.5.refs_1_, bf16[256,1024]{1,0:T(8,128)(2,1)S(1)} %collective-permute-done.12.refs_2_, ...), custom_call_target="tpu_custom_call" | custom-call | flops 1024 | bytes 1024 | tf_op jit(solution)/shard_map/product/pallas_call | solution.py:327
  54.8 0.0 collective-permute-done.16.refs_3_
  54.8 0.0 collective-permute-done.17.refs_4_
  54.8 0.0 collective-permute-done.18.refs_5_
  54.9 1.8 %product.4.refs_3_ = f32[512,1024]{1,0:T(8,128)S(1)} custom-call(bf16[16,512,256]{2,1,0:T(8,128)(2,1)S(1)} %get-tuple-element.12.weight, bf16[256,1024]{1,0:T(8,128)(2,1)S(1)} %collective-permute-done.13.refs_0_, bf16[256,1024]{1,0:T(8,128)(2,1)S(1)} %collective-permute-done.11.refs_1_, bf16[256,1024]{1,0:T(8,128)(2,1)S(1)} %collective-permute-done.14.refs_2_, ...), custom_call_target="tpu_custom_call" | custom-call | flops 1024 | bytes 1024 | tf_op jit(solution)/shard_map/product/pallas_call | solution.py:327
  56.7 4.5 %collective-permute-done.15.refs_0_ = bf16[256,1024]{1,0:T(8,128)(2,1)S(1)} collective-permute-done((bf16[256,1024]{1,0:T(8,128)(2,1)S(1)}, bf16[256,1024]{1,0:T(8,128)(2,1)S(1)}, u32[]{:S(2)}, u32[]{:S(2)}) %collective-permute-start.15) | collective-permute-done | bytes 524320 | tf_op jit(solution)/shard_map/ppermute | solution.py:318
  61.2 0.0 collective-permute-start.23
  61.2 1.9 %collective-permute-done.23.refs_1_ = bf16[256,1024]{1,0:T(8,128)(2,1)S(1)} collective-permute-done((bf16[256,1024]{1,0:T(8,128)(2,1)S(1)}, bf16[256,1024]{1,0:T(8,128)(2,1)S(1)}, u32[]{:S(2)}, u32[]{:S(2)}) %collective-permute-start.23) | collective-permute-done | bytes 524320 | tf_op jit(solution)/shard_map/ppermute | solution.py:21
  63.1 1.7 %product.5 = bf16[512,1024]{1,0:T(8,128)(2,1)} custom-call(bf16[16,512,256]{2,1,0:T(8,128)(2,1)S(1)} %get-tuple-element.12.weight, bf16[256,1024]{1,0:T(8,128)(2,1)S(1)} %collective-permute-done.15.refs_0_, bf16[256,1024]{1,0:T(8,128)(2,1)S(1)} %collective-permute-done.23.refs_1_, f32[512,128]{1,0:T(8,128)S(1)} %get-tuple-element.13.refs_2_, ...), custom_call_target="tpu_custom_call" | custom-call | flops 1024 | bytes 1024 | tf_op jit(solution)/shard_map/product/pallas_call | solution.py:327
  (4 shorter events, 0.0 us)
Async XLA Ops:
  0.0 52.5 %copy-start = (bf16[256,1024]{1,0:T(8,128)(2,1)S(1)}, bf16[256,1024]{1,0:T(8,128)(2,1)}, u32[]{:S(2)}) copy-start(bf16[256,1024]{1,0:T(8,128)(2,1)} %refs_0_.3) | copy-start | bytes 1572868
  0.0 10.4 %collective-permute-start = (bf16[256,256]{1,0:T(8,128)(2,1)}, bf16[256,256]{1,0:T(8,128)(2,1)S(1)}, u32[]{:S(2)}, u32[]{:S(2)}) collective-permute-start(bf16[256,256]{1,0:T(8,128)(2,1)} %refs_0_.2), channel_id=1, source_target_pairs={{0,8},{1,17},{2,10},{3,19},{4,12},{5,21},{6,14},{7,23},{8,0},{9,25... | collective-permute-start | bytes 393224 | tf_op jit(solution)/shard_map/ppermute | solution.py:120
  3.0 9.9 %collective-permute-start.1 = (bf16[256,256]{1,0:T(8,128)(2,1)}, bf16[256,256]{1,0:T(8,128)(2,1)S(1)}, u32[]{:S(2)}, u32[]{:S(2)}) collective-permute-start(bf16[256,256]{1,0:T(8,128)(2,1)} %refs_0_.2), channel_id=1, source_target_pairs={{0,28},{1,5},{2,30},{3,7},{4,24},{5,1},{6,26},{7,3},{8,20},{9,13},... | collective-permute-start | bytes 393224 | tf_op jit(solution)/shard_map/ppermute | solution.py:120
  6.5 10.9 %collective-permute-start.5 = (bf16[256,1024]{1,0:T(8,128)(2,1)}, bf16[256,1024]{1,0:T(8,128)(2,1)S(1)}, u32[]{:S(2)}, u32[]{:S(2)}) collective-permute-start(bf16[256,1024]{1,0:T(8,128)(2,1)} %refs_0_.3), channel_id=1, source_target_pairs={{0,8},{2,6},{4,12},{6,2},{8,0},{10,18},{12,4},{14,22},{16,24},{18,... | collective-permute-start | bytes 1572872 | tf_op jit(solution)/shard_map/ppermute | solution.py:318
  8.8 8.6 %collective-permute-start.4 = (bf16[288,256]{1,0:T(8,128)(2,1)S(1)}, bf16[288,256]{1,0:T(8,128)(2,1)S(1)}, u32[]{:S(2)}, u32[]{:S(2)}) collective-permute-start(bf16[288,256]{1,0:T(8,128)(2,1)S(1)} %pad_maximum_fusion.refs_6_), channel_id=1, source_target_pairs={{0,1},{1,0},{2,3},{3,2},{4,5},{5,4},{6,7},{7,6},{8,9},{9,8},{10,11... | collective-permute-start | bytes 442376 | tf_op jit(solution)/shard_map/ppermute | solution.py:21
  10.4 6.4 %collective-permute-start.2 = (bf16[256,256]{1,0:T(8,128)(2,1)S(1)}, bf16[256,256]{1,0:T(8,128)(2,1)S(1)}, u32[]{:S(2)}, u32[]{:S(2)}) collective-permute-start(bf16[256,256]{1,0:T(8,128)(2,1)S(1)} %collective-permute-done), channel_id=1, source_target_pairs={{0,4},{1,5},{2,6},{3,7},{4,0},{5,1},{6,2},{7,3},{8,12},{9,13},{10,... | collective-permute-start | bytes 393224 | tf_op jit(solution)/shard_map/ppermute | solution.py:120
  10.9 6.4 %collective-permute-start.3 = (bf16[256,256]{1,0:T(8,128)(2,1)S(1)}, bf16[256,256]{1,0:T(8,128)(2,1)S(1)}, u32[]{:S(2)}, u32[]{:S(2)}) collective-permute-start(bf16[256,256]{1,0:T(8,128)(2,1)S(1)} %collective-permute-done), channel_id=1, source_target_pairs={{0,2},{1,9},{2,0},{3,11},{4,6},{5,13},{6,4},{7,15},{8,10},{9,1},{1... | collective-permute-start | bytes 393224 | tf_op jit(solution)/shard_map/ppermute | solution.py:120
  16.8 9.4 %collective-permute-start.12 = (bf16[256,1024]{1,0:T(8,128)(2,1)}, bf16[256,1024]{1,0:T(8,128)(2,1)S(1)}, u32[]{:S(2)}, u32[]{:S(2)}) collective-permute-start(bf16[256,1024]{1,0:T(8,128)(2,1)} %refs_0_.3), channel_id=1, source_target_pairs={{0,4},{2,10},{4,0},{6,14},{8,16},{10,2},{12,20},{14,6},{16,8},{18,... | collective-permute-start | bytes 1572872 | tf_op jit(solution)/shard_map/ppermute | solution.py:318
  17.4 16.2 %collective-permute-start.6 = (bf16[1024,256]{1,0:T(8,128)(2,1)S(1)}, bf16[1024,256]{1,0:T(8,128)(2,1)S(1)}, u32[]{:S(2)}, u32[]{:S(2)}) collective-permute-start(bf16[1024,256]{1,0:T(8,128)(2,1)S(1)} %constant_dynamic-update-slice_fusion.refs_1_), channel_id=1, source_target_pairs={{0,1},{1,0},{2,3},{3,2},{4,5},{5,4},{6,7},{7,6},{8,9},{9,8},{10,11... | collective-permute-start | bytes 1572872 | tf_op jit(solution)/shard_map/ppermute | solution.py:21
  20.8 13.3 %collective-permute-start.10 = (bf16[256,1024]{1,0:T(8,128)(2,1)S(1)}, bf16[256,1024]{1,0:T(8,128)(2,1)S(1)}, u32[]{:S(2)}, u32[]{:S(2)}) collective-permute-start(bf16[256,1024]{1,0:T(8,128)(2,1)S(1)} %collective-permute-done.5.refs_1_), channel_id=1, source_target_pairs={{0,4},{2,10},{4,0},{6,14},{8,16},{10,2},{12,20},{14,6},{16,8},{18,... | collective-permute-start | bytes 1572872 | tf_op jit(solution)/shard_map/ppermute | solution.py:318
  26.2 13.1 %collective-permute-start.13 = (bf16[256,1024]{1,0:T(8,128)(2,1)S(1)}, bf16[256,1024]{1,0:T(8,128)(2,1)S(1)}, u32[]{:S(2)}, u32[]{:S(2)}) collective-permute-start(bf16[256,1024]{1,0:T(8,128)(2,1)S(1)} %collective-permute-done.12.refs_2_), channel_id=1, source_target_pairs={{0,8},{2,6},{4,12},{6,2},{8,0},{10,18},{12,4},{14,22},{16,24},{18,... | collective-permute-start | bytes 1572872 | tf_op jit(solution)/shard_map/ppermute | solution.py:318
  26.2 13.6 %collective-permute-start.8 = (bf16[1024,256]{1,0:T(8,128)(2,1)S(1)}, bf16[1024,256]{1,0:T(8,128)(2,1)S(1)}, u32[]{:S(2)}, u32[]{:S(2)}) collective-permute-start(bf16[1024,256]{1,0:T(8,128)(2,1)S(1)} %constant_dynamic-update-slice_fusion.refs_1_), channel_id=1, source_target_pairs={{0,2},{2,0},{4,6},{6,4},{8,10},{10,8},{12,14},{14,12},{16,18},{18,... | collective-permute-start | bytes 1572872 | tf_op jit(solution)/shard_map/ppermute | solution.py:21
  33.5 6.7 %collective-permute-start.9 = (bf16[1024,256]{1,0:T(8,128)(2,1)S(1)}, bf16[1024,256]{1,0:T(8,128)(2,1)S(1)}, u32[]{:S(2)}, u32[]{:S(2)}) collective-permute-start(bf16[1024,256]{1,0:T(8,128)(2,1)S(1)} %collective-permute-done.6.refs_2_), channel_id=1, source_target_pairs={{0,2},{2,0},{4,6},{6,4},{8,10},{10,8},{12,14},{14,12},{16,18},{18,... | collective-permute-start | bytes 1572872 | tf_op jit(solution)/shard_map/ppermute | solution.py:21
  33.7 6.1 %collective-permute-start.7 = (bf16[256,256]{1,0:T(8,128)(2,1)}, bf16[256,256]{1,0:T(8,128)(2,1)S(1)}, u32[]{:S(2)}, u32[]{:S(2)}) collective-permute-start(bf16[256,256]{1,0:T(8,128)(2,1)} %refs_0_.2), channel_id=1, source_target_pairs={{0,2},{2,0},{4,6},{6,4},{8,10},{10,8},{12,14},{14,12},{16,18},{18,... | collective-permute-start | bytes 393224 | tf_op jit(solution)/shard_map/ppermute | solution.py:21
  34.1 15.2 %collective-permute-start.11 = (bf16[256,1024]{1,0:T(8,128)(2,1)S(1)}, bf16[256,1024]{1,0:T(8,128)(2,1)S(1)}, u32[]{:S(2)}, u32[]{:S(2)}) collective-permute-start(bf16[256,1024]{1,0:T(8,128)(2,1)S(1)} %collective-permute-done.10.refs_3_), channel_id=1, source_target_pairs={{0,8},{2,6},{4,12},{6,2},{8,0},{10,18},{12,4},{14,22},{16,24},{18,... | collective-permute-start | bytes 1572872 | tf_op jit(solution)/shard_map/ppermute | solution.py:318
  39.3 12.1 %collective-permute-start.14 = (bf16[256,1024]{1,0:T(8,128)(2,1)S(1)}, bf16[256,1024]{1,0:T(8,128)(2,1)S(1)}, u32[]{:S(2)}, u32[]{:S(2)}) collective-permute-start(bf16[256,1024]{1,0:T(8,128)(2,1)S(1)} %collective-permute-done.13.refs_0_), channel_id=1, source_target_pairs={{0,4},{2,10},{4,0},{6,14},{8,16},{10,2},{12,20},{14,6},{16,8},{18,... | collective-permute-start | bytes 1572872 | tf_op jit(solution)/shard_map/ppermute | solution.py:318
  39.8 11.6 %collective-permute-start.19 = (bf16[256,1024]{1,0:T(8,128)(2,1)}, bf16[256,1024]{1,0:T(8,128)(2,1)S(1)}, u32[]{:S(2)}, u32[]{:S(2)}) collective-permute-start(bf16[256,1024]{1,0:T(8,128)(2,1)} %refs_0_.3), channel_id=1, source_target_pairs={{0,2},{2,0},{4,6},{6,4},{8,10},{10,8},{12,14},{14,12},{16,18},{18,... | collective-permute-start | bytes 1572872 | tf_op jit(solution)/shard_map/ppermute | solution.py:21
  39.8 12.1 %collective-permute-start.20 = (bf16[256,1024]{1,0:T(8,128)(2,1)S(1)}, bf16[256,1024]{1,0:T(8,128)(2,1)S(1)}, u32[]{:S(2)}, u32[]{:S(2)}) collective-permute-start(bf16[256,1024]{1,0:T(8,128)(2,1)S(1)} %collective-permute-done.5.refs_1_), channel_id=1, source_target_pairs={{0,2},{2,0},{4,6},{6,4},{8,10},{10,8},{12,14},{14,12},{16,18},{18,... | collective-permute-start | bytes 1572872 | tf_op jit(solution)/shard_map/ppermute | solution.py:21
  40.3 11.7 %collective-permute-start.21 = (bf16[256,1024]{1,0:T(8,128)(2,1)S(1)}, bf16[256,1024]{1,0:T(8,128)(2,1)S(1)}, u32[]{:S(2)}, u32[]{:S(2)}) collective-permute-start(bf16[256,1024]{1,0:T(8,128)(2,1)S(1)} %collective-permute-done.12.refs_2_), channel_id=1, source_target_pairs={{0,2},{2,0},{4,6},{6,4},{8,10},{10,8},{12,14},{14,12},{16,18},{18,... | collective-permute-start | bytes 1572872 | tf_op jit(solution)/shard_map/ppermute | solution.py:21
  40.4 0.9 %copy-start.1 = (bf16[256,256]{1,0:T(8,128)(2,1)S(1)}, bf16[256,256]{1,0:T(8,128)(2,1)}, u32[]{:S(2)}) copy-start(bf16[256,256]{1,0:T(8,128)(2,1)} %refs_0_.2) | copy-start | bytes 393220
  49.3 3.2 %collective-permute-start.22 = (bf16[256,1024]{1,0:T(8,128)(2,1)S(1)}, bf16[256,1024]{1,0:T(8,128)(2,1)S(1)}, u32[]{:S(2)}, u32[]{:S(2)}) collective-permute-start(bf16[256,1024]{1,0:T(8,128)(2,1)S(1)} %collective-permute-done.10.refs_3_), channel_id=1, source_target_pairs={{0,2},{2,0},{4,6},{6,4},{8,10},{10,8},{12,14},{14,12},{16,18},{18,... | collective-permute-start | bytes 1572872 | tf_op jit(solution)/shard_map/ppermute | solution.py:21
  51.4 3.4 %collective-permute-start.16 = (bf16[256,1024]{1,0:T(8,128)(2,1)S(1)}, bf16[256,1024]{1,0:T(8,128)(2,1)S(1)}, u32[]{:S(2)}, u32[]{:S(2)}) collective-permute-start(bf16[256,1024]{1,0:T(8,128)(2,1)S(1)} %collective-permute-done.13.refs_0_), channel_id=1, source_target_pairs={{0,2},{2,0},{4,6},{6,4},{8,10},{10,8},{12,14},{14,12},{16,18},{18,... | collective-permute-start | bytes 1572872 | tf_op jit(solution)/shard_map/ppermute | solution.py:21
  51.4 3.4 %collective-permute-start.17 = (bf16[256,1024]{1,0:T(8,128)(2,1)S(1)}, bf16[256,1024]{1,0:T(8,128)(2,1)S(1)}, u32[]{:S(2)}, u32[]{:S(2)}) collective-permute-start(bf16[256,1024]{1,0:T(8,128)(2,1)S(1)} %collective-permute-done.11.refs_1_), channel_id=1, source_target_pairs={{0,2},{2,0},{4,6},{6,4},{8,10},{10,8},{12,14},{14,12},{16,18},{18,... | collective-permute-start | bytes 1572872 | tf_op jit(solution)/shard_map/ppermute | solution.py:21
  51.9 2.9 %collective-permute-start.18 = (bf16[256,1024]{1,0:T(8,128)(2,1)S(1)}, bf16[256,1024]{1,0:T(8,128)(2,1)S(1)}, u32[]{:S(2)}, u32[]{:S(2)}) collective-permute-start(bf16[256,1024]{1,0:T(8,128)(2,1)S(1)} %collective-permute-done.14.refs_2_), channel_id=1, source_target_pairs={{0,2},{2,0},{4,6},{6,4},{8,10},{10,8},{12,14},{14,12},{16,18},{18,... | collective-permute-start | bytes 1572872 | tf_op jit(solution)/shard_map/ppermute | solution.py:21
  52.0 9.2 %collective-permute-start.15 = (bf16[256,1024]{1,0:T(8,128)(2,1)S(1)}, bf16[256,1024]{1,0:T(8,128)(2,1)S(1)}, u32[]{:S(2)}, u32[]{:S(2)}) collective-permute-start(bf16[256,1024]{1,0:T(8,128)(2,1)S(1)} %collective-permute-done.11.refs_1_), channel_id=1, source_target_pairs={{0,4},{2,10},{4,0},{6,14},{8,16},{10,2},{12,20},{14,6},{16,8},{18,... | collective-permute-start | bytes 1572872 | tf_op jit(solution)/shard_map/ppermute | solution.py:318
  61.2 1.9 %collective-permute-start.23 = (bf16[256,1024]{1,0:T(8,128)(2,1)S(1)}, bf16[256,1024]{1,0:T(8,128)(2,1)S(1)}, u32[]{:S(2)}, u32[]{:S(2)}) collective-permute-start(bf16[256,1024]{1,0:T(8,128)(2,1)S(1)} %collective-permute-done.15.refs_0_), channel_id=1, source_target_pairs={{0,2},{2,0},{4,6},{6,4},{8,10},{10,8},{12,14},{14,12},{16,18},{18,... | collective-permute-start | bytes 1572872 | tf_op jit(solution)/shard_map/ppermute | solution.py:21

commit v4 on v3

--- a/solution.py
+++ b/solution.py
@@ -54,13 +54,15 @@
 PAIR_OFFSETS = ((4, 14, 6), (8, 2, 10, 12))
 
 ORDER = {
-    "F2": ("S3",),
+    "F2": ("Ox",),
     "F7": ("K", "F6"),
     "D7": ("P2",),
     "Sx": ("Ox", "F1"),
+    "S3": ("S2",),
+    "S4": ("S2",),
 }
 MERGED = False
-GROUPS = (4, 3, 1)
+GROUPS = (4, 3)
 
 
 class Work:
@@ -320,34 +322,34 @@
     for k in range(n_half):
         work.add(f"D{k}", lambda k=k: work.get(f"F{k}"), lambda value: swap(value, "row", n_row, CORE_BIT))
 
-    def product(first, last, parts):
-        done, (weight, total), before, both = last == n_half, *parts
-        columns = [*range(first, last), *range(n_half + first, n_half + last)]
+    def product(columns, done, parts):
+        (weight, total), before, held = parts
         extra = ([total] if done else []) + ([] if before is None else [before])
         return call(
             functools.partial(product_kernel, columns, before is None, done),
             28,
-            in_specs=[VMEM] * (1 + len(both) + len(extra)),
+            in_specs=[VMEM] * (1 + len(held) + len(extra)),
             out_specs=VMEM,
             out_shape=jax.ShapeDtypeStruct((n_obs, cells), bf16 if done else f32),
             cost_estimate=SMALL,
             name="product",
-        )(weight, *both, *extra)
-
-    groups = GROUPS if n_half == sum(GROUPS) else (n_half // 2, n_half - n_half // 2 - 1, 1)
-    first = 0
-    for g, count in enumerate(groups):
-        at = range(first, first + count)
+        )(weight, *held, *extra)
+
+    groups = GROUPS if n_half == sum(GROUPS) + 1 else (n_half // 2, n_half - n_half // 2 - 1)
+    ends = [sum(groups[:g]) for g in range(len(groups) + 1)]
+    groups = [[f"{what}{k}" for what in "FD" for k in range(*at)] for at in zip(ends[:-1], ends[1:])]
+    groups += [[f"F{n_half - 1}"], [f"D{n_half - 1}"]]
+    for g, group in enumerate(groups):
+        columns = [int(name[1:]) + (n_half if name[0] == "D" else 0) for name in group]
         work.add(
             f"P{g + 1}",
-            lambda g=g, at=at: (
+            lambda g=g, group=group: (
                 work.get("K"),
                 work.get(f"P{g}") if g else None,
-                [work.get(f"F{k}") for k in at] + [work.get(f"D{k}") for k in at],
+                [work.get(name) for name in group],
             ),
-            lambda parts, at=at: product(at.start, at.stop, parts),
+            lambda parts, columns=columns, done=g == len(groups) - 1: product(columns, done, parts),
         )
-        first += count
     return work.get(f"P{len(groups)}")
 
 

time: 65 us -> 63.5 us (0.977)
  waiting for transfers between devices: 31.1 us -> 28.2 us
  starting transfers between devices: 18.8 us -> 20 us
    ppermute x7, waiting for transfers between devices: 18.1 us -> 10.4 us  [per_device(): lax.ppermute(value, 'row', pairs)]
    ppermute x13, waiting for transfers between devices: 7.12 us -> 11 us  [swap(): return lax.ppermute(value, axis, [(i, i ^ bit) for i in range(size)])]
    ppermute x7, starting transfers between devices: 2.98 us -> 5.6 us  [per_device(): lax.ppermute(value, 'row', pairs)]
    ppermute x13, starting transfers between devices: 8.81 us -> 7.51 us  [swap(): return lax.ppermute(value, axis, [(i, i ^ bit) for i in range(size)])]
    ppermute x4, waiting for transfers between devices: 5.83 us -> 6.84 us  [share_sims(): lax.ppermute(value, ('row', 'col'), pairs)]
    pallas_call x3 -> x4, Pallas kernels: 5.82 us -> 5.99 us  [product(): call(functools.partial(product_kernel, columns, before is None, done), 28...]
  transfers between devices with their start and end apart: 24 -> 24, of which waited for: 9 -> 9; matrix products, arithmetic and copies ran while one was open for 3% -> 3% of each run, Pallas kernels for 16% -> 17%
where the time goes in v4:
time: 63.5 us; the launch traced here: 63.3 us
  waiting for transfers between devices  28.2 us (44%)
  starting transfers between devices  20 us (31%)
  Pallas kernels  12.3 us (19%)
  other arithmetic  1.65 us (3%)
  local copies, waits for them, and re-layouts  0.95 us (1%)
    ppermute x13, waiting for transfers between devices, swap(): return lax.ppermute(value, axis, [(i, i ^ bit) for i in range(size)])  11 us
    ppermute x7, waiting for transfers between devices, per_device(): lax.ppermute(value, 'row', pairs)  10.4 us
    ppermute x13, starting transfers between devices, swap(): return lax.ppermute(value, axis, [(i, i ^ bit) for i in range(size)])  7.51 us
    ppermute x4, starting transfers between devices, share_sims(): lax.ppermute(value, ('row', 'col'), pairs)  6.91 us
    ppermute x4, waiting for transfers between devices, share_sims(): lax.ppermute(value, ('row', 'col'), pairs)  6.84 us
    pallas_call x1, Pallas kernels, per_device(): weigh(*arrays)  6.33 us
    pallas_call x4, Pallas kernels, product(): call(functools.partial(product_kernel, columns, before is None, done), 28...  5.99 us
    ppermute x7, starting transfers between devices, per_device(): lax.ppermute(value, 'row', pairs)  5.6 us
  transfers between devices with their start and end apart: 24, of which 9 were waited for; matrix products, arithmetic and copies ran while one was open for 3% of the time, Pallas kernels for 17%

profile of v4, /device:TPU:0, one launch (start us, length us, event | category | flops | bytes accessed | tf_op | source)
XLA Modules:
  0.0 63.3 jit_solution(8307474367594842541)
XLA Ops:
  0.0 0.0 copy-start
  0.0 3.0 %collective-permute-start = (bf16[256,256]{1,0:T(8,128)(2,1)}, bf16[256,256]{1,0:T(8,128)(2,1)S(1)}, u32[]{:S(2)}, u32[]{:S(2)}) collective-permute-start(bf16[256,256]{1,0:T(8,128)(2,1)} %refs_0_.2), channel_id=1, source_target_pairs={{0,8},{1,17},{2,10},{3,19},{4,12},{5,21},{6,14},{7,23},{8,0},{9,25... | collective-permute-start | bytes 393224 | tf_op jit(solution)/shard_map/ppermute | solution.py:122
  3.0 3.4 %collective-permute-start.1 = (bf16[256,256]{1,0:T(8,128)(2,1)}, bf16[256,256]{1,0:T(8,128)(2,1)S(1)}, u32[]{:S(2)}, u32[]{:S(2)}) collective-permute-start(bf16[256,256]{1,0:T(8,128)(2,1)} %refs_0_.2), channel_id=1, source_target_pairs={{0,28},{1,5},{2,30},{3,7},{4,24},{5,1},{6,26},{7,3},{8,20},{9,13},... | collective-permute-start | bytes 393224 | tf_op jit(solution)/shard_map/ppermute | solution.py:122
  6.5 0.7 %collective-permute-start.5 = (bf16[256,1024]{1,0:T(8,128)(2,1)}, bf16[256,1024]{1,0:T(8,128)(2,1)S(1)}, u32[]{:S(2)}, u32[]{:S(2)}) collective-permute-start(bf16[256,1024]{1,0:T(8,128)(2,1)} %refs_0_.3), channel_id=1, source_target_pairs={{0,8},{2,6},{4,12},{6,2},{8,0},{10,18},{12,4},{14,22},{16,24},{18,... | collective-permute-start | bytes 1572872 | tf_op jit(solution)/shard_map/ppermute | solution.py:320
  7.1 0.7 %fusion = (bf16[16,256]{1,0:T(8,128)(2,1)S(1)}, bf16[16,256]{1,0:T(8,128)(2,1)S(1)}) fusion(s32[256,16]{0,1:T(8,128)} %param.6), kind=kLoop, calls=%fused_computation.6 | loop fusion | flops 86016 | bytes 32768 | tf_op jit(solution)/shard_map/convert
  7.9 0.9 %pad_maximum_fusion.refs_6_ = bf16[288,256]{1,0:T(8,128)(2,1)S(1)} fusion(bf16[16,256]{1,0:T(8,128)(2,1)S(1)} %get-tuple-element.20, bf16[16,256]{1,0:T(8,128)(2,1)S(1)} %get-tuple-element.19, bf16[256,256]{1,0:T(8,128)(2,1)} %param.4), kind=kLoop, calls=%fused_computation | loop fusion | flops 442368 | bytes 294912 | tf_op jit(solution)/shard_map/concatenate | solution.py:131
  8.8 1.6 %collective-permute-start.4 = (bf16[288,256]{1,0:T(8,128)(2,1)S(1)}, bf16[288,256]{1,0:T(8,128)(2,1)S(1)}, u32[]{:S(2)}, u32[]{:S(2)}) collective-permute-start(bf16[288,256]{1,0:T(8,128)(2,1)S(1)} %pad_maximum_fusion.refs_6_), channel_id=1, source_target_pairs={{0,1},{1,0},{2,3},{3,2},{4,5},{5,4},{6,7},{7,6},{8,9},{9,8},{10,11... | collective-permute-start | bytes 442376 | tf_op jit(solution)/shard_map/ppermute | solution.py:21
  10.4 0.0 collective-permute-done
  10.4 2.5 %collective-permute-done.1 = bf16[256,256]{1,0:T(8,128)(2,1)S(1)} collective-permute-done((bf16[256,256]{1,0:T(8,128)(2,1)}, bf16[256,256]{1,0:T(8,128)(2,1)S(1)}, u32[]{:S(2)}, u32[]{:S(2)}) %collective-permute-start.1) | collective-permute-done | bytes 131104 | tf_op jit(solution)/shard_map/ppermute | solution.py:122
  12.9 0.5 collective-permute-start.2
  13.4 0.0 collective-permute-start.3
  13.4 0.6 collective-permute-done.4.refs_7_
  14.0 1.0 %collective-permute-start.12 = (bf16[256,1024]{1,0:T(8,128)(2,1)}, bf16[256,1024]{1,0:T(8,128)(2,1)S(1)}, u32[]{:S(2)}, u32[]{:S(2)}) collective-permute-start(bf16[256,1024]{1,0:T(8,128)(2,1)} %refs_0_.3), channel_id=1, source_target_pairs={{0,4},{2,10},{4,0},{6,14},{8,16},{10,2},{12,20},{14,6},{16,8},{18,... | collective-permute-start | bytes 1572872 | tf_op jit(solution)/shard_map/ppermute | solution.py:320
  15.0 4.3 %collective-permute-done.2 = bf16[256,256]{1,0:T(8,128)(2,1)S(1)} collective-permute-done((bf16[256,256]{1,0:T(8,128)(2,1)S(1)}, bf16[256,256]{1,0:T(8,128)(2,1)S(1)}, u32[]{:S(2)}, u32[]{:S(2)}) %collective-permute-start.2) | collective-permute-done | bytes 131104 | tf_op jit(solution)/shard_map/ppermute | solution.py:122
  19.3 0.0 collective-permute-done.3
  19.4 0.0 collective-permute-done.5.refs_1_
  19.4 3.8 %collective-permute-start.6 = (bf16[1024,256]{1,0:T(8,128)(2,1)S(1)}, bf16[1024,256]{1,0:T(8,128)(2,1)S(1)}, u32[]{:S(2)}, u32[]{:S(2)}) collective-permute-start(bf16[1024,256]{1,0:T(8,128)(2,1)S(1)} %constant_dynamic-update-slice_fusion.refs_1_), channel_id=1, source_target_pairs={{0,1},{1,0},{2,3},{3,2},{4,5},{5,4},{6,7},{7,6},{8,9},{9,8},{10,11... | collective-permute-start | bytes 1572872 | tf_op jit(solution)/shard_map/ppermute | solution.py:21
  23.2 1.4 %collective-permute-start.10 = (bf16[256,1024]{1,0:T(8,128)(2,1)S(1)}, bf16[256,1024]{1,0:T(8,128)(2,1)S(1)}, u32[]{:S(2)}, u32[]{:S(2)}) collective-permute-start(bf16[256,1024]{1,0:T(8,128)(2,1)S(1)} %collective-permute-done.5.refs_1_), channel_id=1, source_target_pairs={{0,4},{2,10},{4,0},{6,14},{8,16},{10,2},{12,20},{14,6},{16,8},{18,... | collective-permute-start | bytes 1572872 | tf_op jit(solution)/shard_map/ppermute | solution.py:320
  24.6 0.8 %collective-permute-done.12.refs_2_ = bf16[256,1024]{1,0:T(8,128)(2,1)S(1)} collective-permute-done((bf16[256,1024]{1,0:T(8,128)(2,1)}, bf16[256,1024]{1,0:T(8,128)(2,1)S(1)}, u32[]{:S(2)}, u32[]{:S(2)}) %collective-permute-start.12) | collective-permute-done | bytes 524320 | tf_op jit(solution)/shard_map/ppermute | solution.py:320
  25.4 0.0 collective-permute-start.13
  25.4 0.0 collective-permute-start.8
  25.4 8.9 %collective-permute-done.6.refs_2_ = bf16[1024,256]{1,0:T(8,128)(2,1)S(1)} collective-permute-done((bf16[1024,256]{1,0:T(8,128)(2,1)S(1)}, bf16[1024,256]{1,0:T(8,128)(2,1)S(1)}, u32[]{:S(2)}, u32[]{:S(2)}) %collective-permute-start.6) | collective-permute-done | bytes 524320 | tf_op jit(solution)/shard_map/ppermute | solution.py:21
  34.3 0.0 collective-permute-start.9
  34.3 0.5 collective-permute-start.7
  34.8 2.1 %collective-permute-done.10.refs_3_ = bf16[256,1024]{1,0:T(8,128)(2,1)S(1)} collective-permute-done((bf16[256,1024]{1,0:T(8,128)(2,1)S(1)}, bf16[256,1024]{1,0:T(8,128)(2,1)S(1)}, u32[]{:S(2)}, u32[]{:S(2)}) %collective-permute-start.10) | collective-permute-done | bytes 524320 | tf_op jit(solution)/shard_map/ppermute | solution.py:320
  36.9 0.0 collective-permute-start.11
  36.9 0.0 collective-permute-done.13.refs_0_
  36.9 1.4 %collective-permute-start.14 = (bf16[256,1024]{1,0:T(8,128)(2,1)S(1)}, bf16[256,1024]{1,0:T(8,128)(2,1)S(1)}, u32[]{:S(2)}, u32[]{:S(2)}) collective-permute-start(bf16[256,1024]{1,0:T(8,128)(2,1)S(1)} %collective-permute-done.13.refs_0_), channel_id=1, source_target_pairs={{0,4},{2,10},{4,0},{6,14},{8,16},{10,2},{12,20},{14,6},{16,8},{18,... | collective-permute-start | bytes 1572872 | tf_op jit(solution)/shard_map/ppermute | solution.py:320
  38.3 0.0 collective-permute-done.7.refs_3_
  38.4 0.0 collective-permute-start.19
  38.4 0.0 collective-permute-done.8.refs_4_
  38.4 0.5 collective-permute-start.20
  38.9 0.0 collective-permute-done.9.refs_5_
  38.9 0.1 collective-permute-start.21
  38.9 0.0 copy-start.1
  38.9 0.9 %copy-done.1 = bf16[256,256]{1,0:T(8,128)(2,1)S(1)} copy-done((bf16[256,256]{1,0:T(8,128)(2,1)S(1)}, bf16[256,256]{1,0:T(8,128)(2,1)}, u32[]{:S(2)}) %copy-start.1) | copy-done | bytes 131096
  39.8 6.3 %weights.1 = (bf16[16,512,256]{2,1,0:T(8,128)(2,1)S(1)}, f32[512,128]{1,0:T(8,128)S(1)}) custom-call(bf16[256,256]{1,0:T(8,128)(2,1)S(1)} %copy-done.1, bf16[1024,256]{1,0:T(8,128)(2,1)S(1)} %constant_dynamic-update-slice_fusion.refs_1_, bf16[1024,256]{1,0:T(8,128)(2,1)S(1)} %collective-permute-done.6.refs_2_, ...), custom_call_target="tpu_custom_call" | custom-call | flops 1024 | bytes 1024 | tf_op jit(solution)/shard_map/weights/pallas_call | solution.py:312
  46.2 3.5 %collective-permute-done.11.refs_1_ = bf16[256,1024]{1,0:T(8,128)(2,1)S(1)} collective-permute-done((bf16[256,1024]{1,0:T(8,128)(2,1)S(1)}, bf16[256,1024]{1,0:T(8,128)(2,1)S(1)}, u32[]{:S(2)}, u32[]{:S(2)}) %collective-permute-start.11) | collective-permute-done | bytes 524320 | tf_op jit(solution)/shard_map/ppermute | solution.py:320
  49.7 0.0 collective-permute-start.22
  49.7 0.0 collective-permute-done.14.refs_2_
  49.7 0.5 collective-permute-start.16
  50.2 0.0 collective-permute-done.19.refs_4_
  50.2 0.1 collective-permute-start.17
  50.3 0.0 collective-permute-done.20.refs_5_
  50.3 0.4 collective-permute-start.18
  50.8 0.0 collective-permute-done.21.refs_6_
  50.8 1.1 %collective-permute-start.15 = (bf16[256,1024]{1,0:T(8,128)(2,1)S(1)}, bf16[256,1024]{1,0:T(8,128)(2,1)S(1)}, u32[]{:S(2)}, u32[]{:S(2)}) collective-permute-start(bf16[256,1024]{1,0:T(8,128)(2,1)S(1)} %collective-permute-done.11.refs_1_), channel_id=1, source_target_pairs={{0,4},{2,10},{4,0},{6,14},{8,16},{10,2},{12,20},{14,6},{16,8},{18,... | collective-permute-start | bytes 1572872 | tf_op jit(solution)/shard_map/ppermute | solution.py:320
  51.9 0.0 collective-permute-done.22.refs_7_
  51.9 0.0 copy-done
  51.9 2.3 %product.4.refs_6_ = f32[512,1024]{1,0:T(8,128)S(1)} custom-call(bf16[16,512,256]{2,1,0:T(8,128)(2,1)S(1)} %get-tuple-element.14.weight, bf16[256,1024]{1,0:T(8,128)(2,1)S(1)} %copy-done, bf16[256,1024]{1,0:T(8,128)(2,1)S(1)} %collective-permute-done.5.refs_1_, bf16[256,1024]{1,0:T(8,128)(2,1)S(1)} %collective-permute-done.12.refs_2_, ...), custom_call_target="tpu_custom_call" | custom-call | flops 1024 | bytes 1024 | tf_op jit(solution)/shard_map/product/pallas_call | solution.py:328
  54.2 0.0 collective-permute-done.16.refs_3_
  54.2 0.0 collective-permute-done.17.refs_4_
  54.2 0.0 collective-permute-done.18.refs_5_
  54.2 1.8 %product.5.refs_1_ = f32[512,1024]{1,0:T(8,128)S(1)} custom-call(bf16[16,512,256]{2,1,0:T(8,128)(2,1)S(1)} %get-tuple-element.14.weight, bf16[256,1024]{1,0:T(8,128)(2,1)S(1)} %collective-permute-done.13.refs_0_, bf16[256,1024]{1,0:T(8,128)(2,1)S(1)} %collective-permute-done.11.refs_1_, bf16[256,1024]{1,0:T(8,128)(2,1)S(1)} %collective-permute-done.14.refs_2_, ...), custom_call_target="tpu_custom_call" | custom-call | flops 1024 | bytes 1024 | tf_op jit(solution)/shard_map/product/pallas_call | solution.py:328
  56.0 3.9 %collective-permute-done.15.refs_0_ = bf16[256,1024]{1,0:T(8,128)(2,1)S(1)} collective-permute-done((bf16[256,1024]{1,0:T(8,128)(2,1)S(1)}, bf16[256,1024]{1,0:T(8,128)(2,1)S(1)}, u32[]{:S(2)}, u32[]{:S(2)}) %collective-permute-start.15) | collective-permute-done | bytes 524320 | tf_op jit(solution)/shard_map/ppermute | solution.py:320
  59.9 0.0 collective-permute-start.23
  59.9 0.4 product.6.refs_2_
  60.4 1.5 %collective-permute-done.23.refs_0_ = bf16[256,1024]{1,0:T(8,128)(2,1)S(1)} collective-permute-done((bf16[256,1024]{1,0:T(8,128)(2,1)S(1)}, bf16[256,1024]{1,0:T(8,128)(2,1)S(1)}, u32[]{:S(2)}, u32[]{:S(2)}) %collective-permute-start.23) | collective-permute-done | bytes 524320 | tf_op jit(solution)/shard_map/ppermute | solution.py:21
  61.9 1.4 %product.7 = bf16[512,1024]{1,0:T(8,128)(2,1)} custom-call(bf16[16,512,256]{2,1,0:T(8,128)(2,1)S(1)} %get-tuple-element.14.weight, bf16[256,1024]{1,0:T(8,128)(2,1)S(1)} %collective-permute-done.23.refs_0_, f32[512,128]{1,0:T(8,128)S(1)} %get-tuple-element.15.refs_1_, f32[512,1024]{1,0:T(8,128)S(1)} %product.6.refs_2_), custom_call_target="tpu_custom_call" | custom-call | flops 1024 | bytes 1024 | tf_op jit(solution)/shard_map/product/pallas_call | solution.py:328
  (4 shorter events, 0.0 us)
Async XLA Ops:
  0.0 51.9 %copy-start = (bf16[256,1024]{1,0:T(8,128)(2,1)S(1)}, bf16[256,1024]{1,0:T(8,128)(2,1)}, u32[]{:S(2)}) copy-start(bf16[256,1024]{1,0:T(8,128)(2,1)} %refs_0_.3) | copy-start | bytes 1572868
  0.0 10.4 %collective-permute-start = (bf16[256,256]{1,0:T(8,128)(2,1)}, bf16[256,256]{1,0:T(8,128)(2,1)S(1)}, u32[]{:S(2)}, u32[]{:S(2)}) collective-permute-start(bf16[256,256]{1,0:T(8,128)(2,1)} %refs_0_.2), channel_id=1, source_target_pairs={{0,8},{1,17},{2,10},{3,19},{4,12},{5,21},{6,14},{7,23},{8,0},{9,25... | collective-permute-start | bytes 393224 | tf_op jit(solution)/shard_map/ppermute | solution.py:122
  3.0 9.9 %collective-permute-start.1 = (bf16[256,256]{1,0:T(8,128)(2,1)}, bf16[256,256]{1,0:T(8,128)(2,1)S(1)}, u32[]{:S(2)}, u32[]{:S(2)}) collective-permute-start(bf16[256,256]{1,0:T(8,128)(2,1)} %refs_0_.2), channel_id=1, source_target_pairs={{0,28},{1,5},{2,30},{3,7},{4,24},{5,1},{6,26},{7,3},{8,20},{9,13},... | collective-permute-start | bytes 393224 | tf_op jit(solution)/shard_map/ppermute | solution.py:122
  6.5 12.9 %collective-permute-start.5 = (bf16[256,1024]{1,0:T(8,128)(2,1)}, bf16[256,1024]{1,0:T(8,128)(2,1)S(1)}, u32[]{:S(2)}, u32[]{:S(2)}) collective-permute-start(bf16[256,1024]{1,0:T(8,128)(2,1)} %refs_0_.3), channel_id=1, source_target_pairs={{0,8},{2,6},{4,12},{6,2},{8,0},{10,18},{12,4},{14,22},{16,24},{18,... | collective-permute-start | bytes 1572872 | tf_op jit(solution)/shard_map/ppermute | solution.py:320
  8.8 5.2 %collective-permute-start.4 = (bf16[288,256]{1,0:T(8,128)(2,1)S(1)}, bf16[288,256]{1,0:T(8,128)(2,1)S(1)}, u32[]{:S(2)}, u32[]{:S(2)}) collective-permute-start(bf16[288,256]{1,0:T(8,128)(2,1)S(1)} %pad_maximum_fusion.refs_6_), channel_id=1, source_target_pairs={{0,1},{1,0},{2,3},{3,2},{4,5},{5,4},{6,7},{7,6},{8,9},{9,8},{10,11... | collective-permute-start | bytes 442376 | tf_op jit(solution)/shard_map/ppermute | solution.py:21
  12.9 6.4 %collective-permute-start.2 = (bf16[256,256]{1,0:T(8,128)(2,1)S(1)}, bf16[256,256]{1,0:T(8,128)(2,1)S(1)}, u32[]{:S(2)}, u32[]{:S(2)}) collective-permute-start(bf16[256,256]{1,0:T(8,128)(2,1)S(1)} %collective-permute-done), channel_id=1, source_target_pairs={{0,4},{1,5},{2,6},{3,7},{4,0},{5,1},{6,2},{7,3},{8,12},{9,13},{10,... | collective-permute-start | bytes 393224 | tf_op jit(solution)/shard_map/ppermute | solution.py:122
  13.4 6.0 %collective-permute-start.3 = (bf16[256,256]{1,0:T(8,128)(2,1)S(1)}, bf16[256,256]{1,0:T(8,128)(2,1)S(1)}, u32[]{:S(2)}, u32[]{:S(2)}) collective-permute-start(bf16[256,256]{1,0:T(8,128)(2,1)S(1)} %collective-permute-done), channel_id=1, source_target_pairs={{0,2},{1,9},{2,0},{3,11},{4,6},{5,13},{6,4},{7,15},{8,10},{9,1},{1... | collective-permute-start | bytes 393224 | tf_op jit(solution)/shard_map/ppermute | solution.py:122
  14.0 11.4 %collective-permute-start.12 = (bf16[256,1024]{1,0:T(8,128)(2,1)}, bf16[256,1024]{1,0:T(8,128)(2,1)S(1)}, u32[]{:S(2)}, u32[]{:S(2)}) collective-permute-start(bf16[256,1024]{1,0:T(8,128)(2,1)} %refs_0_.3), channel_id=1, source_target_pairs={{0,4},{2,10},{4,0},{6,14},{8,16},{10,2},{12,20},{14,6},{16,8},{18,... | collective-permute-start | bytes 1572872 | tf_op jit(solution)/shard_map/ppermute | solution.py:320
  19.4 14.9 %collective-permute-start.6 = (bf16[1024,256]{1,0:T(8,128)(2,1)S(1)}, bf16[1024,256]{1,0:T(8,128)(2,1)S(1)}, u32[]{:S(2)}, u32[]{:S(2)}) collective-permute-start(bf16[1024,256]{1,0:T(8,128)(2,1)S(1)} %constant_dynamic-update-slice_fusion.refs_1_), channel_id=1, source_target_pairs={{0,1},{1,0},{2,3},{3,2},{4,5},{5,4},{6,7},{7,6},{8,9},{9,8},{10,11... | collective-permute-start | bytes 1572872 | tf_op jit(solution)/shard_map/ppermute | solution.py:21
  23.2 13.7 %collective-permute-start.10 = (bf16[256,1024]{1,0:T(8,128)(2,1)S(1)}, bf16[256,1024]{1,0:T(8,128)(2,1)S(1)}, u32[]{:S(2)}, u32[]{:S(2)}) collective-permute-start(bf16[256,1024]{1,0:T(8,128)(2,1)S(1)} %collective-permute-done.5.refs_1_), channel_id=1, source_target_pairs={{0,4},{2,10},{4,0},{6,14},{8,16},{10,2},{12,20},{14,6},{16,8},{18,... | collective-permute-start | bytes 1572872 | tf_op jit(solution)/shard_map/ppermute | solution.py:320
  25.4 11.5 %collective-permute-start.13 = (bf16[256,1024]{1,0:T(8,128)(2,1)S(1)}, bf16[256,1024]{1,0:T(8,128)(2,1)S(1)}, u32[]{:S(2)}, u32[]{:S(2)}) collective-permute-start(bf16[256,1024]{1,0:T(8,128)(2,1)S(1)} %collective-permute-done.12.refs_2_), channel_id=1, source_target_pairs={{0,8},{2,6},{4,12},{6,2},{8,0},{10,18},{12,4},{14,22},{16,24},{18,... | collective-permute-start | bytes 1572872 | tf_op jit(solution)/shard_map/ppermute | solution.py:320
  25.4 13.0 %collective-permute-start.8 = (bf16[1024,256]{1,0:T(8,128)(2,1)S(1)}, bf16[1024,256]{1,0:T(8,128)(2,1)S(1)}, u32[]{:S(2)}, u32[]{:S(2)}) collective-permute-start(bf16[1024,256]{1,0:T(8,128)(2,1)S(1)} %constant_dynamic-update-slice_fusion.refs_1_), channel_id=1, source_target_pairs={{0,2},{2,0},{4,6},{6,4},{8,10},{10,8},{12,14},{14,12},{16,18},{18,... | collective-permute-start | bytes 1572872 | tf_op jit(solution)/shard_map/ppermute | solution.py:21
  34.3 4.6 %collective-permute-start.9 = (bf16[1024,256]{1,0:T(8,128)(2,1)S(1)}, bf16[1024,256]{1,0:T(8,128)(2,1)S(1)}, u32[]{:S(2)}, u32[]{:S(2)}) collective-permute-start(bf16[1024,256]{1,0:T(8,128)(2,1)S(1)} %collective-permute-done.6.refs_2_), channel_id=1, source_target_pairs={{0,2},{2,0},{4,6},{6,4},{8,10},{10,8},{12,14},{14,12},{16,18},{18,... | collective-permute-start | bytes 1572872 | tf_op jit(solution)/shard_map/ppermute | solution.py:21
  34.3 4.1 %collective-permute-start.7 = (bf16[256,256]{1,0:T(8,128)(2,1)}, bf16[256,256]{1,0:T(8,128)(2,1)S(1)}, u32[]{:S(2)}, u32[]{:S(2)}) collective-permute-start(bf16[256,256]{1,0:T(8,128)(2,1)} %refs_0_.2), channel_id=1, source_target_pairs={{0,2},{2,0},{4,6},{6,4},{8,10},{10,8},{12,14},{14,12},{16,18},{18,... | collective-permute-start | bytes 393224 | tf_op jit(solution)/shard_map/ppermute | solution.py:21
  36.9 12.8 %collective-permute-start.11 = (bf16[256,1024]{1,0:T(8,128)(2,1)S(1)}, bf16[256,1024]{1,0:T(8,128)(2,1)S(1)}, u32[]{:S(2)}, u32[]{:S(2)}) collective-permute-start(bf16[256,1024]{1,0:T(8,128)(2,1)S(1)} %collective-permute-done.10.refs_3_), channel_id=1, source_target_pairs={{0,8},{2,6},{4,12},{6,2},{8,0},{10,18},{12,4},{14,22},{16,24},{18,... | collective-permute-start | bytes 1572872 | tf_op jit(solution)/shard_map/ppermute | solution.py:320
  36.9 12.8 %collective-permute-start.14 = (bf16[256,1024]{1,0:T(8,128)(2,1)S(1)}, bf16[256,1024]{1,0:T(8,128)(2,1)S(1)}, u32[]{:S(2)}, u32[]{:S(2)}) collective-permute-start(bf16[256,1024]{1,0:T(8,128)(2,1)S(1)} %collective-permute-done.13.refs_0_), channel_id=1, source_target_pairs={{0,4},{2,10},{4,0},{6,14},{8,16},{10,2},{12,20},{14,6},{16,8},{18,... | collective-permute-start | bytes 1572872 | tf_op jit(solution)/shard_map/ppermute | solution.py:320
  38.4 11.9 %collective-permute-start.19 = (bf16[256,1024]{1,0:T(8,128)(2,1)}, bf16[256,1024]{1,0:T(8,128)(2,1)S(1)}, u32[]{:S(2)}, u32[]{:S(2)}) collective-permute-start(bf16[256,1024]{1,0:T(8,128)(2,1)} %refs_0_.3), channel_id=1, source_target_pairs={{0,2},{2,0},{4,6},{6,4},{8,10},{10,8},{12,14},{14,12},{16,18},{18,... | collective-permute-start | bytes 1572872 | tf_op jit(solution)/shard_map/ppermute | solution.py:21
  38.4 12.0 %collective-permute-start.20 = (bf16[256,1024]{1,0:T(8,128)(2,1)S(1)}, bf16[256,1024]{1,0:T(8,128)(2,1)S(1)}, u32[]{:S(2)}, u32[]{:S(2)}) collective-permute-start(bf16[256,1024]{1,0:T(8,128)(2,1)S(1)} %collective-permute-done.5.refs_1_), channel_id=1, source_target_pairs={{0,2},{2,0},{4,6},{6,4},{8,10},{10,8},{12,14},{14,12},{16,18},{18,... | collective-permute-start | bytes 1572872 | tf_op jit(solution)/shard_map/ppermute | solution.py:21
  38.9 11.9 %collective-permute-start.21 = (bf16[256,1024]{1,0:T(8,128)(2,1)S(1)}, bf16[256,1024]{1,0:T(8,128)(2,1)S(1)}, u32[]{:S(2)}, u32[]{:S(2)}) collective-permute-start(bf16[256,1024]{1,0:T(8,128)(2,1)S(1)} %collective-permute-done.12.refs_2_), channel_id=1, source_target_pairs={{0,2},{2,0},{4,6},{6,4},{8,10},{10,8},{12,14},{14,12},{16,18},{18,... | collective-permute-start | bytes 1572872 | tf_op jit(solution)/shard_map/ppermute | solution.py:21
  38.9 0.9 %copy-start.1 = (bf16[256,256]{1,0:T(8,128)(2,1)S(1)}, bf16[256,256]{1,0:T(8,128)(2,1)}, u32[]{:S(2)}) copy-start(bf16[256,256]{1,0:T(8,128)(2,1)} %refs_0_.2) | copy-start | bytes 393220
  49.7 2.1 %collective-permute-start.22 = (bf16[256,1024]{1,0:T(8,128)(2,1)S(1)}, bf16[256,1024]{1,0:T(8,128)(2,1)S(1)}, u32[]{:S(2)}, u32[]{:S(2)}) collective-permute-start(bf16[256,1024]{1,0:T(8,128)(2,1)S(1)} %collective-permute-done.10.refs_3_), channel_id=1, source_target_pairs={{0,2},{2,0},{4,6},{6,4},{8,10},{10,8},{12,14},{14,12},{16,18},{18,... | collective-permute-start | bytes 1572872 | tf_op jit(solution)/shard_map/ppermute | solution.py:21
  49.7 4.5 %collective-permute-start.16 = (bf16[256,1024]{1,0:T(8,128)(2,1)S(1)}, bf16[256,1024]{1,0:T(8,128)(2,1)S(1)}, u32[]{:S(2)}, u32[]{:S(2)}) collective-permute-start(bf16[256,1024]{1,0:T(8,128)(2,1)S(1)} %collective-permute-done.13.refs_0_), channel_id=1, source_target_pairs={{0,2},{2,0},{4,6},{6,4},{8,10},{10,8},{12,14},{14,12},{16,18},{18,... | collective-permute-start | bytes 1572872 | tf_op jit(solution)/shard_map/ppermute | solution.py:21
  50.2 4.0 %collective-permute-start.17 = (bf16[256,1024]{1,0:T(8,128)(2,1)S(1)}, bf16[256,1024]{1,0:T(8,128)(2,1)S(1)}, u32[]{:S(2)}, u32[]{:S(2)}) collective-permute-start(bf16[256,1024]{1,0:T(8,128)(2,1)S(1)} %collective-permute-done.11.refs_1_), channel_id=1, source_target_pairs={{0,2},{2,0},{4,6},{6,4},{8,10},{10,8},{12,14},{14,12},{16,18},{18,... | collective-permute-start | bytes 1572872 | tf_op jit(solution)/shard_map/ppermute | solution.py:21
  50.3 3.9 %collective-permute-start.18 = (bf16[256,1024]{1,0:T(8,128)(2,1)S(1)}, bf16[256,1024]{1,0:T(8,128)(2,1)S(1)}, u32[]{:S(2)}, u32[]{:S(2)}) collective-permute-start(bf16[256,1024]{1,0:T(8,128)(2,1)S(1)} %collective-permute-done.14.refs_2_), channel_id=1, source_target_pairs={{0,2},{2,0},{4,6},{6,4},{8,10},{10,8},{12,14},{14,12},{16,18},{18,... | collective-permute-start | bytes 1572872 | tf_op jit(solution)/shard_map/ppermute | solution.py:21
  50.8 9.2 %collective-permute-start.15 = (bf16[256,1024]{1,0:T(8,128)(2,1)S(1)}, bf16[256,1024]{1,0:T(8,128)(2,1)S(1)}, u32[]{:S(2)}, u32[]{:S(2)}) collective-permute-start(bf16[256,1024]{1,0:T(8,128)(2,1)S(1)} %collective-permute-done.11.refs_1_), channel_id=1, source_target_pairs={{0,4},{2,10},{4,0},{6,14},{8,16},{10,2},{12,20},{14,6},{16,8},{18,... | collective-permute-start | bytes 1572872 | tf_op jit(solution)/shard_map/ppermute | solution.py:320
  59.9 1.9 %collective-permute-start.23 = (bf16[256,1024]{1,0:T(8,128)(2,1)S(1)}, bf16[256,1024]{1,0:T(8,128)(2,1)S(1)}, u32[]{:S(2)}, u32[]{:S(2)}) collective-permute-start(bf16[256,1024]{1,0:T(8,128)(2,1)S(1)} %collective-permute-done.15.refs_0_), channel_id=1, source_target_pairs={{0,2},{2,0},{4,6},{6,4},{8,10},{10,8},{12,14},{14,12},{16,18},{18,... | collective-permute-start | bytes 1572872 | tf_op jit(solution)/shard_map/ppermute | solution.py:21

commit v5 on v4

--- a/solution.py
+++ b/solution.py
@@ -50,16 +50,15 @@
     return held
 
 
-PAIR_STEPS = ((False, 4, 8), (False, 14, 2), (True, 2, 2), (True, 1, 4))
-PAIR_OFFSETS = ((4, 14, 6), (8, 2, 10, 12))
+PAIR_STEPS = ((False, 4, 8), (False, 1, 2), (True, 2, 2), (True, 10, 4))
+PAIR_OFFSETS = ((4, None, 6, 14), (8, 2, 10, 12))
+SPARE = 1
 
 ORDER = {
     "F2": ("Ox",),
     "F7": ("K", "F6"),
     "D7": ("P2",),
     "Sx": ("Ox", "F1"),
-    "S3": ("S2",),
-    "S4": ("S2",),
 }
 MERGED = False
 GROUPS = (4, 3)
@@ -134,15 +133,16 @@
         obs_at = [(6, 0), (7, 0)]
     add_swap("Sx", "mine", "col", n_col, 1)
     blocks = [((0, 0), (0, 0))]
-    for k in range(3):
+    kept = [k for k in range(4) if k != SPARE]
+    for k in kept:
         blocks += [((1, k * depth),) * 2, ((2, k * depth),) * 2]
-    blocks += [((2, 3 * depth), (1, 3 * depth))]
+    blocks += [((2, SPARE * depth), (1, SPARE * depth))]
     blocks += [tuple((s + len(names), k) for s, k in block) for block in blocks]
     table = []
     for r in range(n_row):
         for c in range(2):
             here, there = PAIR_OFFSETS[c], PAIR_OFFSETS[1 - c]
-            offs = [0] + [o for k in range(3) for o in (here[k], there[k])] + [PAIR_OFFSETS[1][3]]
+            offs = [0] + [o for k in kept for o in (here[k], there[k])] + [PAIR_OFFSETS[1][SPARE]]
             table.append([r ^ o for o in offs] + [r ^ CORE_BIT ^ o for o in offs])
             assert sorted(table[-1]) == list(range(n_row))
     for name in tuple(names):

time: 63.5 us -> 62.2 us (0.980)
  waiting for transfers between devices: 28.2 us -> 24 us
  starting transfers between devices: 20 us -> 22.9 us
    ppermute x13, starting transfers between devices: 7.51 us -> 12.1 us  [swap(): return lax.ppermute(value, axis, [(i, i ^ bit) for i in range(size)])]
    ppermute x13, waiting for transfers between devices: 11 us -> 8.39 us  [swap(): return lax.ppermute(value, axis, [(i, i ^ bit) for i in range(size)])]
    ppermute x4, waiting for transfers between devices: 6.84 us -> 4.67 us  [share_sims(): lax.ppermute(value, ('row', 'col'), pairs)]
    ppermute x4, starting transfers between devices: 6.91 us -> 4.89 us  [share_sims(): lax.ppermute(value, ('row', 'col'), pairs)]
  transfers between devices with their start and end apart: 24 -> 24, of which waited for: 9 -> 8; matrix products, arithmetic and copies ran while one was open for 3% -> 3% of each run, Pallas kernels for 17% -> 18%
where the time goes in v5:
time: 62.2 us; the launch traced here: 61.9 us
  waiting for transfers between devices  24 us (39%)
  starting transfers between devices  22.9 us (37%)
  Pallas kernels  12.3 us (20%)
  other arithmetic  1.65 us (3%)
  local copies, waits for them, and re-layouts  0.95 us (2%)
    ppermute x13, starting transfers between devices, swap(): return lax.ppermute(value, axis, [(i, i ^ bit) for i in range(size)])  12.1 us
    ppermute x7, waiting for transfers between devices, per_device(): lax.ppermute(value, 'row', pairs)  11 us
    ppermute x13, waiting for transfers between devices, swap(): return lax.ppermute(value, axis, [(i, i ^ bit) for i in range(size)])  8.39 us
    pallas_call x1, Pallas kernels, per_device(): weigh(*arrays)  6.33 us
    pallas_call x4, Pallas kernels, product(): call(functools.partial(product_kernel, columns, before is None, done), 28...  5.99 us
    ppermute x7, starting transfers between devices, per_device(): lax.ppermute(value, 'row', pairs)  5.89 us
    ppermute x4, starting transfers between devices, share_sims(): lax.ppermute(value, ('row', 'col'), pairs)  4.89 us
    ppermute x4, waiting for transfers between devices, share_sims(): lax.ppermute(value, ('row', 'col'), pairs)  4.67 us
  transfers between devices with their start and end apart: 24, of which 8 were waited for; matrix products, arithmetic and copies ran while one was open for 3% of the time, Pallas kernels for 18%

profile of v5, /device:TPU:0, one launch (start us, length us, event | category | flops | bytes accessed | tf_op | source)
XLA Modules:
  0.0 61.9 jit_solution(16624269153532232653)
XLA Ops:
  0.0 0.0 copy-start
  0.0 3.0 %collective-permute-start = (bf16[256,256]{1,0:T(8,128)(2,1)}, bf16[256,256]{1,0:T(8,128)(2,1)S(1)}, u32[]{:S(2)}, u32[]{:S(2)}) collective-permute-start(bf16[256,256]{1,0:T(8,128)(2,1)} %refs_0_.2), channel_id=1, source_target_pairs={{0,8},{1,17},{2,10},{3,19},{4,12},{5,21},{6,14},{7,23},{8,0},{9,25... | collective-permute-start | bytes 393224 | tf_op jit(solution)/shard_map/ppermute | solution.py:121
  3.0 0.0 collective-permute-start.1
  3.0 0.1 collective-permute-start.5
  3.2 0.7 %fusion = (bf16[16,256]{1,0:T(8,128)(2,1)S(1)}, bf16[16,256]{1,0:T(8,128)(2,1)S(1)}) fusion(s32[256,16]{0,1:T(8,128)} %param.6), kind=kLoop, calls=%fused_computation.6 | loop fusion | flops 86016 | bytes 32768 | tf_op jit(solution)/shard_map/convert
  3.9 0.9 %pad_maximum_fusion.refs_6_ = bf16[288,256]{1,0:T(8,128)(2,1)S(1)} fusion(bf16[16,256]{1,0:T(8,128)(2,1)S(1)} %get-tuple-element.18, bf16[16,256]{1,0:T(8,128)(2,1)S(1)} %get-tuple-element.17, bf16[256,256]{1,0:T(8,128)(2,1)} %param.4), kind=kLoop, calls=%fused_computation | loop fusion | flops 442368 | bytes 294912 | tf_op jit(solution)/shard_map/concatenate | solution.py:130
  4.8 5.5 %collective-permute-start.4 = (bf16[288,256]{1,0:T(8,128)(2,1)S(1)}, bf16[288,256]{1,0:T(8,128)(2,1)S(1)}, u32[]{:S(2)}, u32[]{:S(2)}) collective-permute-start(bf16[288,256]{1,0:T(8,128)(2,1)S(1)} %pad_maximum_fusion.refs_6_), channel_id=1, source_target_pairs={{0,1},{1,0},{2,3},{3,2},{4,5},{5,4},{6,7},{7,6},{8,9},{9,8},{10,11... | collective-permute-start | bytes 442376 | tf_op jit(solution)/shard_map/ppermute | solution.py:21
  10.4 0.0 collective-permute-done
  10.4 0.5 collective-permute-start.2
  10.9 1.4 %collective-permute-start.3 = (bf16[256,256]{1,0:T(8,128)(2,1)S(1)}, bf16[256,256]{1,0:T(8,128)(2,1)S(1)}, u32[]{:S(2)}, u32[]{:S(2)}) collective-permute-start(bf16[256,256]{1,0:T(8,128)(2,1)S(1)} %collective-permute-done), channel_id=1, source_target_pairs={{0,20},{1,9},{2,22},{3,11},{4,16},{5,13},{6,18},{7,15},{8,28},{9,1... | collective-permute-start | bytes 393224 | tf_op jit(solution)/shard_map/ppermute | solution.py:121
  12.2 0.0 collective-permute-done.1
  12.2 1.2 %collective-permute-done.4.refs_7_ = bf16[288,256]{1,0:T(8,128)(2,1)S(1)} collective-permute-done((bf16[288,256]{1,0:T(8,128)(2,1)S(1)}, bf16[288,256]{1,0:T(8,128)(2,1)S(1)}, u32[]{:S(2)}, u32[]{:S(2)}) %collective-permute-start.4) | collective-permute-done | bytes 147488 | tf_op jit(solution)/shard_map/ppermute | solution.py:21
  13.5 0.5 collective-permute-start.12
  14.0 3.5 %collective-permute-done.2 = bf16[256,256]{1,0:T(8,128)(2,1)S(1)} collective-permute-done((bf16[256,256]{1,0:T(8,128)(2,1)S(1)}, bf16[256,256]{1,0:T(8,128)(2,1)S(1)}, u32[]{:S(2)}, u32[]{:S(2)}) %collective-permute-start.2) | collective-permute-done | bytes 131104 | tf_op jit(solution)/shard_map/ppermute | solution.py:121
  17.5 1.2 %collective-permute-done.3 = bf16[256,256]{1,0:T(8,128)(2,1)S(1)} collective-permute-done((bf16[256,256]{1,0:T(8,128)(2,1)S(1)}, bf16[256,256]{1,0:T(8,128)(2,1)S(1)}, u32[]{:S(2)}, u32[]{:S(2)}) %collective-permute-start.3) | collective-permute-done | bytes 131104 | tf_op jit(solution)/shard_map/ppermute | solution.py:121
  18.7 0.0 collective-permute-done.5.refs_1_
  18.7 4.5 %collective-permute-start.6 = (bf16[1024,256]{1,0:T(8,128)(2,1)S(1)}, bf16[1024,256]{1,0:T(8,128)(2,1)S(1)}, u32[]{:S(2)}, u32[]{:S(2)}) collective-permute-start(bf16[1024,256]{1,0:T(8,128)(2,1)S(1)} %constant_dynamic-update-slice_fusion.refs_1_), channel_id=1, source_target_pairs={{0,1},{1,0},{2,3},{3,2},{4,5},{5,4},{6,7},{7,6},{8,9},{9,8},{10,11... | collective-permute-start | bytes 1572872 | tf_op jit(solution)/shard_map/ppermute | solution.py:21
  23.1 1.4 %collective-permute-start.10 = (bf16[256,1024]{1,0:T(8,128)(2,1)S(1)}, bf16[256,1024]{1,0:T(8,128)(2,1)S(1)}, u32[]{:S(2)}, u32[]{:S(2)}) collective-permute-start(bf16[256,1024]{1,0:T(8,128)(2,1)S(1)} %collective-permute-done.5.refs_1_), channel_id=1, source_target_pairs={{0,4},{2,10},{4,0},{6,14},{8,16},{10,2},{12,20},{14,6},{16,8},{18,... | collective-permute-start | bytes 1572872 | tf_op jit(solution)/shard_map/ppermute | solution.py:320
  24.5 0.0 collective-permute-done.12.refs_2_
  24.5 0.7 %collective-permute-start.13 = (bf16[256,1024]{1,0:T(8,128)(2,1)S(1)}, bf16[256,1024]{1,0:T(8,128)(2,1)S(1)}, u32[]{:S(2)}, u32[]{:S(2)}) collective-permute-start(bf16[256,1024]{1,0:T(8,128)(2,1)S(1)} %collective-permute-done.12.refs_2_), channel_id=1, source_target_pairs={{0,8},{2,6},{4,12},{6,2},{8,0},{10,18},{12,4},{14,22},{16,24},{18,... | collective-permute-start | bytes 1572872 | tf_op jit(solution)/shard_map/ppermute | solution.py:320
  25.2 0.0 collective-permute-start.8
  25.2 5.7 %collective-permute-done.6.refs_2_ = bf16[1024,256]{1,0:T(8,128)(2,1)S(1)} collective-permute-done((bf16[1024,256]{1,0:T(8,128)(2,1)S(1)}, bf16[1024,256]{1,0:T(8,128)(2,1)S(1)}, u32[]{:S(2)}, u32[]{:S(2)}) %collective-permute-start.6) | collective-permute-done | bytes 524320 | tf_op jit(solution)/shard_map/ppermute | solution.py:21
  30.9 0.0 collective-permute-start.9
  30.9 0.5 collective-permute-start.7
  31.4 6.3 %collective-permute-done.10.refs_3_ = bf16[256,1024]{1,0:T(8,128)(2,1)S(1)} collective-permute-done((bf16[256,1024]{1,0:T(8,128)(2,1)S(1)}, bf16[256,1024]{1,0:T(8,128)(2,1)S(1)}, u32[]{:S(2)}, u32[]{:S(2)}) %collective-permute-start.10) | collective-permute-done | bytes 524320 | tf_op jit(solution)/shard_map/ppermute | solution.py:320
  37.7 0.0 collective-permute-start.11
  37.7 0.0 collective-permute-done.13.refs_0_
  37.7 1.6 %collective-permute-start.14 = (bf16[256,1024]{1,0:T(8,128)(2,1)S(1)}, bf16[256,1024]{1,0:T(8,128)(2,1)S(1)}, u32[]{:S(2)}, u32[]{:S(2)}) collective-permute-start(bf16[256,1024]{1,0:T(8,128)(2,1)S(1)} %collective-permute-done.13.refs_0_), channel_id=1, source_target_pairs={{0,4},{2,10},{4,0},{6,14},{8,16},{10,2},{12,20},{14,6},{16,8},{18,... | collective-permute-start | bytes 1572872 | tf_op jit(solution)/shard_map/ppermute | solution.py:320
  39.4 0.0 collective-permute-done.7.refs_3_
  39.4 0.0 collective-permute-start.19
  39.4 0.0 collective-permute-done.8.refs_4_
  39.4 0.5 collective-permute-start.20
  39.9 0.0 collective-permute-done.9.refs_5_
  39.9 0.1 collective-permute-start.21
  40.0 0.0 copy-start.1
  40.0 0.9 %copy-done.1 = bf16[256,256]{1,0:T(8,128)(2,1)S(1)} copy-done((bf16[256,256]{1,0:T(8,128)(2,1)S(1)}, bf16[256,256]{1,0:T(8,128)(2,1)}, u32[]{:S(2)}) %copy-start.1) | copy-done | bytes 131096
  40.9 6.3 %weights.1 = (bf16[16,512,256]{2,1,0:T(8,128)(2,1)S(1)}, f32[512,128]{1,0:T(8,128)S(1)}) custom-call(bf16[256,256]{1,0:T(8,128)(2,1)S(1)} %copy-done.1, bf16[1024,256]{1,0:T(8,128)(2,1)S(1)} %constant_dynamic-update-slice_fusion.refs_1_, bf16[1024,256]{1,0:T(8,128)(2,1)S(1)} %collective-permute-done.6.refs_2_, ...), custom_call_target="tpu_custom_call" | custom-call | flops 1024 | bytes 1024 | tf_op jit(solution)/shard_map/weights/pallas_call | solution.py:312
  47.2 1.1 %collective-permute-done.11.refs_1_ = bf16[256,1024]{1,0:T(8,128)(2,1)S(1)} collective-permute-done((bf16[256,1024]{1,0:T(8,128)(2,1)S(1)}, bf16[256,1024]{1,0:T(8,128)(2,1)S(1)}, u32[]{:S(2)}, u32[]{:S(2)}) %collective-permute-start.11) | collective-permute-done | bytes 524320 | tf_op jit(solution)/shard_map/ppermute | solution.py:320
  48.4 0.0 collective-permute-start.22
  48.4 0.0 collective-permute-done.14.refs_2_
  48.4 0.5 collective-permute-start.16
  48.9 0.0 collective-permute-done.19.refs_4_
  48.9 0.1 collective-permute-start.17
  48.9 0.0 collective-permute-done.20.refs_5_
  49.0 0.4 collective-permute-start.18
  49.4 0.0 collective-permute-done.21.refs_6_
  49.4 1.5 %collective-permute-start.15 = (bf16[256,1024]{1,0:T(8,128)(2,1)S(1)}, bf16[256,1024]{1,0:T(8,128)(2,1)S(1)}, u32[]{:S(2)}, u32[]{:S(2)}) collective-permute-start(bf16[256,1024]{1,0:T(8,128)(2,1)S(1)} %collective-permute-done.11.refs_1_), channel_id=1, source_target_pairs={{0,4},{2,10},{4,0},{6,14},{8,16},{10,2},{12,20},{14,6},{16,8},{18,... | collective-permute-start | bytes 1572872 | tf_op jit(solution)/shard_map/ppermute | solution.py:320
  50.9 0.0 collective-permute-done.22.refs_7_
  50.9 0.0 copy-done
  50.9 2.3 %product.4.refs_6_ = f32[512,1024]{1,0:T(8,128)S(1)} custom-call(bf16[16,512,256]{2,1,0:T(8,128)(2,1)S(1)} %get-tuple-element.12.weight, bf16[256,1024]{1,0:T(8,128)(2,1)S(1)} %copy-done, bf16[256,1024]{1,0:T(8,128)(2,1)S(1)} %collective-permute-done.5.refs_1_, bf16[256,1024]{1,0:T(8,128)(2,1)S(1)} %collective-permute-done.12.refs_2_, ...), custom_call_target="tpu_custom_call" | custom-call | flops 1024 | bytes 1024 | tf_op jit(solution)/shard_map/product/pallas_call | solution.py:328
  53.3 0.0 collective-permute-done.16.refs_3_
  53.3 0.0 collective-permute-done.17.refs_4_
  53.3 0.0 collective-permute-done.18.refs_5_
  53.3 1.8 %product.5.refs_1_ = f32[512,1024]{1,0:T(8,128)S(1)} custom-call(bf16[16,512,256]{2,1,0:T(8,128)(2,1)S(1)} %get-tuple-element.12.weight, bf16[256,1024]{1,0:T(8,128)(2,1)S(1)} %collective-permute-done.13.refs_0_, bf16[256,1024]{1,0:T(8,128)(2,1)S(1)} %collective-permute-done.11.refs_1_, bf16[256,1024]{1,0:T(8,128)(2,1)S(1)} %collective-permute-done.14.refs_2_, ...), custom_call_target="tpu_custom_call" | custom-call | flops 1024 | bytes 1024 | tf_op jit(solution)/shard_map/product/pallas_call | solution.py:328
  55.1 3.5 %collective-permute-done.15.refs_0_ = bf16[256,1024]{1,0:T(8,128)(2,1)S(1)} collective-permute-done((bf16[256,1024]{1,0:T(8,128)(2,1)S(1)}, bf16[256,1024]{1,0:T(8,128)(2,1)S(1)}, u32[]{:S(2)}, u32[]{:S(2)}) %collective-permute-start.15) | collective-permute-done | bytes 524320 | tf_op jit(solution)/shard_map/ppermute | solution.py:320
  58.6 0.0 collective-permute-start.23
  58.6 0.4 product.6.refs_2_
  59.0 1.5 %collective-permute-done.23.refs_0_ = bf16[256,1024]{1,0:T(8,128)(2,1)S(1)} collective-permute-done((bf16[256,1024]{1,0:T(8,128)(2,1)S(1)}, bf16[256,1024]{1,0:T(8,128)(2,1)S(1)}, u32[]{:S(2)}, u32[]{:S(2)}) %collective-permute-start.23) | collective-permute-done | bytes 524320 | tf_op jit(solution)/shard_map/ppermute | solution.py:21
  60.5 1.4 %product.7 = bf16[512,1024]{1,0:T(8,128)(2,1)} custom-call(bf16[16,512,256]{2,1,0:T(8,128)(2,1)S(1)} %get-tuple-element.12.weight, bf16[256,1024]{1,0:T(8,128)(2,1)S(1)} %collective-permute-done.23.refs_0_, f32[512,128]{1,0:T(8,128)S(1)} %get-tuple-element.13.refs_1_, f32[512,1024]{1,0:T(8,128)S(1)} %product.6.refs_2_), custom_call_target="tpu_custom_call" | custom-call | flops 1024 | bytes 1024 | tf_op jit(solution)/shard_map/product/pallas_call | solution.py:328
  (4 shorter events, 0.0 us)
Async XLA Ops:
  0.0 50.9 %copy-start = (bf16[256,1024]{1,0:T(8,128)(2,1)S(1)}, bf16[256,1024]{1,0:T(8,128)(2,1)}, u32[]{:S(2)}) copy-start(bf16[256,1024]{1,0:T(8,128)(2,1)} %refs_0_.3) | copy-start | bytes 1572868
  0.0 10.4 %collective-permute-start = (bf16[256,256]{1,0:T(8,128)(2,1)}, bf16[256,256]{1,0:T(8,128)(2,1)S(1)}, u32[]{:S(2)}, u32[]{:S(2)}) collective-permute-start(bf16[256,256]{1,0:T(8,128)(2,1)} %refs_0_.2), channel_id=1, source_target_pairs={{0,8},{1,17},{2,10},{3,19},{4,12},{5,21},{6,14},{7,23},{8,0},{9,25... | collective-permute-start | bytes 393224 | tf_op jit(solution)/shard_map/ppermute | solution.py:121
  3.0 9.2 %collective-permute-start.1 = (bf16[256,256]{1,0:T(8,128)(2,1)}, bf16[256,256]{1,0:T(8,128)(2,1)S(1)}, u32[]{:S(2)}, u32[]{:S(2)}) collective-permute-start(bf16[256,256]{1,0:T(8,128)(2,1)} %refs_0_.2), channel_id=1, source_target_pairs={{0,2},{1,5},{2,0},{3,7},{4,6},{5,1},{6,4},{7,3},{8,10},{9,13},{10,... | collective-permute-start | bytes 393224 | tf_op jit(solution)/shard_map/ppermute | solution.py:121
  3.0 15.7 %collective-permute-start.5 = (bf16[256,1024]{1,0:T(8,128)(2,1)}, bf16[256,1024]{1,0:T(8,128)(2,1)S(1)}, u32[]{:S(2)}, u32[]{:S(2)}) collective-permute-start(bf16[256,1024]{1,0:T(8,128)(2,1)} %refs_0_.3), channel_id=1, source_target_pairs={{0,8},{2,6},{4,12},{6,2},{8,0},{10,18},{12,4},{14,22},{16,24},{18,... | collective-permute-start | bytes 1572872 | tf_op jit(solution)/shard_map/ppermute | solution.py:320
  4.8 8.6 %collective-permute-start.4 = (bf16[288,256]{1,0:T(8,128)(2,1)S(1)}, bf16[288,256]{1,0:T(8,128)(2,1)S(1)}, u32[]{:S(2)}, u32[]{:S(2)}) collective-permute-start(bf16[288,256]{1,0:T(8,128)(2,1)S(1)} %pad_maximum_fusion.refs_6_), channel_id=1, source_target_pairs={{0,1},{1,0},{2,3},{3,2},{4,5},{5,4},{6,7},{7,6},{8,9},{9,8},{10,11... | collective-permute-start | bytes 442376 | tf_op jit(solution)/shard_map/ppermute | solution.py:21
  10.4 7.1 %collective-permute-start.2 = (bf16[256,256]{1,0:T(8,128)(2,1)S(1)}, bf16[256,256]{1,0:T(8,128)(2,1)S(1)}, u32[]{:S(2)}, u32[]{:S(2)}) collective-permute-start(bf16[256,256]{1,0:T(8,128)(2,1)S(1)} %collective-permute-done), channel_id=1, source_target_pairs={{0,4},{1,5},{2,6},{3,7},{4,0},{5,1},{6,2},{7,3},{8,12},{9,13},{10,... | collective-permute-start | bytes 393224 | tf_op jit(solution)/shard_map/ppermute | solution.py:121
  10.9 7.8 %collective-permute-start.3 = (bf16[256,256]{1,0:T(8,128)(2,1)S(1)}, bf16[256,256]{1,0:T(8,128)(2,1)S(1)}, u32[]{:S(2)}, u32[]{:S(2)}) collective-permute-start(bf16[256,256]{1,0:T(8,128)(2,1)S(1)} %collective-permute-done), channel_id=1, source_target_pairs={{0,20},{1,9},{2,22},{3,11},{4,16},{5,13},{6,18},{7,15},{8,28},{9,1... | collective-permute-start | bytes 393224 | tf_op jit(solution)/shard_map/ppermute | solution.py:121
  13.5 11.0 %collective-permute-start.12 = (bf16[256,1024]{1,0:T(8,128)(2,1)}, bf16[256,1024]{1,0:T(8,128)(2,1)S(1)}, u32[]{:S(2)}, u32[]{:S(2)}) collective-permute-start(bf16[256,1024]{1,0:T(8,128)(2,1)} %refs_0_.3), channel_id=1, source_target_pairs={{0,4},{2,10},{4,0},{6,14},{8,16},{10,2},{12,20},{14,6},{16,8},{18,... | collective-permute-start | bytes 1572872 | tf_op jit(solution)/shard_map/ppermute | solution.py:320
  18.7 12.2 %collective-permute-start.6 = (bf16[1024,256]{1,0:T(8,128)(2,1)S(1)}, bf16[1024,256]{1,0:T(8,128)(2,1)S(1)}, u32[]{:S(2)}, u32[]{:S(2)}) collective-permute-start(bf16[1024,256]{1,0:T(8,128)(2,1)S(1)} %constant_dynamic-update-slice_fusion.refs_1_), channel_id=1, source_target_pairs={{0,1},{1,0},{2,3},{3,2},{4,5},{5,4},{6,7},{7,6},{8,9},{9,8},{10,11... | collective-permute-start | bytes 1572872 | tf_op jit(solution)/shard_map/ppermute | solution.py:21
  23.1 14.6 %collective-permute-start.10 = (bf16[256,1024]{1,0:T(8,128)(2,1)S(1)}, bf16[256,1024]{1,0:T(8,128)(2,1)S(1)}, u32[]{:S(2)}, u32[]{:S(2)}) collective-permute-start(bf16[256,1024]{1,0:T(8,128)(2,1)S(1)} %collective-permute-done.5.refs_1_), channel_id=1, source_target_pairs={{0,4},{2,10},{4,0},{6,14},{8,16},{10,2},{12,20},{14,6},{16,8},{18,... | collective-permute-start | bytes 1572872 | tf_op jit(solution)/shard_map/ppermute | solution.py:320
  24.5 13.2 %collective-permute-start.13 = (bf16[256,1024]{1,0:T(8,128)(2,1)S(1)}, bf16[256,1024]{1,0:T(8,128)(2,1)S(1)}, u32[]{:S(2)}, u32[]{:S(2)}) collective-permute-start(bf16[256,1024]{1,0:T(8,128)(2,1)S(1)} %collective-permute-done.12.refs_2_), channel_id=1, source_target_pairs={{0,8},{2,6},{4,12},{6,2},{8,0},{10,18},{12,4},{14,22},{16,24},{18,... | collective-permute-start | bytes 1572872 | tf_op jit(solution)/shard_map/ppermute | solution.py:320
  25.2 14.1 %collective-permute-start.8 = (bf16[1024,256]{1,0:T(8,128)(2,1)S(1)}, bf16[1024,256]{1,0:T(8,128)(2,1)S(1)}, u32[]{:S(2)}, u32[]{:S(2)}) collective-permute-start(bf16[1024,256]{1,0:T(8,128)(2,1)S(1)} %constant_dynamic-update-slice_fusion.refs_1_), channel_id=1, source_target_pairs={{0,2},{2,0},{4,6},{6,4},{8,10},{10,8},{12,14},{14,12},{16,18},{18,... | collective-permute-start | bytes 1572872 | tf_op jit(solution)/shard_map/ppermute | solution.py:21
  30.9 9.0 %collective-permute-start.9 = (bf16[1024,256]{1,0:T(8,128)(2,1)S(1)}, bf16[1024,256]{1,0:T(8,128)(2,1)S(1)}, u32[]{:S(2)}, u32[]{:S(2)}) collective-permute-start(bf16[1024,256]{1,0:T(8,128)(2,1)S(1)} %collective-permute-done.6.refs_2_), channel_id=1, source_target_pairs={{0,2},{2,0},{4,6},{6,4},{8,10},{10,8},{12,14},{14,12},{16,18},{18,... | collective-permute-start | bytes 1572872 | tf_op jit(solution)/shard_map/ppermute | solution.py:21
  30.9 8.5 %collective-permute-start.7 = (bf16[256,256]{1,0:T(8,128)(2,1)}, bf16[256,256]{1,0:T(8,128)(2,1)S(1)}, u32[]{:S(2)}, u32[]{:S(2)}) collective-permute-start(bf16[256,256]{1,0:T(8,128)(2,1)} %refs_0_.2), channel_id=1, source_target_pairs={{0,2},{2,0},{4,6},{6,4},{8,10},{10,8},{12,14},{14,12},{16,18},{18,... | collective-permute-start | bytes 393224 | tf_op jit(solution)/shard_map/ppermute | solution.py:21
  37.7 10.6 %collective-permute-start.11 = (bf16[256,1024]{1,0:T(8,128)(2,1)S(1)}, bf16[256,1024]{1,0:T(8,128)(2,1)S(1)}, u32[]{:S(2)}, u32[]{:S(2)}) collective-permute-start(bf16[256,1024]{1,0:T(8,128)(2,1)S(1)} %collective-permute-done.10.refs_3_), channel_id=1, source_target_pairs={{0,8},{2,6},{4,12},{6,2},{8,0},{10,18},{12,4},{14,22},{16,24},{18,... | collective-permute-start | bytes 1572872 | tf_op jit(solution)/shard_map/ppermute | solution.py:320
  37.7 10.6 %collective-permute-start.14 = (bf16[256,1024]{1,0:T(8,128)(2,1)S(1)}, bf16[256,1024]{1,0:T(8,128)(2,1)S(1)}, u32[]{:S(2)}, u32[]{:S(2)}) collective-permute-start(bf16[256,1024]{1,0:T(8,128)(2,1)S(1)} %collective-permute-done.13.refs_0_), channel_id=1, source_target_pairs={{0,4},{2,10},{4,0},{6,14},{8,16},{10,2},{12,20},{14,6},{16,8},{18,... | collective-permute-start | bytes 1572872 | tf_op jit(solution)/shard_map/ppermute | solution.py:320
  39.4 9.5 %collective-permute-start.19 = (bf16[256,1024]{1,0:T(8,128)(2,1)}, bf16[256,1024]{1,0:T(8,128)(2,1)S(1)}, u32[]{:S(2)}, u32[]{:S(2)}) collective-permute-start(bf16[256,1024]{1,0:T(8,128)(2,1)} %refs_0_.3), channel_id=1, source_target_pairs={{0,2},{2,0},{4,6},{6,4},{8,10},{10,8},{12,14},{14,12},{16,18},{18,... | collective-permute-start | bytes 1572872 | tf_op jit(solution)/shard_map/ppermute | solution.py:21
  39.4 9.6 %collective-permute-start.20 = (bf16[256,1024]{1,0:T(8,128)(2,1)S(1)}, bf16[256,1024]{1,0:T(8,128)(2,1)S(1)}, u32[]{:S(2)}, u32[]{:S(2)}) collective-permute-start(bf16[256,1024]{1,0:T(8,128)(2,1)S(1)} %collective-permute-done.5.refs_1_), channel_id=1, source_target_pairs={{0,2},{2,0},{4,6},{6,4},{8,10},{10,8},{12,14},{14,12},{16,18},{18,... | collective-permute-start | bytes 1572872 | tf_op jit(solution)/shard_map/ppermute | solution.py:21
  39.9 9.5 %collective-permute-start.21 = (bf16[256,1024]{1,0:T(8,128)(2,1)S(1)}, bf16[256,1024]{1,0:T(8,128)(2,1)S(1)}, u32[]{:S(2)}, u32[]{:S(2)}) collective-permute-start(bf16[256,1024]{1,0:T(8,128)(2,1)S(1)} %collective-permute-done.12.refs_2_), channel_id=1, source_target_pairs={{0,2},{2,0},{4,6},{6,4},{8,10},{10,8},{12,14},{14,12},{16,18},{18,... | collective-permute-start | bytes 1572872 | tf_op jit(solution)/shard_map/ppermute | solution.py:21
  40.0 0.9 %copy-start.1 = (bf16[256,256]{1,0:T(8,128)(2,1)S(1)}, bf16[256,256]{1,0:T(8,128)(2,1)}, u32[]{:S(2)}) copy-start(bf16[256,256]{1,0:T(8,128)(2,1)} %refs_0_.2) | copy-start | bytes 393220
  48.4 2.6 %collective-permute-start.22 = (bf16[256,1024]{1,0:T(8,128)(2,1)S(1)}, bf16[256,1024]{1,0:T(8,128)(2,1)S(1)}, u32[]{:S(2)}, u32[]{:S(2)}) collective-permute-start(bf16[256,1024]{1,0:T(8,128)(2,1)S(1)} %collective-permute-done.10.refs_3_), channel_id=1, source_target_pairs={{0,2},{2,0},{4,6},{6,4},{8,10},{10,8},{12,14},{14,12},{16,18},{18,... | collective-permute-start | bytes 1572872 | tf_op jit(solution)/shard_map/ppermute | solution.py:21
  48.4 4.9 %collective-permute-start.16 = (bf16[256,1024]{1,0:T(8,128)(2,1)S(1)}, bf16[256,1024]{1,0:T(8,128)(2,1)S(1)}, u32[]{:S(2)}, u32[]{:S(2)}) collective-permute-start(bf16[256,1024]{1,0:T(8,128)(2,1)S(1)} %collective-permute-done.13.refs_0_), channel_id=1, source_target_pairs={{0,2},{2,0},{4,6},{6,4},{8,10},{10,8},{12,14},{14,12},{16,18},{18,... | collective-permute-start | bytes 1572872 | tf_op jit(solution)/shard_map/ppermute | solution.py:21
  48.9 4.4 %collective-permute-start.17 = (bf16[256,1024]{1,0:T(8,128)(2,1)S(1)}, bf16[256,1024]{1,0:T(8,128)(2,1)S(1)}, u32[]{:S(2)}, u32[]{:S(2)}) collective-permute-start(bf16[256,1024]{1,0:T(8,128)(2,1)S(1)} %collective-permute-done.11.refs_1_), channel_id=1, source_target_pairs={{0,2},{2,0},{4,6},{6,4},{8,10},{10,8},{12,14},{14,12},{16,18},{18,... | collective-permute-start | bytes 1572872 | tf_op jit(solution)/shard_map/ppermute | solution.py:21
  49.0 4.3 %collective-permute-start.18 = (bf16[256,1024]{1,0:T(8,128)(2,1)S(1)}, bf16[256,1024]{1,0:T(8,128)(2,1)S(1)}, u32[]{:S(2)}, u32[]{:S(2)}) collective-permute-start(bf16[256,1024]{1,0:T(8,128)(2,1)S(1)} %collective-permute-done.14.refs_2_), channel_id=1, source_target_pairs={{0,2},{2,0},{4,6},{6,4},{8,10},{10,8},{12,14},{14,12},{16,18},{18,... | collective-permute-start | bytes 1572872 | tf_op jit(solution)/shard_map/ppermute | solution.py:21
  49.4 9.2 %collective-permute-start.15 = (bf16[256,1024]{1,0:T(8,128)(2,1)S(1)}, bf16[256,1024]{1,0:T(8,128)(2,1)S(1)}, u32[]{:S(2)}, u32[]{:S(2)}) collective-permute-start(bf16[256,1024]{1,0:T(8,128)(2,1)S(1)} %collective-permute-done.11.refs_1_), channel_id=1, source_target_pairs={{0,4},{2,10},{4,0},{6,14},{8,16},{10,2},{12,20},{14,6},{16,8},{18,... | collective-permute-start | bytes 1572872 | tf_op jit(solution)/shard_map/ppermute | solution.py:320
  58.6 1.9 %collective-permute-start.23 = (bf16[256,1024]{1,0:T(8,128)(2,1)S(1)}, bf16[256,1024]{1,0:T(8,128)(2,1)S(1)}, u32[]{:S(2)}, u32[]{:S(2)}) collective-permute-start(bf16[256,1024]{1,0:T(8,128)(2,1)S(1)} %collective-permute-done.15.refs_0_), channel_id=1, source_target_pairs={{0,2},{2,0},{4,6},{6,4},{8,10},{10,8},{12,14},{14,12},{16,18},{18,... | collective-permute-start | bytes 1572872 | tf_op jit(solution)/shard_map/ppermute | solution.py:21

commit v6 on v5

--- a/solution.py
+++ b/solution.py
@@ -56,6 +56,7 @@
 
 ORDER = {
     "F2": ("Ox",),
+    "F3": ("S4",),
     "F7": ("K", "F6"),
     "D7": ("P2",),
     "Sx": ("Ox", "F1"),

time: 62.2 us -> 62.2 us (level)
  no operation moved by 1% of the time
where the time goes in v6:
time: 62.2 us; the launch traced here: 61.9 us
  waiting for transfers between devices  24 us (39%)
  starting transfers between devices  22.9 us (37%)
  Pallas kernels  12.3 us (20%)
  other arithmetic  1.65 us (3%)
  local copies, waits for them, and re-layouts  0.95 us (2%)
    ppermute x13, starting transfers between devices, swap(): return lax.ppermute(value, axis, [(i, i ^ bit) for i in range(size)])  12.1 us
    ppermute x7, waiting for transfers between devices, per_device(): lax.ppermute(value, 'row', pairs)  11 us
    ppermute x13, waiting for transfers between devices, swap(): return lax.ppermute(value, axis, [(i, i ^ bit) for i in range(size)])  8.39 us
    pallas_call x1, Pallas kernels, per_device(): weigh(*arrays)  6.33 us
    pallas_call x4, Pallas kernels, product(): call(functools.partial(product_kernel, columns, before is None, done), 28...  5.99 us
    ppermute x7, starting transfers between devices, per_device(): lax.ppermute(value, 'row', pairs)  5.89 us
    ppermute x4, starting transfers between devices, share_sims(): lax.ppermute(value, ('row', 'col'), pairs)  4.89 us
    ppermute x4, waiting for transfers between devices, share_sims(): lax.ppermute(value, ('row', 'col'), pairs)  4.67 us
  transfers between devices with their start and end apart: 24, of which 8 were waited for; matrix products, arithmetic and copies ran while one was open for 3% of the time, Pallas kernels for 18%

profile of v6, /device:TPU:0, one launch (start us, length us, event | category | flops | bytes accessed | tf_op | source)
XLA Modules:
  0.0 61.9 jit_solution(16624269153532232653)
XLA Ops:
  0.0 0.0 copy-start
  0.0 3.0 %collective-permute-start = (bf16[256,256]{1,0:T(8,128)(2,1)}, bf16[256,256]{1,0:T(8,128)(2,1)S(1)}, u32[]{:S(2)}, u32[]{:S(2)}) collective-permute-start(bf16[256,256]{1,0:T(8,128)(2,1)} %refs_0_.2), channel_id=1, source_target_pairs={{0,8},{1,17},{2,10},{3,19},{4,12},{5,21},{6,14},{7,23},{8,0},{9,25... | collective-permute-start | bytes 393224 | tf_op jit(solution)/shard_map/ppermute | solution.py:122
  3.0 0.0 collective-permute-start.1
  3.0 0.1 collective-permute-start.5
  3.2 0.7 %fusion = (bf16[16,256]{1,0:T(8,128)(2,1)S(1)}, bf16[16,256]{1,0:T(8,128)(2,1)S(1)}) fusion(s32[256,16]{0,1:T(8,128)} %param.6), kind=kLoop, calls=%fused_computation.6 | loop fusion | flops 86016 | bytes 32768 | tf_op jit(solution)/shard_map/convert
  3.9 0.9 %pad_maximum_fusion.refs_6_ = bf16[288,256]{1,0:T(8,128)(2,1)S(1)} fusion(bf16[16,256]{1,0:T(8,128)(2,1)S(1)} %get-tuple-element.20, bf16[16,256]{1,0:T(8,128)(2,1)S(1)} %get-tuple-element.19, bf16[256,256]{1,0:T(8,128)(2,1)} %param.4), kind=kLoop, calls=%fused_computation | loop fusion | flops 442368 | bytes 294912 | tf_op jit(solution)/shard_map/concatenate | solution.py:131
  4.8 5.5 %collective-permute-start.4 = (bf16[288,256]{1,0:T(8,128)(2,1)S(1)}, bf16[288,256]{1,0:T(8,128)(2,1)S(1)}, u32[]{:S(2)}, u32[]{:S(2)}) collective-permute-start(bf16[288,256]{1,0:T(8,128)(2,1)S(1)} %pad_maximum_fusion.refs_6_), channel_id=1, source_target_pairs={{0,1},{1,0},{2,3},{3,2},{4,5},{5,4},{6,7},{7,6},{8,9},{9,8},{10,11... | collective-permute-start | bytes 442376 | tf_op jit(solution)/shard_map/ppermute | solution.py:21
  10.4 0.0 collective-permute-done
  10.4 0.5 collective-permute-start.2
  10.9 1.4 %collective-permute-start.3 = (bf16[256,256]{1,0:T(8,128)(2,1)S(1)}, bf16[256,256]{1,0:T(8,128)(2,1)S(1)}, u32[]{:S(2)}, u32[]{:S(2)}) collective-permute-start(bf16[256,256]{1,0:T(8,128)(2,1)S(1)} %collective-permute-done), channel_id=1, source_target_pairs={{0,20},{1,9},{2,22},{3,11},{4,16},{5,13},{6,18},{7,15},{8,28},{9,1... | collective-permute-start | bytes 393224 | tf_op jit(solution)/shard_map/ppermute | solution.py:122
  12.2 0.0 collective-permute-done.1
  12.2 1.2 %collective-permute-done.4.refs_7_ = bf16[288,256]{1,0:T(8,128)(2,1)S(1)} collective-permute-done((bf16[288,256]{1,0:T(8,128)(2,1)S(1)}, bf16[288,256]{1,0:T(8,128)(2,1)S(1)}, u32[]{:S(2)}, u32[]{:S(2)}) %collective-permute-start.4) | collective-permute-done | bytes 147488 | tf_op jit(solution)/shard_map/ppermute | solution.py:21
  13.5 0.5 collective-permute-start.12
  14.0 3.5 %collective-permute-done.2 = bf16[256,256]{1,0:T(8,128)(2,1)S(1)} collective-permute-done((bf16[256,256]{1,0:T(8,128)(2,1)S(1)}, bf16[256,256]{1,0:T(8,128)(2,1)S(1)}, u32[]{:S(2)}, u32[]{:S(2)}) %collective-permute-start.2) | collective-permute-done | bytes 131104 | tf_op jit(solution)/shard_map/ppermute | solution.py:122
  17.5 1.2 %collective-permute-done.3 = bf16[256,256]{1,0:T(8,128)(2,1)S(1)} collective-permute-done((bf16[256,256]{1,0:T(8,128)(2,1)S(1)}, bf16[256,256]{1,0:T(8,128)(2,1)S(1)}, u32[]{:S(2)}, u32[]{:S(2)}) %collective-permute-start.3) | collective-permute-done | bytes 131104 | tf_op jit(solution)/shard_map/ppermute | solution.py:122
  18.7 0.0 collective-permute-done.5.refs_1_
  18.7 4.5 %collective-permute-start.6 = (bf16[1024,256]{1,0:T(8,128)(2,1)S(1)}, bf16[1024,256]{1,0:T(8,128)(2,1)S(1)}, u32[]{:S(2)}, u32[]{:S(2)}) collective-permute-start(bf16[1024,256]{1,0:T(8,128)(2,1)S(1)} %constant_dynamic-update-slice_fusion.refs_1_), channel_id=1, source_target_pairs={{0,1},{1,0},{2,3},{3,2},{4,5},{5,4},{6,7},{7,6},{8,9},{9,8},{10,11... | collective-permute-start | bytes 1572872 | tf_op jit(solution)/shard_map/ppermute | solution.py:21
  23.1 1.4 %collective-permute-start.10 = (bf16[256,1024]{1,0:T(8,128)(2,1)S(1)}, bf16[256,1024]{1,0:T(8,128)(2,1)S(1)}, u32[]{:S(2)}, u32[]{:S(2)}) collective-permute-start(bf16[256,1024]{1,0:T(8,128)(2,1)S(1)} %collective-permute-done.5.refs_1_), channel_id=1, source_target_pairs={{0,4},{2,10},{4,0},{6,14},{8,16},{10,2},{12,20},{14,6},{16,8},{18,... | collective-permute-start | bytes 1572872 | tf_op jit(solution)/shard_map/ppermute | solution.py:321
  24.5 0.0 collective-permute-done.12.refs_2_
  24.5 0.7 %collective-permute-start.13 = (bf16[256,1024]{1,0:T(8,128)(2,1)S(1)}, bf16[256,1024]{1,0:T(8,128)(2,1)S(1)}, u32[]{:S(2)}, u32[]{:S(2)}) collective-permute-start(bf16[256,1024]{1,0:T(8,128)(2,1)S(1)} %collective-permute-done.12.refs_2_), channel_id=1, source_target_pairs={{0,8},{2,6},{4,12},{6,2},{8,0},{10,18},{12,4},{14,22},{16,24},{18,... | collective-permute-start | bytes 1572872 | tf_op jit(solution)/shard_map/ppermute | solution.py:321
  25.2 0.0 collective-permute-start.8
  25.2 5.7 %collective-permute-done.6.refs_2_ = bf16[1024,256]{1,0:T(8,128)(2,1)S(1)} collective-permute-done((bf16[1024,256]{1,0:T(8,128)(2,1)S(1)}, bf16[1024,256]{1,0:T(8,128)(2,1)S(1)}, u32[]{:S(2)}, u32[]{:S(2)}) %collective-permute-start.6) | collective-permute-done | bytes 524320 | tf_op jit(solution)/shard_map/ppermute | solution.py:21
  30.9 0.0 collective-permute-start.9
  30.9 0.5 collective-permute-start.7
  31.4 6.3 %collective-permute-done.10.refs_3_ = bf16[256,1024]{1,0:T(8,128)(2,1)S(1)} collective-permute-done((bf16[256,1024]{1,0:T(8,128)(2,1)S(1)}, bf16[256,1024]{1,0:T(8,128)(2,1)S(1)}, u32[]{:S(2)}, u32[]{:S(2)}) %collective-permute-start.10) | collective-permute-done | bytes 524320 | tf_op jit(solution)/shard_map/ppermute | solution.py:321
  37.7 0.0 collective-permute-start.11
  37.7 0.0 collective-permute-done.13.refs_0_
  37.7 1.6 %collective-permute-start.14 = (bf16[256,1024]{1,0:T(8,128)(2,1)S(1)}, bf16[256,1024]{1,0:T(8,128)(2,1)S(1)}, u32[]{:S(2)}, u32[]{:S(2)}) collective-permute-start(bf16[256,1024]{1,0:T(8,128)(2,1)S(1)} %collective-permute-done.13.refs_0_), channel_id=1, source_target_pairs={{0,4},{2,10},{4,0},{6,14},{8,16},{10,2},{12,20},{14,6},{16,8},{18,... | collective-permute-start | bytes 1572872 | tf_op jit(solution)/shard_map/ppermute | solution.py:321
  39.4 0.0 collective-permute-done.7.refs_3_
  39.4 0.0 collective-permute-start.19
  39.4 0.0 collective-permute-done.8.refs_4_
  39.4 0.5 collective-permute-start.20
  39.9 0.0 collective-permute-done.9.refs_5_
  39.9 0.1 collective-permute-start.21
  40.0 0.0 copy-start.1
  40.0 0.9 %copy-done.1 = bf16[256,256]{1,0:T(8,128)(2,1)S(1)} copy-done((bf16[256,256]{1,0:T(8,128)(2,1)S(1)}, bf16[256,256]{1,0:T(8,128)(2,1)}, u32[]{:S(2)}) %copy-start.1) | copy-done | bytes 131096
  40.9 6.3 %weights.1 = (bf16[16,512,256]{2,1,0:T(8,128)(2,1)S(1)}, f32[512,128]{1,0:T(8,128)S(1)}) custom-call(bf16[256,256]{1,0:T(8,128)(2,1)S(1)} %copy-done.1, bf16[1024,256]{1,0:T(8,128)(2,1)S(1)} %constant_dynamic-update-slice_fusion.refs_1_, bf16[1024,256]{1,0:T(8,128)(2,1)S(1)} %collective-permute-done.6.refs_2_, ...), custom_call_target="tpu_custom_call" | custom-call | flops 1024 | bytes 1024 | tf_op jit(solution)/shard_map/weights/pallas_call | solution.py:313
  47.2 1.1 %collective-permute-done.11.refs_1_ = bf16[256,1024]{1,0:T(8,128)(2,1)S(1)} collective-permute-done((bf16[256,1024]{1,0:T(8,128)(2,1)S(1)}, bf16[256,1024]{1,0:T(8,128)(2,1)S(1)}, u32[]{:S(2)}, u32[]{:S(2)}) %collective-permute-start.11) | collective-permute-done | bytes 524320 | tf_op jit(solution)/shard_map/ppermute | solution.py:321
  48.4 0.0 collective-permute-start.22
  48.4 0.0 collective-permute-done.14.refs_2_
  48.4 0.5 collective-permute-start.16
  48.9 0.0 collective-permute-done.19.refs_4_
  48.9 0.1 collective-permute-start.17
  48.9 0.0 collective-permute-done.20.refs_5_
  49.0 0.4 collective-permute-start.18
  49.4 0.0 collective-permute-done.21.refs_6_
  49.4 1.5 %collective-permute-start.15 = (bf16[256,1024]{1,0:T(8,128)(2,1)S(1)}, bf16[256,1024]{1,0:T(8,128)(2,1)S(1)}, u32[]{:S(2)}, u32[]{:S(2)}) collective-permute-start(bf16[256,1024]{1,0:T(8,128)(2,1)S(1)} %collective-permute-done.11.refs_1_), channel_id=1, source_target_pairs={{0,4},{2,10},{4,0},{6,14},{8,16},{10,2},{12,20},{14,6},{16,8},{18,... | collective-permute-start | bytes 1572872 | tf_op jit(solution)/shard_map/ppermute | solution.py:321
  50.9 0.0 collective-permute-done.22.refs_7_
  50.9 0.0 copy-done
  50.9 2.3 %product.4.refs_6_ = f32[512,1024]{1,0:T(8,128)S(1)} custom-call(bf16[16,512,256]{2,1,0:T(8,128)(2,1)S(1)} %get-tuple-element.13.weight, bf16[256,1024]{1,0:T(8,128)(2,1)S(1)} %copy-done, bf16[256,1024]{1,0:T(8,128)(2,1)S(1)} %collective-permute-done.5.refs_1_, bf16[256,1024]{1,0:T(8,128)(2,1)S(1)} %collective-permute-done.12.refs_2_, ...), custom_call_target="tpu_custom_call" | custom-call | flops 1024 | bytes 1024 | tf_op jit(solution)/shard_map/product/pallas_call | solution.py:329
  53.3 0.0 collective-permute-done.16.refs_3_
  53.3 0.0 collective-permute-done.17.refs_4_
  53.3 0.0 collective-permute-done.18.refs_5_
  53.3 1.8 %product.5.refs_1_ = f32[512,1024]{1,0:T(8,128)S(1)} custom-call(bf16[16,512,256]{2,1,0:T(8,128)(2,1)S(1)} %get-tuple-element.13.weight, bf16[256,1024]{1,0:T(8,128)(2,1)S(1)} %collective-permute-done.13.refs_0_, bf16[256,1024]{1,0:T(8,128)(2,1)S(1)} %collective-permute-done.11.refs_1_, bf16[256,1024]{1,0:T(8,128)(2,1)S(1)} %collective-permute-done.14.refs_2_, ...), custom_call_target="tpu_custom_call" | custom-call | flops 1024 | bytes 1024 | tf_op jit(solution)/shard_map/product/pallas_call | solution.py:329
  55.1 3.5 %collective-permute-done.15.refs_0_ = bf16[256,1024]{1,0:T(8,128)(2,1)S(1)} collective-permute-done((bf16[256,1024]{1,0:T(8,128)(2,1)S(1)}, bf16[256,1024]{1,0:T(8,128)(2,1)S(1)}, u32[]{:S(2)}, u32[]{:S(2)}) %collective-permute-start.15) | collective-permute-done | bytes 524320 | tf_op jit(solution)/shard_map/ppermute | solution.py:321
  58.6 0.0 collective-permute-start.23
  58.6 0.4 product.6.refs_2_
  59.0 1.5 %collective-permute-done.23.refs_0_ = bf16[256,1024]{1,0:T(8,128)(2,1)S(1)} collective-permute-done((bf16[256,1024]{1,0:T(8,128)(2,1)S(1)}, bf16[256,1024]{1,0:T(8,128)(2,1)S(1)}, u32[]{:S(2)}, u32[]{:S(2)}) %collective-permute-start.23) | collective-permute-done | bytes 524320 | tf_op jit(solution)/shard_map/ppermute | solution.py:21
  60.5 1.4 %product.7 = bf16[512,1024]{1,0:T(8,128)(2,1)} custom-call(bf16[16,512,256]{2,1,0:T(8,128)(2,1)S(1)} %get-tuple-element.13.weight, bf16[256,1024]{1,0:T(8,128)(2,1)S(1)} %collective-permute-done.23.refs_0_, f32[512,128]{1,0:T(8,128)S(1)} %get-tuple-element.15.refs_1_, f32[512,1024]{1,0:T(8,128)S(1)} %product.6.refs_2_), custom_call_target="tpu_custom_call" | custom-call | flops 1024 | bytes 1024 | tf_op jit(solution)/shard_map/product/pallas_call | solution.py:329
  (4 shorter events, 0.0 us)
Async XLA Ops:
  0.0 50.9 %copy-start = (bf16[256,1024]{1,0:T(8,128)(2,1)S(1)}, bf16[256,1024]{1,0:T(8,128)(2,1)}, u32[]{:S(2)}) copy-start(bf16[256,1024]{1,0:T(8,128)(2,1)} %refs_0_.3) | copy-start | bytes 1572868
  0.0 10.4 %collective-permute-start = (bf16[256,256]{1,0:T(8,128)(2,1)}, bf16[256,256]{1,0:T(8,128)(2,1)S(1)}, u32[]{:S(2)}, u32[]{:S(2)}) collective-permute-start(bf16[256,256]{1,0:T(8,128)(2,1)} %refs_0_.2), channel_id=1, source_target_pairs={{0,8},{1,17},{2,10},{3,19},{4,12},{5,21},{6,14},{7,23},{8,0},{9,25... | collective-permute-start | bytes 393224 | tf_op jit(solution)/shard_map/ppermute | solution.py:122
  3.0 9.2 %collective-permute-start.1 = (bf16[256,256]{1,0:T(8,128)(2,1)}, bf16[256,256]{1,0:T(8,128)(2,1)S(1)}, u32[]{:S(2)}, u32[]{:S(2)}) collective-permute-start(bf16[256,256]{1,0:T(8,128)(2,1)} %refs_0_.2), channel_id=1, source_target_pairs={{0,2},{1,5},{2,0},{3,7},{4,6},{5,1},{6,4},{7,3},{8,10},{9,13},{10,... | collective-permute-start | bytes 393224 | tf_op jit(solution)/shard_map/ppermute | solution.py:122
  3.0 15.7 %collective-permute-start.5 = (bf16[256,1024]{1,0:T(8,128)(2,1)}, bf16[256,1024]{1,0:T(8,128)(2,1)S(1)}, u32[]{:S(2)}, u32[]{:S(2)}) collective-permute-start(bf16[256,1024]{1,0:T(8,128)(2,1)} %refs_0_.3), channel_id=1, source_target_pairs={{0,8},{2,6},{4,12},{6,2},{8,0},{10,18},{12,4},{14,22},{16,24},{18,... | collective-permute-start | bytes 1572872 | tf_op jit(solution)/shard_map/ppermute | solution.py:321
  4.8 8.6 %collective-permute-start.4 = (bf16[288,256]{1,0:T(8,128)(2,1)S(1)}, bf16[288,256]{1,0:T(8,128)(2,1)S(1)}, u32[]{:S(2)}, u32[]{:S(2)}) collective-permute-start(bf16[288,256]{1,0:T(8,128)(2,1)S(1)} %pad_maximum_fusion.refs_6_), channel_id=1, source_target_pairs={{0,1},{1,0},{2,3},{3,2},{4,5},{5,4},{6,7},{7,6},{8,9},{9,8},{10,11... | collective-permute-start | bytes 442376 | tf_op jit(solution)/shard_map/ppermute | solution.py:21
  10.4 7.1 %collective-permute-start.2 = (bf16[256,256]{1,0:T(8,128)(2,1)S(1)}, bf16[256,256]{1,0:T(8,128)(2,1)S(1)}, u32[]{:S(2)}, u32[]{:S(2)}) collective-permute-start(bf16[256,256]{1,0:T(8,128)(2,1)S(1)} %collective-permute-done), channel_id=1, source_target_pairs={{0,4},{1,5},{2,6},{3,7},{4,0},{5,1},{6,2},{7,3},{8,12},{9,13},{10,... | collective-permute-start | bytes 393224 | tf_op jit(solution)/shard_map/ppermute | solution.py:122
  10.9 7.8 %collective-permute-start.3 = (bf16[256,256]{1,0:T(8,128)(2,1)S(1)}, bf16[256,256]{1,0:T(8,128)(2,1)S(1)}, u32[]{:S(2)}, u32[]{:S(2)}) collective-permute-start(bf16[256,256]{1,0:T(8,128)(2,1)S(1)} %collective-permute-done), channel_id=1, source_target_pairs={{0,20},{1,9},{2,22},{3,11},{4,16},{5,13},{6,18},{7,15},{8,28},{9,1... | collective-permute-start | bytes 393224 | tf_op jit(solution)/shard_map/ppermute | solution.py:122
  13.5 11.0 %collective-permute-start.12 = (bf16[256,1024]{1,0:T(8,128)(2,1)}, bf16[256,1024]{1,0:T(8,128)(2,1)S(1)}, u32[]{:S(2)}, u32[]{:S(2)}) collective-permute-start(bf16[256,1024]{1,0:T(8,128)(2,1)} %refs_0_.3), channel_id=1, source_target_pairs={{0,4},{2,10},{4,0},{6,14},{8,16},{10,2},{12,20},{14,6},{16,8},{18,... | collective-permute-start | bytes 1572872 | tf_op jit(solution)/shard_map/ppermute | solution.py:321
  18.7 12.2 %collective-permute-start.6 = (bf16[1024,256]{1,0:T(8,128)(2,1)S(1)}, bf16[1024,256]{1,0:T(8,128)(2,1)S(1)}, u32[]{:S(2)}, u32[]{:S(2)}) collective-permute-start(bf16[1024,256]{1,0:T(8,128)(2,1)S(1)} %constant_dynamic-update-slice_fusion.refs_1_), channel_id=1, source_target_pairs={{0,1},{1,0},{2,3},{3,2},{4,5},{5,4},{6,7},{7,6},{8,9},{9,8},{10,11... | collective-permute-start | bytes 1572872 | tf_op jit(solution)/shard_map/ppermute | solution.py:21
  23.1 14.6 %collective-permute-start.10 = (bf16[256,1024]{1,0:T(8,128)(2,1)S(1)}, bf16[256,1024]{1,0:T(8,128)(2,1)S(1)}, u32[]{:S(2)}, u32[]{:S(2)}) collective-permute-start(bf16[256,1024]{1,0:T(8,128)(2,1)S(1)} %collective-permute-done.5.refs_1_), channel_id=1, source_target_pairs={{0,4},{2,10},{4,0},{6,14},{8,16},{10,2},{12,20},{14,6},{16,8},{18,... | collective-permute-start | bytes 1572872 | tf_op jit(solution)/shard_map/ppermute | solution.py:321
  24.5 13.2 %collective-permute-start.13 = (bf16[256,1024]{1,0:T(8,128)(2,1)S(1)}, bf16[256,1024]{1,0:T(8,128)(2,1)S(1)}, u32[]{:S(2)}, u32[]{:S(2)}) collective-permute-start(bf16[256,1024]{1,0:T(8,128)(2,1)S(1)} %collective-permute-done.12.refs_2_), channel_id=1, source_target_pairs={{0,8},{2,6},{4,12},{6,2},{8,0},{10,18},{12,4},{14,22},{16,24},{18,... | collective-permute-start | bytes 1572872 | tf_op jit(solution)/shard_map/ppermute | solution.py:321
  25.2 14.1 %collective-permute-start.8 = (bf16[1024,256]{1,0:T(8,128)(2,1)S(1)}, bf16[1024,256]{1,0:T(8,128)(2,1)S(1)}, u32[]{:S(2)}, u32[]{:S(2)}) collective-permute-start(bf16[1024,256]{1,0:T(8,128)(2,1)S(1)} %constant_dynamic-update-slice_fusion.refs_1_), channel_id=1, source_target_pairs={{0,2},{2,0},{4,6},{6,4},{8,10},{10,8},{12,14},{14,12},{16,18},{18,... | collective-permute-start | bytes 1572872 | tf_op jit(solution)/shard_map/ppermute | solution.py:21
  30.9 9.0 %collective-permute-start.9 = (bf16[1024,256]{1,0:T(8,128)(2,1)S(1)}, bf16[1024,256]{1,0:T(8,128)(2,1)S(1)}, u32[]{:S(2)}, u32[]{:S(2)}) collective-permute-start(bf16[1024,256]{1,0:T(8,128)(2,1)S(1)} %collective-permute-done.6.refs_2_), channel_id=1, source_target_pairs={{0,2},{2,0},{4,6},{6,4},{8,10},{10,8},{12,14},{14,12},{16,18},{18,... | collective-permute-start | bytes 1572872 | tf_op jit(solution)/shard_map/ppermute | solution.py:21
  30.9 8.5 %collective-permute-start.7 = (bf16[256,256]{1,0:T(8,128)(2,1)}, bf16[256,256]{1,0:T(8,128)(2,1)S(1)}, u32[]{:S(2)}, u32[]{:S(2)}) collective-permute-start(bf16[256,256]{1,0:T(8,128)(2,1)} %refs_0_.2), channel_id=1, source_target_pairs={{0,2},{2,0},{4,6},{6,4},{8,10},{10,8},{12,14},{14,12},{16,18},{18,... | collective-permute-start | bytes 393224 | tf_op jit(solution)/shard_map/ppermute | solution.py:21
  37.7 10.6 %collective-permute-start.11 = (bf16[256,1024]{1,0:T(8,128)(2,1)S(1)}, bf16[256,1024]{1,0:T(8,128)(2,1)S(1)}, u32[]{:S(2)}, u32[]{:S(2)}) collective-permute-start(bf16[256,1024]{1,0:T(8,128)(2,1)S(1)} %collective-permute-done.10.refs_3_), channel_id=1, source_target_pairs={{0,8},{2,6},{4,12},{6,2},{8,0},{10,18},{12,4},{14,22},{16,24},{18,... | collective-permute-start | bytes 1572872 | tf_op jit(solution)/shard_map/ppermute | solution.py:321
  37.7 10.6 %collective-permute-start.14 = (bf16[256,1024]{1,0:T(8,128)(2,1)S(1)}, bf16[256,1024]{1,0:T(8,128)(2,1)S(1)}, u32[]{:S(2)}, u32[]{:S(2)}) collective-permute-start(bf16[256,1024]{1,0:T(8,128)(2,1)S(1)} %collective-permute-done.13.refs_0_), channel_id=1, source_target_pairs={{0,4},{2,10},{4,0},{6,14},{8,16},{10,2},{12,20},{14,6},{16,8},{18,... | collective-permute-start | bytes 1572872 | tf_op jit(solution)/shard_map/ppermute | solution.py:321
  39.4 9.5 %collective-permute-start.19 = (bf16[256,1024]{1,0:T(8,128)(2,1)}, bf16[256,1024]{1,0:T(8,128)(2,1)S(1)}, u32[]{:S(2)}, u32[]{:S(2)}) collective-permute-start(bf16[256,1024]{1,0:T(8,128)(2,1)} %refs_0_.3), channel_id=1, source_target_pairs={{0,2},{2,0},{4,6},{6,4},{8,10},{10,8},{12,14},{14,12},{16,18},{18,... | collective-permute-start | bytes 1572872 | tf_op jit(solution)/shard_map/ppermute | solution.py:21
  39.4 9.6 %collective-permute-start.20 = (bf16[256,1024]{1,0:T(8,128)(2,1)S(1)}, bf16[256,1024]{1,0:T(8,128)(2,1)S(1)}, u32[]{:S(2)}, u32[]{:S(2)}) collective-permute-start(bf16[256,1024]{1,0:T(8,128)(2,1)S(1)} %collective-permute-done.5.refs_1_), channel_id=1, source_target_pairs={{0,2},{2,0},{4,6},{6,4},{8,10},{10,8},{12,14},{14,12},{16,18},{18,... | collective-permute-start | bytes 1572872 | tf_op jit(solution)/shard_map/ppermute | solution.py:21
  39.9 9.5 %collective-permute-start.21 = (bf16[256,1024]{1,0:T(8,128)(2,1)S(1)}, bf16[256,1024]{1,0:T(8,128)(2,1)S(1)}, u32[]{:S(2)}, u32[]{:S(2)}) collective-permute-start(bf16[256,1024]{1,0:T(8,128)(2,1)S(1)} %collective-permute-done.12.refs_2_), channel_id=1, source_target_pairs={{0,2},{2,0},{4,6},{6,4},{8,10},{10,8},{12,14},{14,12},{16,18},{18,... | collective-permute-start | bytes 1572872 | tf_op jit(solution)/shard_map/ppermute | solution.py:21
  40.0 0.9 %copy-start.1 = (bf16[256,256]{1,0:T(8,128)(2,1)S(1)}, bf16[256,256]{1,0:T(8,128)(2,1)}, u32[]{:S(2)}) copy-start(bf16[256,256]{1,0:T(8,128)(2,1)} %refs_0_.2) | copy-start | bytes 393220
  48.4 2.6 %collective-permute-start.22 = (bf16[256,1024]{1,0:T(8,128)(2,1)S(1)}, bf16[256,1024]{1,0:T(8,128)(2,1)S(1)}, u32[]{:S(2)}, u32[]{:S(2)}) collective-permute-start(bf16[256,1024]{1,0:T(8,128)(2,1)S(1)} %collective-permute-done.10.refs_3_), channel_id=1, source_target_pairs={{0,2},{2,0},{4,6},{6,4},{8,10},{10,8},{12,14},{14,12},{16,18},{18,... | collective-permute-start | bytes 1572872 | tf_op jit(solution)/shard_map/ppermute | solution.py:21
  48.4 4.9 %collective-permute-start.16 = (bf16[256,1024]{1,0:T(8,128)(2,1)S(1)}, bf16[256,1024]{1,0:T(8,128)(2,1)S(1)}, u32[]{:S(2)}, u32[]{:S(2)}) collective-permute-start(bf16[256,1024]{1,0:T(8,128)(2,1)S(1)} %collective-permute-done.13.refs_0_), channel_id=1, source_target_pairs={{0,2},{2,0},{4,6},{6,4},{8,10},{10,8},{12,14},{14,12},{16,18},{18,... | collective-permute-start | bytes 1572872 | tf_op jit(solution)/shard_map/ppermute | solution.py:21
  48.9 4.4 %collective-permute-start.17 = (bf16[256,1024]{1,0:T(8,128)(2,1)S(1)}, bf16[256,1024]{1,0:T(8,128)(2,1)S(1)}, u32[]{:S(2)}, u32[]{:S(2)}) collective-permute-start(bf16[256,1024]{1,0:T(8,128)(2,1)S(1)} %collective-permute-done.11.refs_1_), channel_id=1, source_target_pairs={{0,2},{2,0},{4,6},{6,4},{8,10},{10,8},{12,14},{14,12},{16,18},{18,... | collective-permute-start | bytes 1572872 | tf_op jit(solution)/shard_map/ppermute | solution.py:21
  49.0 4.3 %collective-permute-start.18 = (bf16[256,1024]{1,0:T(8,128)(2,1)S(1)}, bf16[256,1024]{1,0:T(8,128)(2,1)S(1)}, u32[]{:S(2)}, u32[]{:S(2)}) collective-permute-start(bf16[256,1024]{1,0:T(8,128)(2,1)S(1)} %collective-permute-done.14.refs_2_), channel_id=1, source_target_pairs={{0,2},{2,0},{4,6},{6,4},{8,10},{10,8},{12,14},{14,12},{16,18},{18,... | collective-permute-start | bytes 1572872 | tf_op jit(solution)/shard_map/ppermute | solution.py:21
  49.4 9.2 %collective-permute-start.15 = (bf16[256,1024]{1,0:T(8,128)(2,1)S(1)}, bf16[256,1024]{1,0:T(8,128)(2,1)S(1)}, u32[]{:S(2)}, u32[]{:S(2)}) collective-permute-start(bf16[256,1024]{1,0:T(8,128)(2,1)S(1)} %collective-permute-done.11.refs_1_), channel_id=1, source_target_pairs={{0,4},{2,10},{4,0},{6,14},{8,16},{10,2},{12,20},{14,6},{16,8},{18,... | collective-permute-start | bytes 1572872 | tf_op jit(solution)/shard_map/ppermute | solution.py:321
  58.6 1.9 %collective-permute-start.23 = (bf16[256,1024]{1,0:T(8,128)(2,1)S(1)}, bf16[256,1024]{1,0:T(8,128)(2,1)S(1)}, u32[]{:S(2)}, u32[]{:S(2)}) collective-permute-start(bf16[256,1024]{1,0:T(8,128)(2,1)S(1)} %collective-permute-done.15.refs_0_), channel_id=1, source_target_pairs={{0,2},{2,0},{4,6},{6,4},{8,10},{10,8},{12,14},{14,12},{16,18},{18,... | collective-permute-start | bytes 1572872 | tf_op jit(solution)/shard_map/ppermute | solution.py:21
